TPU v7x, 32 devices: a whole 2x2x4 slice. The times are simulated.
32 devices in a mesh: rng: 8 (over y, x, core), xr: 4 (over z).
Axes of the slice: x: 2, y: 2, z: 4, core: 2. Of those that a mesh axis runs over, the one named last changes fastest.
Arguments:
- incident: float32 [4, 128, 512], P(None, 'rng', 'xr'), may hold values from -6 to 6
- inverse_diag: float32 [4, 128, 512], P(None, 'rng', 'xr'), may hold values from -4 to 4
- previous: float32 [4, 128, 512], P(None, 'rng', 'xr'), may hold values from -4 to 4
- heights: float32 [128, 512], P('rng', 'xr'), may hold values from -3 to 3
- neighbours: int32 [24, 128, 512], P(None, 'rng', 'xr'), may hold values from 0 to 47, as said below
- counts: int32 [128, 512], P('rng', 'xr'), may hold values from 1 to 24
- transmit: float32 [8, 2, 64], P('rng'), may hold values from 0.02 to 1
- angle_weights: float32 [2, 2, 64], replicated, may hold values from -0.15 to 0.15
Outputs:
- forward_currents: float32 [4, 128, 512], P(None, 'rng', 'xr')
- currents: float32 [4, 128, 512], P(None, 'rng', 'xr')
Inputs may be any that keep to these rules, and one draw needn't show every extreme that they name: `neighbours`: the entries of one patch's list are distinct; slots at or beyond the patch's count hold entries that are not used.
All inputs are finite; a program needn't handle non-finite values.
Results may differ from a plain program's by a relative error of at most 0.0003.
Values sent between devices are 32-bit elements; how exact they have to be, the bound alone decides.
No kernel may reach another device: no remote copies, remote signals or barrier semaphores. Data moves between devices by JAX's collectives and lax.ppermute only.
A program may use at most 128 MiB of HBM per device.

v0:
```python
import functools
import math

import jax
import jax.numpy as jnp
from jax import lax
from jax.experimental import pallas as pl
from jax.experimental.pallas import tpu as pltpu
from jax.sharding import PartitionSpec as P

F = 2
Q = 64
H = 3
LMAX = 24
OFFSETS = 48
SUB = 8
LANES = 128
PERIOD = 64
TOP = SUB
GREEN = 0.25
TURN = 2.0 * math.pi
SLOT = 24
HIGHEST = lax.Precision.HIGHEST
BOTH = ("rng", "xr")
f32 = jnp.float32


def iota(shape, dim):
    return lax.broadcasted_iota(jnp.int32, shape, dim)


def roll(x, shift, axis=1):
    shift = shift % x.shape[axis]
    return x if shift == 0 else pltpu.roll(x, shift, axis)


def cos_sin(turns):
    quarter = jnp.floor(4.0 * turns + 0.5)
    rest = turns - 0.25 * quarter
    which = quarter.astype(jnp.int32)
    sq = rest * rest
    s = rest * (TURN + sq * (-(TURN**3) / 6 + sq * (TURN**5 / 120 + sq * (-(TURN**7) / 5040 + sq * (TURN**9 / 362880)))))
    c = 1.0 + sq * (-(TURN**2) / 2 + sq * (TURN**4 / 24 + sq * (-(TURN**6) / 720 + sq * (TURN**8 / 40320))))
    odd = (which & 1) == 1
    cos = jnp.where(odd, s, c)
    sin = jnp.where(odd, c, s)
    cos = jnp.where(((which + 1) & 2) == 2, -cos, cos)
    sin = jnp.where((which & 2) == 2, -sin, sin)
    return cos, sin


def times(a, b):
    return a[0] * b[0] - a[1] * b[1], a[0] * b[1] + a[1] * b[0]


def conj_times(a, b):
    return a[0] * b[0] + a[1] * b[1], a[0] * b[1] - a[1] * b[0]


def wave(step_x, x, step_y, y, lift, heights):
    phase = (step_x * x + step_y * y) & (PERIOD - 1)
    return cos_sin(phase.astype(f32) * (1.0 / PERIOD) + (lift / TURN) * heights)


def offset_of(code):
    full = code + (1 if code >= OFFSETS // 2 else 0)
    return full // (2 * H + 1) - H, full % (2 * H + 1) - H


def vmem():
    return pl.BlockSpec(memory_space=pltpu.VMEM)


def smem():
    return pl.BlockSpec(memory_space=pltpu.SMEM)


def call(body, out, n_in, scratch=(), flops=2_000_000):
    return pl.pallas_call(
        body,
        out_shape=tuple(jax.ShapeDtypeStruct(s, f32) for s in out),
        in_specs=[smem()] + [vmem()] * n_in,
        out_specs=tuple(vmem() for _ in out),
        scratch_shapes=list(scratch),
        compiler_params=pltpu.CompilerParams(vmem_limit_bytes=48 * 1024 * 1024),
        cost_estimate=pl.CostEstimate(flops=flops, bytes_accessed=1 << 20, transcendentals=0),
    )


def pack_columns(fields, right):
    rows = fields[0].shape[0]
    lane = iota((rows, LANES), 1)
    packed = jnp.zeros((rows, LANES), f32)
    for k, field in enumerate(fields):
        moved = roll(field, H * k - (LANES - H) if right else H * k)
        packed = jnp.where((lane >= H * k) & (lane < H * (k + 1)), moved, packed)
    return packed


def unpack_columns(from_left, from_right, k):
    lane = iota(from_left.shape, 1)
    left = jnp.where(lane >= LANES - H, roll(from_left, LANES - H - H * k), 0.0)
    return jnp.where(lane < H, roll(from_right, -H * k), left)


def shifted(inner, edge, dy):
    if dy == 0:
        return inner
    lane = iota(inner.shape, 1)
    outside = lane >= LANES - dy if dy > 0 else lane < -dy
    return jnp.where(outside, roll(edge, -dy), roll(inner, -dy))


def columns_body(place, prev, heights, inverse, send_a, send_b):
    fields = [prev[k] for k in range(2 * F)] + [heights[...]] + [inverse[k] for k in range(2 * F)]
    right = pack_columns(fields, True)
    left = pack_columns(fields, False)
    even = (place[1] & 1) == 0
    send_a[...] = jnp.where(even, right, left)
    send_b[...] = jnp.where(even, left, right)


N_FIELDS = 4 * F + 1
ROWS_SENT = 40


def rows_body(place, prev, heights, inverse, recv_a, recv_b, send_a, send_b):
    even_c = (place[1] & 1) == 0
    even_r = (place[0] & 1) == 0
    rows = heights.shape[0]
    fields = [prev[k] for k in range(2 * F)] + [heights[...]] + [inverse[k] for k in range(2 * F)]
    fields.append(jnp.where(even_c, recv_b[...], recv_a[...]))
    fields.append(jnp.where(even_c, recv_a[...], recv_b[...]))
    for k, field in enumerate(fields):
        last, first = field[rows - H :], field[:H]
        send_a[H * k : H * (k + 1)] = jnp.where(even_r, last, first)
        send_b[H * k : H * (k + 1)] = jnp.where(even_r, first, last)
    used = H * len(fields)
    send_a[used:] = jnp.zeros((ROWS_SENT - used, LANES), f32)
    send_b[used:] = jnp.zeros((ROWS_SENT - used, LANES), f32)


def tables_body(place, heights, inverse, weights_unused, tables, gens, left_mat, right_mat):
    rows = heights.shape[0]
    x0 = place[0] * rows
    y0 = place[1] * LANES
    angle = iota((2 * SUB, LANES), 0) - SUB
    y = iota((2 * SUB, LANES), 1) + y0
    for i in range(rows):
        h = heights[i : i + 1, :]
        x = jnp.full((2 * SUB, LANES), x0 + i, jnp.int32)
        lanes = pl.ds(i * LANES, LANES)
        h2 = jnp.broadcast_to(h, (2 * SUB, LANES)) * angle.astype(f32)
        c2, s2 = wave(0, x, angle, y, 0.03, h2)
        tables[4, i] = c2[SUB:]
        tables[5, i] = s2[SUB:]
        right_mat[0 : 2 * SUB, lanes] = c2
        right_mat[2 * SUB : 4 * SUB, lanes] = s2
        for direction in range(2):
            c1, s1 = wave(angle * (1 - 2 * direction), x, 0, y, 0.24, h2)
            tables[2 * direction, i] = c1[SUB:]
            tables[2 * direction + 1, i] = s1[SUB:]
            for f in range(F):
                zr = inverse[2 * f, i : i + 1, :]
                zi = inverse[2 * f + 1, i : i + 1, :]
                base = (direction * F + f) * 4 * SUB
                left_mat[base : base + 2 * SUB, lanes] = zr * c1 - zi * s1
                left_mat[base + 2 * SUB : base + 4 * SUB, lanes] = zr * s1 + zi * c1
    both = lax.dot_general(
        left_mat[...], right_mat[...], (((1,), (1,)), ((), ())), precision=HIGHEST, preferred_element_type=f32
    )
    lane = iota((SUB, LANES), 1)
    for direction in range(2):
        for f in range(F):
            base = (direction * F + f) * 4 * SUB
            for half in range(2):
                p = both[base + half * SUB : base + (half + 1) * SUB]
                q = both[base + (2 + half) * SUB : base + (3 + half) * SUB]
                for part in range(2):
                    if part == 0:
                        g = p - roll(q, -2 * SUB)
                    else:
                        g = roll(p, -2 * SUB) + q
                    g = jnp.where(lane < 2 * SUB, g, 0.0)
                    g = pltpu.roll(g, 0, 1, stride=2 * SUB, stride_axis=0)
                    row = jnp.sum(g, axis=0, keepdims=True)
                    at = direction * SUB + f * 4 + part * 2 + (1 - half)
                    gens[at : at + 1] = row


def project(left_mat, right_mat, tables, first, cs, rows, f_out):
    for i in range(rows):
        lanes = pl.ds(i * LANES, LANES)
        right_mat[0:SUB, lanes] = tables[4, i]
        right_mat[SUB : 2 * SUB, lanes] = tables[5, i]
        c1, s1 = tables[first, i], tables[first + 1, i]
        for f in range(F):
            re, im = conj_times((c1, s1), (cs[2 * f, i : i + 1, :], cs[2 * f + 1, i : i + 1, :]))
            left_mat[2 * f * SUB : (2 * f + 1) * SUB, lanes] = re
            left_mat[(2 * f + 1) * SUB : (2 * f + 2) * SUB, lanes] = im
    sums = lax.dot_general(
        left_mat[0 : 4 * SUB], right_mat[...], (((1,), (1,)), ((), ())), precision=HIGHEST, preferred_element_type=f32
    )
    lane = iota((SUB, LANES), 1)
    for f in range(F):
        gr = sums[2 * f * SUB : (2 * f + 1) * SUB]
        gi = sums[(2 * f + 1) * SUB : (2 * f + 2) * SUB]
        re = gr + roll(gi, -SUB)
        im = gi - roll(gr, -SUB)
        packed = jnp.where(lane < SUB, re, jnp.where(lane < 2 * SUB, roll(im, SUB), 0.0))
        packed = pltpu.roll(packed, 0, 1, stride=2 * SUB, stride_axis=0)
        f_out(f, jnp.sum(packed, axis=0, keepdims=True))


def carrier(f, direction, x, y, heights):
    sign = 1 - 2 * direction
    return wave(sign * (1 + 2 * f), x, f - 4, y, 0.3 + 0.2 * f, heights)


def place_ids(place, rows, cols, first_row, first_col, own_rows):
    x = place[0] * own_rows + first_row + iota((rows, cols), 0)
    y = place[1] * LANES + first_col + iota((rows, cols), 1)
    return x, y


def near_body(
    n_r, n_c, place, prev, heights, inverse, incident, neighbours, counts, transmit, cols_a, cols_b, rows_a, rows_b,
    gens, tables, payload, green, source, ext, inner, edge, edge_l, edge_r, moved, cs, left_mat, right_mat, common,
):
    rows = heights.shape[0]
    d, c = place[0], place[1]
    even_c = (c & 1) == 0
    even_r = (d & 1) == 0
    below = jnp.where(even_r, rows_a[...], rows_b[...])
    above = jnp.where(even_r, rows_b[...], rows_a[...])
    edge_l[...] = jnp.zeros(edge_l.shape, f32)
    edge_r[...] = jnp.zeros(edge_r.shape, f32)
    edge_l[TOP : TOP + rows] = jnp.where(even_c, cols_b[...], cols_a[...])
    edge_r[TOP : TOP + rows] = jnp.where(even_c, cols_a[...], cols_b[...])
    at = H * N_FIELDS
    edge_l[TOP - H : TOP] = above[at : at + H]
    edge_l[TOP + rows : TOP + rows + H] = below[at : at + H]
    edge_r[TOP - H : TOP] = above[at + H : at + 2 * H]
    edge_r[TOP + rows : TOP + rows + H] = below[at + H : at + 2 * H]
    fields = [prev[k] for k in range(2 * F)] + [heights[...]] + [inverse[k] for k in range(2 * F)]
    from_left, from_right = edge_l[...], edge_r[...]
    for k, field in enumerate(fields):
        inner[k] = jnp.zeros(inner.shape[1:], f32)
        inner[k, TOP : TOP + rows] = field
        inner[k, TOP - H : TOP] = above[H * k : H * (k + 1)]
        inner[k, TOP + rows : TOP + rows + H] = below[H * k : H * (k + 1)]
        side = unpack_columns(from_left, from_right, k)
        if k >= 2 * F:
            ext[2 * (k - 2 * F)] = inner[k]
            ext[2 * (k - 2 * F) + 1] = side
        if k <= 2 * F:
            middle = inner[k]
            for dy in range(-H, H + 1):
                moved[k * (2 * H + 1) + dy + H] = shifted(middle, side, dy)
    h = heights[...]
    count = counts[...]
    low = jnp.zeros(count.shape, jnp.int32)
    high = jnp.zeros(count.shape, jnp.int32)
    half = OFFSETS // 2
    one = jnp.ones(count.shape, jnp.int32)
    for slot in range(LMAX):
        code = neighbours[slot]
        live = count > slot
        is_low = code < half
        bit = lax.shift_left(one, jnp.where(is_low, code, code - half))
        low = low | jnp.where(live & is_low, bit, 0)
        high = high | jnp.where(live & (code >= half), bit, 0)
    near = [jnp.zeros((rows, LANES), f32) for _ in range(2 * F)]
    for code in range(OFFSETS):
        dx, dy = offset_of(code)
        window = lambda k: moved[k * (2 * H + 1) + dy + H, TOP + dx : TOP + dx + rows]
        lift = window(2 * F) - h
        squared = float(dx * dx + dy * dy) + lift * lift
        inverse_r = lax.rsqrt(squared)
        r = squared * inverse_r
        bits = low if code < half else high
        there = (bits & (1 << (code % half))) != 0
        size = jnp.where(there, GREEN * inverse_r, 0.0)
        for f in range(F):
            cos, sin = cos_sin(r * (0.25 * (1.0 + 0.25 * f)))
            g = (size * cos, size * sin)
            green[4 * code + 2 * f] = g[0]
            green[4 * code + 2 * f + 1] = g[1]
            got = times(g, (window(2 * f), window(2 * f + 1)))
            near[2 * f] += got[0]
            near[2 * f + 1] += got[1]
    x, y = place_ids(place, rows, LANES, 0, 0, rows)
    sources = []
    for f in range(F):
        z = (inverse[2 * f], inverse[2 * f + 1])
        s = times(z, (incident[2 * f] - near[2 * f], incident[2 * f + 1] - near[2 * f + 1]))
        sources += s
        source[2 * f] = s[0]
        source[2 * f + 1] = s[1]
        got = conj_times(carrier(f, 0, x, y, h), s)
        cs[2 * f] = got[0]
        cs[2 * f + 1] = got[1]

    def keep(f, row):
        common[2 * SUB + f : 2 * SUB + f + 1] = row

    right_mat[2 * SUB :] = jnp.zeros((right_mat.shape[0] - 2 * SUB, right_mat.shape[1]), f32)
    project(left_mat, right_mat, tables, 0, cs, rows, keep)
    common[0 : 2 * SUB] = gens[...]
    common[2 * SUB + 2 : 2 * SUB + 3] = transmit[...]
    tail = common[2 * SUB : 3 * SUB]
    for direction in range(2):
        part = common[direction * SUB : (direction + 1) * SUB]

        def fill(s, _, part=part, tail=tail):
            payload[s, 0:SUB] = part
            payload[s, SUB : 2 * SUB] = tail
            return 0

        if direction == 0:
            lax.fori_loop(d * n_c, n_r * n_c, fill, 0)
        else:
            lax.fori_loop(0, d * n_c, fill, 0)
    lasts = pack_columns(sources, True)
    firsts = pack_columns(sources, False)
    at = 2 * SUB - 4

    def send(dr, dc, put):
        dst = (d + dr) * n_c + c + dc
        ok = (d + dr >= 0) & (d + dr < n_r) & (c + dc >= 0) & (c + dc < n_c)

        @pl.when(ok)
        def _():
            put(dst)

    def rows_to(dr):
        def put(dst):
            for k in range(2 * F):
                s = sources[k]
                payload[dst, at + H * k : at + H * (k + 1)] = s[rows - H :] if dr > 0 else s[:H]

        return put

    def cols_to(dc):
        packed = lasts if dc > 0 else firsts

        def put(dst):
            payload[dst, at : at + SUB] = packed[:SUB] + roll(packed[SUB:], LANES // 2)

        return put

    def corner_to(dr, dc):
        packed = lasts if dc > 0 else firsts

        def put(dst):
            payload[dst, at : at + H] = packed[rows - H :] if dr > 0 else packed[:H]

        return put

    for dr in (-1, 1):
        send(dr, 0, rows_to(dr))
        send(0, dr, cols_to(dr))
        for dc in (-1, 1):
            send(dr, dc, corner_to(dr, dc))


def toeplitz(gen, sub, lane):
    first = jnp.broadcast_to(gen[0:1], (SUB, LANES))
    second = jnp.broadcast_to(gen[1:2], (SUB, LANES))
    tiles = []
    for a1 in range(Q // SUB):
        by = 2 * SUB * a1 - SUB
        inside = (lane >= by + sub) & (lane < by + sub + LANES)
        one = pltpu.roll(first, by % LANES, 1, stride=1, stride_axis=0)
        two = pltpu.roll(second, by % LANES, 1, stride=1, stride_axis=0)
        tiles.append(jnp.where(inside, one, two))
    return tiles


def to_column(row, sub, lane):
    return [
        jnp.sum(jnp.where(lane == 2 * SUB * a1 + sub, row, 0.0), axis=1, keepdims=True) for a1 in range(Q // SUB)
    ]


def to_row(columns, sub, lane):
    total = jnp.zeros((SUB, LANES), f32)
    for a1, column in enumerate(columns):
        total = jnp.where(lane == 2 * SUB * a1 + sub, column, total)
    return jnp.broadcast_to(jnp.sum(total, axis=0, keepdims=True), (SUB, LANES))


def sweep_step(gens, feeds, share, weights, carry, spread):
    sub = iota((SUB, LANES), 0)
    lane = iota((SUB, LANES), 1)
    wide = lambda row: jnp.broadcast_to(row, (SUB, LANES))
    low = (lane & SUB) == 0
    out = []
    for f in range(F):
        amp = times((wide(weights[2 * f]), wide(weights[2 * f + 1])), carry[f])
        re = toeplitz(gens[4 * f : 4 * f + 2], sub, lane)
        im = toeplitz(gens[4 * f + 2 : 4 * f + 4], sub, lane)
        col_r, col_i = [], []
        for kr, ki in zip(re, im, strict=True):
            got = times((kr, ki), amp)
            col_r.append(jnp.sum(got[0], axis=1, keepdims=True))
            col_i.append(jnp.sum(got[1], axis=1, keepdims=True))
        feed = wide(feeds[f : f + 1])
        t = wide(share)
        if f == 1:
            t = roll(t, -SUB)
        t = jnp.where(low, t, 0.0)
        out.append(
            (
                t * (carry[f][0] + feed - spread * to_row(col_r, sub, lane)),
                t * (carry[f][1] + roll(feed, -SUB) - spread * to_row(col_i, sub, lane)),
            )
        )
    return out


def amplitudes(weights, carry, spread):
    sub = iota((SUB, LANES), 0)
    lane = iota((SUB, LANES), 1)
    out = []
    for f in range(F):
        amp = times((weights[2 * f], weights[2 * f + 1]), carry[f])
        out.append([to_column(spread * part, sub, lane) for part in amp])
    return out


def powers(base, count):
    out = [None, base]
    for _ in range(2, count):
        out.append(times(out[-1], base))
    return out


def radiate(amp, f, splat, direction, x, y, heights):
    u1 = powers(wave(1 - 2 * direction, x, 0, y, 0.24, heights), Q // SUB)
    u2 = powers(wave(0, x, 1, y, 0.03, heights), SUB)
    return u1, u2


def radiated(f, splat, u1, u2, carried):
    total = None
    for a1 in range(Q // SUB):
        ar, ai = splat(f, 0, SUB * a1), splat(f, 1, SUB * a1)
        inner = (ar, ai)
        for a2 in range(1, SUB):
            got = times((splat(f, 0, SUB * a1 + a2), splat(f, 1, SUB * a1 + a2)), u2[a2])
            inner = (inner[0] + got[0], inner[1] + got[1])
        if a1 == 0:
            total = inner
        else:
            got = times(u1[a1], inner)
            total = (total[0] + got[0], total[1] + got[1])
    return times(carried, total)


def sums_of(recv, at, n_c):
    total = recv[at, 0 : 2 * SUB]
    for k in range(1, n_c):
        total = total + recv[at + k, 0 : 2 * SUB]
    return total


def new_body(
    n_r, n_c, spread, place, recv, green, source, ext, heights, inverse, incident, tables, weights,
    forward, driven, payload, carries, amps, inner, moved, edge_l, edge_r, cs, left_mat, right_mat, common,
):
    rows = heights.shape[0]
    d, c = place[0], place[1]
    wts = [weights[k : k + 1] for k in range(2 * F)]
    zero = jnp.zeros((SUB, LANES), f32)
    for k in range(2 * F):
        carries[0, k] = zero

    def lap(j, carry):
        sums = sums_of(recv, j * n_c, n_c)
        share = recv[j * n_c, SUB + 2 : SUB + 3]
        new = sweep_step(sums[:SUB], sums[SUB : SUB + 2], share, wts, [(carry[0], carry[1]), (carry[2], carry[3])], spread)
        flat = (new[0][0], new[0][1], new[1][0], new[1][1])
        for k in range(2 * F):
            carries[j + 1, k] = flat[k]
        return flat

    lax.fori_loop(0, jnp.minimum(d + 1, n_r - 1), lap, (zero,) * (2 * F))
    for which in range(3):
        at = jnp.clip(d + which - 1, 0, n_r - 1)
        carry = [(carries[at, 2 * f], carries[at, 2 * f + 1]) for f in range(F)]
        for f, parts in enumerate(amplitudes(wts, carry, spread)):
            for part, columns in enumerate(parts):
                for a1, column in enumerate(columns):
                    amps[which, 2 * f + part, SUB * a1 : SUB * (a1 + 1)] = jnp.broadcast_to(column, (SUB, LANES))

    at = 2 * SUB - 4

    def got(dr, dc, start, size):
        src = jnp.clip(d + dr, 0, n_r - 1) * n_c + jnp.clip(c + dc, 0, n_c - 1)
        ok = (d + dr >= 0) & (d + dr < n_r) & (c + dc >= 0) & (c + dc < n_c)
        return jnp.where(ok, recv[src, start : start + size], 0.0)

    edge_l[...] = jnp.zeros(edge_l.shape, f32)
    edge_r[...] = jnp.zeros(edge_r.shape, f32)
    for edge, dc in ((edge_l, -1), (edge_r, 1)):
        side = got(0, dc, at, SUB)
        edge[TOP : TOP + SUB] = side
        edge[TOP + SUB : TOP + rows] = roll(side, -(LANES // 2))
        edge[TOP - H : TOP] = got(-1, dc, at, H)
        edge[TOP + rows : TOP + rows + H] = got(1, dc, at, H)
    from_left, from_right = edge_l[...], edge_r[...]
    for k in range(2 * F):
        inner[k] = jnp.zeros(inner.shape[1:], f32)
        inner[k, TOP : TOP + rows] = source[k]
        inner[k, TOP - H : TOP] = got(-1, 0, at + H * k, H)
        inner[k, TOP + rows : TOP + rows + H] = got(1, 0, at + H * k, H)
    sides = [unpack_columns(from_left, from_right, k) for k in range(2 * F)]

    weak = {}
    tiles = (rows + 2 * SUB) // SUB
    for tile in range(tiles):
        which = 0 if tile == 0 else 2 if tile == tiles - 1 else 1
        splat = lambda f, part, a, which=which: amps[which, 2 * f + part, a : a + 1]
        rows_at = slice(SUB * tile, SUB * (tile + 1))
        for side in range(2):
            x, y = place_ids(place, SUB, LANES, SUB * tile - TOP, 0, rows)
            if side == 1:
                lane = iota((SUB, LANES), 1)
                y = y + jnp.where(lane < LANES // 2, LANES, -LANES)
            h = ext[side, rows_at]
            u1, u2 = radiate(None, 0, None, 0, x, y, h)
            for f in range(F):
                w = radiated(f, splat, u1, u2, carrier(f, 0, x, y, h))
                z = (ext[2 * (1 + 2 * f) + side, rows_at], ext[2 * (2 + 2 * f) + side, rows_at])
                lost = times(z, w)
                for part in range(2):
                    k = 2 * f + part
                    if side == 0:
                        inner[k, rows_at] = inner[k, rows_at] - lost[part]
                        weak[tile, k] = w[part]
                    else:
                        sides[k] = (sides[k] if isinstance(sides[k], list) else [sides[k]]) + [
                            sides_tile(sides[k], rows_at) - lost[part]
                        ]
    for k in range(2 * F):
        side = jnp.concatenate(sides[k][1:], axis=0)
        middle = inner[k]
        forward[k] = middle[TOP : TOP + rows]
        for dy in range(-H, H + 1):
            moved[k * (2 * H + 1) + dy + H] = shifted(middle, side, dy)
    near = [jnp.zeros((rows, LANES), f32) for _ in range(2 * F)]
    for code in range(OFFSETS):
        dx, dy = offset_of(code)
        window = lambda k: moved[k * (2 * H + 1) + dy + H, TOP + dx : TOP + dx + rows]
        for f in range(F):
            g = (green[4 * code + 2 * f], green[4 * code + 2 * f + 1])
            add = times(g, (window(2 * f), window(2 * f + 1)))
            near[2 * f] += add[0]
            near[2 * f + 1] += add[1]
    x, y = place_ids(place, rows, LANES, 0, 0, rows)
    h = heights[...]
    for f in range(F):
        rest = []
        for part in range(2):
            k = 2 * f + part
            w = jnp.concatenate([weak[tile, k] for tile in range(1, tiles - 1)], axis=0)
            rest.append(incident[k] - near[k] - w)
        s = times((inverse[2 * f], inverse[2 * f + 1]), rest)
        driven[2 * f] = s[0]
        driven[2 * f + 1] = s[1]
        add = conj_times(carrier(f, 1, x, y, h), s)
        cs[2 * f] = add[0]
        cs[2 * f + 1] = add[1]

    def keep(f, row):
        common[f : f + 1] = row

    right_mat[2 * SUB :] = jnp.zeros((right_mat.shape[0] - 2 * SUB, right_mat.shape[1]), f32)
    project(left_mat, right_mat, tables, 2, cs, rows, keep)
    pair = common[0:2]

    def fill(s, _):
        payload[s] = pair
        return 0

    lax.fori_loop(0, n_r * n_c, fill, 0)


def sides_tile(side, rows_at):
    return side[0][rows_at] if isinstance(side, list) else side[rows_at]


def last_body(n_r, n_c, spread, place, recv, feeds, driven, heights, inverse, weights, currents, amps):
    rows = heights.shape[0]
    d = place[0]
    wts = [weights[k : k + 1] for k in range(2 * F)]
    zero = jnp.zeros((SUB, LANES), f32)

    def lap(k, carry):
        j = n_r - 1 - k
        gens = sums_of(recv, j * n_c, n_c)[:SUB]
        share = recv[j * n_c, SUB + 2 : SUB + 3]
        feed = feeds[j * n_c]
        for i in range(1, n_c):
            feed = feed + feeds[j * n_c + i]
        new = sweep_step(gens, feed, share, wts, [(carry[0], carry[1]), (carry[2], carry[3])], spread)
        return (new[0][0], new[0][1], new[1][0], new[1][1])

    carry = lax.fori_loop(0, n_r - 1 - d, lap, (zero,) * (2 * F))
    carry = [(carry[0], carry[1]), (carry[2], carry[3])]
    for f, parts in enumerate(amplitudes(wts, carry, spread)):
        for part, columns in enumerate(parts):
            for a1, column in enumerate(columns):
                amps[2 * f + part, SUB * a1 : SUB * (a1 + 1)] = jnp.broadcast_to(column, (SUB, LANES))
    splat = lambda f, part, a: amps[2 * f + part, a : a + 1]
    for tile in range(rows // SUB):
        rows_at = slice(SUB * tile, SUB * (tile + 1))
        x, y = place_ids(place, SUB, LANES, SUB * tile, 0, rows)
        h = heights[rows_at]
        u1, u2 = radiate(None, 0, None, 1, x, y, h)
        for f in range(F):
            w = radiated(f, splat, u1, u2, carrier(f, 1, x, y, h))
            lost = times((inverse[2 * f, rows_at], inverse[2 * f + 1, rows_at]), w)
            currents[2 * f, rows_at] = driven[2 * f, rows_at] - lost[0]
            currents[2 * f + 1, rows_at] = driven[2 * f + 1, rows_at] - lost[1]


def swaps(n):
    first = [(i, i ^ 1) for i in range(n) if i ^ 1 < n]
    second = [(i, i + 1) for i in range(1, n - 1, 2)] + [(i + 1, i) for i in range(1, n - 1, 2)]
    return first, second


def swap(axis, n, a, b):
    first, second = swaps(n)
    return lax.ppermute(a, axis, first), lax.ppermute(b, axis, second)


def lanes_of(values):
    lead = values.shape[:-1]
    split = values.reshape(lead + (Q // SUB, SUB))
    return jnp.concatenate([split, jnp.zeros_like(split)], -1).reshape(lead + (2 * Q,))


def per_device(n_r, n_c, incident, inverse_diag, previous, heights, neighbours, counts, transmit, angle_weights):
    rows, cols = heights.shape
    patches = rows * cols
    spread = 1.0 / math.sqrt(rows * cols * n_c)
    slots = n_r * n_c
    place = jnp.stack([lax.axis_index("rng"), lax.axis_index("xr")]).astype(jnp.int32)
    weights = lanes_of(angle_weights.reshape(2 * F, Q))
    share = transmit.reshape(F, Q // SUB, SUB)
    share = jnp.concatenate([share[0], share[1]], -1).reshape(1, 2 * Q)
    tall = rows + 2 * SUB
    cols_a, cols_b = call(columns_body, [(rows, LANES)] * 2, 3)(place, previous, heights, inverse_diag)
    tables, gens = call(
        tables_body,
        [(6, rows, SUB, LANES), (2 * SUB, LANES)],
        3,
        [pltpu.VMEM((16 * SUB, patches), f32), pltpu.VMEM((16 * SUB, patches), f32)],
    )(place, heights, inverse_diag, weights)
    cols_a, cols_b = swap("xr", n_c, cols_a, cols_b)
    rows_a, rows_b = call(rows_body, [(ROWS_SENT, LANES)] * 2, 5)(
        place, previous, heights, inverse_diag, cols_a, cols_b
    )
    rows_a, rows_b = swap("rng", n_r, rows_a, rows_b)
    payload, green, source, ext = call(
        functools.partial(near_body, n_r, n_c),
        [(slots, SLOT, LANES), (4 * OFFSETS, rows, LANES), (2 * F, rows, LANES), (4 * F + 2, tall, LANES)],
        13,
        [
            pltpu.VMEM((N_FIELDS, tall, LANES), f32),
            pltpu.VMEM((SUB, LANES), f32),
            pltpu.VMEM((tall, LANES), f32),
            pltpu.VMEM((tall, LANES), f32),
            pltpu.VMEM(((2 * F + 1) * (2 * H + 1), tall, LANES), f32),
            pltpu.VMEM((2 * F, rows, LANES), f32),
            pltpu.VMEM((4 * SUB, patches), f32),
            pltpu.VMEM((16 * SUB, patches), f32),
            pltpu.VMEM((3 * SUB, LANES), f32),
        ],
    )(
        place, previous, heights, inverse_diag, incident, neighbours, counts, share,
        cols_a, cols_b, rows_a, rows_b, gens, tables,
    )
    recv = lax.all_to_all(payload, BOTH, 0, 0)
    forward, driven, payload = call(
        functools.partial(new_body, n_r, n_c, spread),
        [(2 * F, rows, LANES), (2 * F, rows, LANES), (slots, 2, LANES)],
        9,
        [
            pltpu.VMEM((n_r + 1, 2 * F, SUB, LANES), f32),
            pltpu.VMEM((3, 2 * F, Q, LANES), f32),
            pltpu.VMEM((2 * F, tall, LANES), f32),
            pltpu.VMEM((2 * F * (2 * H + 1), tall, LANES), f32),
            pltpu.VMEM((tall, LANES), f32),
            pltpu.VMEM((tall, LANES), f32),
            pltpu.VMEM((2 * F, rows, LANES), f32),
            pltpu.VMEM((4 * SUB, patches), f32),
            pltpu.VMEM((16 * SUB, patches), f32),
            pltpu.VMEM((SUB, LANES), f32),
        ],
    )(place, recv, green, source, ext, heights, inverse_diag, incident, tables, weights)
    feeds = lax.all_to_all(payload, BOTH, 0, 0)
    (currents,) = call(
        functools.partial(last_body, n_r, n_c, spread),
        [(2 * F, rows, LANES)],
        6,
        [pltpu.VMEM((2 * F, Q, LANES), f32)],
    )(place, recv, feeds, driven, heights, inverse_diag, weights)
    return forward, currents


def solution(mesh):
    body = functools.partial(per_device, mesh.shape["rng"], mesh.shape["xr"])
    field = P(None, "rng", "xr")
    return jax.shard_map(
        body,
        mesh=mesh,
        in_specs=(field, field, field, P("rng", "xr"), field, P("rng", "xr"), P("rng", None, None), P()),
        out_specs=(field, field),
        check_vma=False,
    )
```

profile of v0, /device:TPU:0, one launch (start us, length us, event | category | flops | bytes accessed | tf_op | source)
XLA Modules:
  0.0 66.6 jit_solution(14365262824151968536)
XLA Ops:
  0.6 0.1 pad_add_fusion.place
  0.7 0.0 copy-start
  0.7 0.8 %copy-done = f32[4,16,128]{2,1,0:T(8,128)S(1)} copy-done((f32[4,16,128]{2,1,0:T(8,128)S(1)}, f32[4,16,128]{2,1,0:T(8,128)}, u32[]{:S(2)}) %copy-start) | copy-done | bytes 32792
  1.5 0.0 copy-start.5
  1.5 0.7 %copy-done.5 = f32[16,128]{1,0:T(8,128)S(1)} copy-done((f32[16,128]{1,0:T(8,128)S(1)}, f32[16,128]{1,0:T(8,128)}, u32[]{:S(2)}) %copy-start.5) | copy-done | bytes 8216
  2.2 0.0 copy-start.9
  2.2 0.8 %copy-done.9 = f32[4,16,128]{2,1,0:T(8,128)S(1)} copy-done((f32[4,16,128]{2,1,0:T(8,128)S(1)}, f32[4,16,128]{2,1,0:T(8,128)}, u32[]{:S(2)}) %copy-start.9) | copy-done | bytes 32792
  2.9 0.0 copy-start.4
  2.9 0.6 shard_map.95
  3.6 3.1 %collective-permute-start = (f32[16,128]{1,0:T(8,128)S(1)}, f32[16,128]{1,0:T(8,128)S(1)}, u32[]{:S(2)}, u32[]{:S(2)}) collective-permute-start(f32[16,128]{1,0:T(8,128)S(1)} %get-tuple-element.15), channel_id=1, source_target_pairs={{0,1},{1,0},{2,3},{3,2},{4,5},{5,4},{6,7},{7,6},{8,9},{9,8},{10,11... | collective-permute-start | bytes 24584 | tf_op jit(solution)/shard_map/ppermute | solution.py:637
  6.7 0.6 collective-permute-start.1
  7.3 0.8 %slice_reduce_fusion.1 = (f32[64]{0:T(128)S(1)}, f32[64]{0:T(128)S(1)}) fusion(f32[1,2,64]{2,1,0:T(2,128)} %param.14), kind=kLoop, calls=%fused_computation.3 | loop fusion | bytes 1024 | tf_op jit(solution)/shard_map/slice | solution.py:654
  8.1 0.1 squeeze.6
  8.2 0.1 squeeze.7
  8.2 0.0 collective-permute-done.recv_a.cols_a
  8.3 0.0 collective-permute-done.1.recv_b.cols_b
  8.3 0.0 copy-start.1
  8.3 0.8 %copy-done.1 = f32[4,16,128]{2,1,0:T(8,128)S(1)} copy-done((f32[4,16,128]{2,1,0:T(8,128)S(1)}, f32[4,16,128]{2,1,0:T(8,128)}, u32[]{:S(2)}) %copy-start.1) | copy-done | bytes 32792
  9.0 0.0 copy-start.6
  9.1 0.7 %copy-done.6 = f32[16,128]{1,0:T(8,128)S(1)} copy-done((f32[16,128]{1,0:T(8,128)S(1)}, f32[16,128]{1,0:T(8,128)}, u32[]{:S(2)}) %copy-start.6) | copy-done | bytes 8216
  9.7 0.0 copy-start.10
  9.7 0.8 %copy-done.10 = f32[4,16,128]{2,1,0:T(8,128)S(1)} copy-done((f32[4,16,128]{2,1,0:T(8,128)S(1)}, f32[4,16,128]{2,1,0:T(8,128)}, u32[]{:S(2)}) %copy-start.10) | copy-done | bytes 32792
  10.5 0.6 shard_map.96
  11.1 0.1 collective-permute-start.2
  11.1 0.7 collective-permute-start.3
  11.8 0.1 pad_maximum_fusion
  11.9 0.1 reshape.15.transmit
  12.0 0.8 %reshape_reshape.3 = f32[4,8,8]{2,1,0:T(8,128)S(1)} reshape(f32[2,2,64]{2,1,0:T(2,128)} %param.15) | data formatting | bytes 2048 | tf_op jit(solution)/shard_map/reshape;reshape | solution.py:642
  12.7 0.1 reshape.16.weights_unused.weights
  12.8 0.0 copy-start.2
  12.8 0.8 %copy-done.2 = f32[4,16,128]{2,1,0:T(8,128)S(1)} copy-done((f32[4,16,128]{2,1,0:T(8,128)S(1)}, f32[4,16,128]{2,1,0:T(8,128)}, u32[]{:S(2)}) %copy-start.2) | copy-done | bytes 32792
  13.6 0.0 copy-start.7
  13.6 0.7 %copy-done.7 = f32[16,128]{1,0:T(8,128)S(1)} copy-done((f32[16,128]{1,0:T(8,128)S(1)}, f32[16,128]{1,0:T(8,128)}, u32[]{:S(2)}) %copy-start.7) | copy-done | bytes 8216
  14.3 2.3 %shard_map.97 = (f32[6,16,8,128]{3,2,1,0:T(8,128)S(1)}, f32[16,128]{1,0:T(8,128)S(1)}) custom-call(s32[2]{0:T(128)S(1)} %pad_add_fusion.place, f32[16,128]{1,0:T(8,128)S(1)} %copy-done.7, f32[4,16,128]{2,1,0:T(8,128)S(1)} %copy-done.2, f32[4,128]{1,0:T(4,128)S(1)} %reshape.16.weights_unused.weights), custom_call_target="tpu_custom_call" | custom-call | flops 2000000 | bytes 1048576 | tf_op jit(solution)/shard_map/pallas_call | solution.py:657
  16.6 0.0 collective-permute-done.2.rows_a
  16.6 0.0 collective-permute-done.3.rows_b
  16.6 0.0 copy-start.3
  16.6 0.7 %copy-done.3 = f32[4,16,128]{2,1,0:T(8,128)S(1)} copy-done((f32[4,16,128]{2,1,0:T(8,128)S(1)}, f32[4,16,128]{2,1,0:T(8,128)}, u32[]{:S(2)}) %copy-start.3) | copy-done | bytes 32792
  17.3 0.0 copy-start.8
  17.4 0.7 %copy-done.8 = f32[16,128]{1,0:T(8,128)S(1)} copy-done((f32[16,128]{1,0:T(8,128)S(1)}, f32[16,128]{1,0:T(8,128)}, u32[]{:S(2)}) %copy-start.8) | copy-done | bytes 8216
  18.0 0.0 copy-start.11
  18.0 0.8 %copy-done.11 = f32[4,16,128]{2,1,0:T(8,128)S(1)} copy-done((f32[4,16,128]{2,1,0:T(8,128)S(1)}, f32[4,16,128]{2,1,0:T(8,128)}, u32[]{:S(2)}) %copy-start.11) | copy-done | bytes 32792
  18.8 0.0 copy-start.12
  18.8 0.9 %copy-done.12 = s32[24,16,128]{2,1,0:T(8,128)S(1)} copy-done((s32[24,16,128]{2,1,0:T(8,128)S(1)}, s32[24,16,128]{2,1,0:T(8,128)}, u32[]{:S(2)}) %copy-start.12) | copy-done | bytes 196632
  19.7 0.0 copy-start.13
  19.7 0.8 %copy-done.13 = f32[4,16,128]{2,1,0:T(8,128)S(1)} copy-done((f32[4,16,128]{2,1,0:T(8,128)S(1)}, f32[4,16,128]{2,1,0:T(8,128)}, u32[]{:S(2)}) %copy-start.13) | copy-done | bytes 32792
  20.5 0.0 copy-start.14
  20.5 0.7 %copy-done.14 = s32[16,128]{1,0:T(8,128)S(1)} copy-done((s32[16,128]{1,0:T(8,128)S(1)}, s32[16,128]{1,0:T(8,128)}, u32[]{:S(2)}) %copy-start.14) | copy-done | bytes 8216
  21.2 3.2 %shard_map.98 = (f32[32,24,128]{2,1,0:T(8,128)S(1)}, f32[192,16,128]{2,1,0:T(8,128)S(1)}, f32[4,16,128]{2,1,0:T(8,128)S(1)}, f32[10,32,128]{2,1,0:T(8,128)S(1)}) custom-call(s32[2]{0:T(128)S(1)} %pad_add_fusion.place, f32[4,16,128]{2,1,0:T(8,128)S(1)} %copy-done.11, f32[16,128]{1,0:T(8,128)S(1)} %copy-done.8, f32[4,16,128]{2,1,0:T(8,128)S(1)} %copy-done.3, ...), custom_call_target="tpu_custom_call" | custom-call | flops 2000000 | bytes 1048576 | tf_op jit(solution)/shard_map/pallas_call | solution.py:668
  24.4 22.3 %all_to_all.10.recv = f32[32,24,128]{2,1,0:T(8,128)S(1)} all-to-all(f32[32,24,128]{2,1,0:T(8,128)S(1)} %get-tuple-element.21), channel_id=1, replica_groups=mesh['rng'=8,'xr'=4] {'rng','xr'}, dimensions={0} | all-to-all | bytes 786432 | tf_op jit(solution)/shard_map/all_to_all | solution.py:687
  46.7 0.0 copy-done.4
  46.7 4.1 %shard_map.99 = (f32[4,16,128]{2,1,0:T(8,128)}, f32[4,16,128]{2,1,0:T(8,128)S(1)}, f32[32,2,128]{2,1,0:T(2,128)S(1)}) custom-call(s32[2]{0:T(128)S(1)} %pad_add_fusion.place, f32[32,24,128]{2,1,0:T(8,128)S(1)} %all_to_all.10.recv, f32[192,16,128]{2,1,0:T(8,128)S(1)} %get-tuple-element.22.green, f32[4,16,128]{2,1,0:T(8,128)S(1)} %get-tuple-element.23.source, ...), custom_call_target="tpu_custom_call" | custom-call | flops 2000000 | bytes 1048576 | tf_op jit(solution)/shard_map/pallas_call | solution.py:688
  50.7 12.4 %all_to_all.11.feeds = f32[32,2,128]{2,1,0:T(2,128)S(1)} all-to-all(f32[32,2,128]{2,1,0:T(2,128)S(1)} %get-tuple-element.26), channel_id=1, replica_groups=mesh['rng'=8,'xr'=4] {'rng','xr'}, dimensions={0} | all-to-all | bytes 65536 | tf_op jit(solution)/shard_map/all_to_all | solution.py:705
  63.2 3.4 %shard_map.100 = f32[4,16,128]{2,1,0:T(8,128)} custom-call(s32[2]{0:T(128)S(1)} %pad_add_fusion.place, f32[32,24,128]{2,1,0:T(8,128)S(1)} %all_to_all.10.recv, f32[32,2,128]{2,1,0:T(2,128)S(1)} %all_to_all.11.feeds, f32[4,16,128]{2,1,0:T(8,128)S(1)} %get-tuple-element.27.driven, f32[16,128]{1,0:T(8,128)S(1)} %copy-done.8, f32[4,16,128]{2,1,0:T(8,128)S(1)} %copy-done.4, ...), custom_call_target="tpu_custom_call" | custom-call | flops 2000000 | bytes 1048576 | tf_op jit(solution)/shard_map/pallas_call | solution.py:706
  (1 shorter events, 0.0 us)
Async XLA Ops:
  0.7 0.8 %copy-start = (f32[4,16,128]{2,1,0:T(8,128)S(1)}, f32[4,16,128]{2,1,0:T(8,128)}, u32[]{:S(2)}) copy-start(f32[4,16,128]{2,1,0:T(8,128)} %inverse.11) | copy-start | bytes 98308
  1.5 0.7 %copy-start.5 = (f32[16,128]{1,0:T(8,128)S(1)}, f32[16,128]{1,0:T(8,128)}, u32[]{:S(2)}) copy-start(f32[16,128]{1,0:T(8,128)} %heights.11) | copy-start | bytes 24580
  2.2 0.8 %copy-start.9 = (f32[4,16,128]{2,1,0:T(8,128)S(1)}, f32[4,16,128]{2,1,0:T(8,128)}, u32[]{:S(2)}) copy-start(f32[4,16,128]{2,1,0:T(8,128)} %prev.5) | copy-start | bytes 98308
  2.9 43.7 %copy-start.4 = (f32[4,16,128]{2,1,0:T(8,128)S(1)}, f32[4,16,128]{2,1,0:T(8,128)}, u32[]{:S(2)}) copy-start(f32[4,16,128]{2,1,0:T(8,128)} %inverse.11) | copy-start | bytes 98308
  3.6 4.7 %collective-permute-start = (f32[16,128]{1,0:T(8,128)S(1)}, f32[16,128]{1,0:T(8,128)S(1)}, u32[]{:S(2)}, u32[]{:S(2)}) collective-permute-start(f32[16,128]{1,0:T(8,128)S(1)} %get-tuple-element.15), channel_id=1, source_target_pairs={{0,1},{1,0},{2,3},{3,2},{4,5},{5,4},{6,7},{7,6},{8,9},{9,8},{10,11... | collective-permute-start | bytes 24584 | tf_op jit(solution)/shard_map/ppermute | solution.py:637
  6.7 1.6 %collective-permute-start.1 = (f32[16,128]{1,0:T(8,128)S(1)}, f32[16,128]{1,0:T(8,128)S(1)}, u32[]{:S(2)}, u32[]{:S(2)}) collective-permute-start(f32[16,128]{1,0:T(8,128)S(1)} %get-tuple-element.16), channel_id=1, source_target_pairs={{1,2},{2,1},{5,6},{6,5},{9,10},{10,9},{13,14},{14,13},{17,18},{18,... | collective-permute-start | bytes 24584 | tf_op jit(solution)/shard_map/ppermute | solution.py:637
  8.3 0.8 %copy-start.1 = (f32[4,16,128]{2,1,0:T(8,128)S(1)}, f32[4,16,128]{2,1,0:T(8,128)}, u32[]{:S(2)}) copy-start(f32[4,16,128]{2,1,0:T(8,128)} %inverse.11) | copy-start | bytes 98308
  9.0 0.7 %copy-start.6 = (f32[16,128]{1,0:T(8,128)S(1)}, f32[16,128]{1,0:T(8,128)}, u32[]{:S(2)}) copy-start(f32[16,128]{1,0:T(8,128)} %heights.11) | copy-start | bytes 24580
  9.7 0.8 %copy-start.10 = (f32[4,16,128]{2,1,0:T(8,128)S(1)}, f32[4,16,128]{2,1,0:T(8,128)}, u32[]{:S(2)}) copy-start(f32[4,16,128]{2,1,0:T(8,128)} %prev.5) | copy-start | bytes 98308
  11.1 5.5 %collective-permute-start.2 = (f32[40,128]{1,0:T(8,128)S(1)}, f32[40,128]{1,0:T(8,128)S(1)}, u32[]{:S(2)}, u32[]{:S(2)}) collective-permute-start(f32[40,128]{1,0:T(8,128)S(1)} %get-tuple-element.17), channel_id=1, source_target_pairs={{0,4},{4,0},{8,12},{12,8},{16,20},{20,16},{24,28},{28,24},{1,5},{5... | collective-permute-start | bytes 61448 | tf_op jit(solution)/shard_map/ppermute | solution.py:637
  11.1 5.4 %collective-permute-start.3 = (f32[40,128]{1,0:T(8,128)S(1)}, f32[40,128]{1,0:T(8,128)S(1)}, u32[]{:S(2)}, u32[]{:S(2)}) collective-permute-start(f32[40,128]{1,0:T(8,128)S(1)} %get-tuple-element.18), channel_id=1, source_target_pairs={{4,8},{12,16},{20,24},{8,4},{16,12},{24,20},{5,9},{13,17},{21,25},... | collective-permute-start | bytes 61448 | tf_op jit(solution)/shard_map/ppermute | solution.py:637
  12.8 0.8 %copy-start.2 = (f32[4,16,128]{2,1,0:T(8,128)S(1)}, f32[4,16,128]{2,1,0:T(8,128)}, u32[]{:S(2)}) copy-start(f32[4,16,128]{2,1,0:T(8,128)} %inverse.11) | copy-start | bytes 98308
  13.6 0.7 %copy-start.7 = (f32[16,128]{1,0:T(8,128)S(1)}, f32[16,128]{1,0:T(8,128)}, u32[]{:S(2)}) copy-start(f32[16,128]{1,0:T(8,128)} %heights.11) | copy-start | bytes 24580
  16.6 0.8 %copy-start.3 = (f32[4,16,128]{2,1,0:T(8,128)S(1)}, f32[4,16,128]{2,1,0:T(8,128)}, u32[]{:S(2)}) copy-start(f32[4,16,128]{2,1,0:T(8,128)} %inverse.11) | copy-start | bytes 98308
  17.3 0.7 %copy-start.8 = (f32[16,128]{1,0:T(8,128)S(1)}, f32[16,128]{1,0:T(8,128)}, u32[]{:S(2)}) copy-start(f32[16,128]{1,0:T(8,128)} %heights.11) | copy-start | bytes 24580
  18.0 0.8 %copy-start.11 = (f32[4,16,128]{2,1,0:T(8,128)S(1)}, f32[4,16,128]{2,1,0:T(8,128)}, u32[]{:S(2)}) copy-start(f32[4,16,128]{2,1,0:T(8,128)} %prev.5) | copy-start | bytes 98308
  18.8 0.9 %copy-start.12 = (s32[24,16,128]{2,1,0:T(8,128)S(1)}, s32[24,16,128]{2,1,0:T(8,128)}, u32[]{:S(2)}) copy-start(s32[24,16,128]{2,1,0:T(8,128)} %neighbours.1) | copy-start | bytes 589828
  19.7 0.8 %copy-start.13 = (f32[4,16,128]{2,1,0:T(8,128)S(1)}, f32[4,16,128]{2,1,0:T(8,128)}, u32[]{:S(2)}) copy-start(f32[4,16,128]{2,1,0:T(8,128)} %incident.3) | copy-start | bytes 98308
  20.5 0.7 %copy-start.14 = (s32[16,128]{1,0:T(8,128)S(1)}, s32[16,128]{1,0:T(8,128)}, u32[]{:S(2)}) copy-start(s32[16,128]{1,0:T(8,128)} %counts.1) | copy-start | bytes 24580
where the time goes:
time: 67.6 us; the launch traced here: 66.6 us
  blocking collectives  34.7 us (51%)
  Pallas kernels  14.1 us (21%)
  local copies, waits for them, and re-layouts  12.3 us (18%)
  starting transfers between devices  4.47 us (7%)
  between operations  0.72 us (1%)
    all_to_all x1, blocking collectives, per_device(): recv = lax.all_to_all(payload, BOTH, 0, 0)  22.3 us
    all_to_all x1, blocking collectives, per_device(): feeds = lax.all_to_all(payload, BOTH, 0, 0)  12.4 us
    unnamed x30, local copies, waits for them, and re-layouts  10.5 us
    ppermute x4, starting transfers between devices, swap(): return (lax.ppermute(a, axis, first), lax.ppermute(b, axis, second))  4.47 us
    pallas_call x1, Pallas kernels, per_device(): call(functools.partial(new_body, n_r, n_c, spread), [(2 * F, rows, LANES)...  4.08 us
    pallas_call x1, Pallas kernels, per_device(): call(functools.partial(last_body, n_r, n_c, spread), [(2 * F, rows, LANES...  3.41 us
    pallas_call x1, Pallas kernels, per_device(): call(functools.partial(near_body, n_r, n_c), [(slots, SLOT, LANES), (4 *...  3.18 us
    pallas_call x1, Pallas kernels, per_device(): call(tables_body, [(6, rows, SUB, LANES), (2 * SUB, LANES)], 3, [pltpu.VM...  2.28 us
  transfers between devices with their start and end apart: 4, of which 0 were waited for; matrix products, arithmetic and copies ran while one was open for 3% of the time, Pallas kernels for 3%

commit v1 on v0

v1 whole, which is shorter than its diff:
```python
import functools
import math

import jax
import jax.numpy as jnp
from jax import lax
from jax.experimental import pallas as pl
from jax.experimental.pallas import tpu as pltpu
from jax.sharding import PartitionSpec as P

F = 2
Q = 64
H = 3
LMAX = 24
OFFSETS = 48
SUB = 8
LANES = 128
PERIOD = 64
TOP = SUB
GREEN = 0.25
TURN = 2.0 * math.pi
SLOT = 16
HALO_AT = SUB + 3
HIGHEST = lax.Precision.HIGHEST
BOTH = ("rng", "xr")
f32 = jnp.float32


def iota(shape, dim):
    return lax.broadcasted_iota(jnp.int32, shape, dim)


def roll(x, shift, axis=1):
    shift = shift % x.shape[axis]
    return x if shift == 0 else pltpu.roll(x, shift, axis)


def cos_sin(turns):
    quarter = jnp.floor(4.0 * turns + 0.5)
    rest = turns - 0.25 * quarter
    which = quarter.astype(jnp.int32)
    sq = rest * rest
    s = rest * (TURN + sq * (-(TURN**3) / 6 + sq * (TURN**5 / 120 + sq * (-(TURN**7) / 5040 + sq * (TURN**9 / 362880)))))
    c = 1.0 + sq * (-(TURN**2) / 2 + sq * (TURN**4 / 24 + sq * (-(TURN**6) / 720 + sq * (TURN**8 / 40320))))
    odd = (which & 1) == 1
    cos = jnp.where(odd, s, c)
    sin = jnp.where(odd, c, s)
    cos = jnp.where(((which + 1) & 2) == 2, -cos, cos)
    sin = jnp.where((which & 2) == 2, -sin, sin)
    return cos, sin


def times(a, b):
    return a[0] * b[0] - a[1] * b[1], a[0] * b[1] + a[1] * b[0]


def conj_times(a, b):
    return a[0] * b[0] + a[1] * b[1], a[0] * b[1] - a[1] * b[0]


def wave(step_x, x, step_y, y, lift, heights):
    phase = (step_x * x + step_y * y) & (PERIOD - 1)
    return cos_sin(phase.astype(f32) * (1.0 / PERIOD) + (lift / TURN) * heights)


def offset_of(code):
    full = code + (1 if code >= OFFSETS // 2 else 0)
    return full // (2 * H + 1) - H, full % (2 * H + 1) - H


VMEM = pl.BlockSpec(memory_space=pltpu.VMEM)
PLAIN = pl.BlockSpec()


def call(body, out, ins, scratch=(), flops=2_000_000):
    return pl.pallas_call(
        body,
        out_shape=tuple(jax.ShapeDtypeStruct(s, f32) if isinstance(s, tuple) else s for s in out),
        in_specs=list(ins),
        out_specs=tuple(VMEM for _ in out),
        scratch_shapes=list(scratch),
        compiler_params=pltpu.CompilerParams(vmem_limit_bytes=48 * 1024 * 1024),
        cost_estimate=pl.CostEstimate(flops=flops, bytes_accessed=1 << 20, transcendentals=0),
    )


def place_of():
    return lax.axis_index("rng"), lax.axis_index("xr")


def pack_columns(fields, right):
    rows = fields[0].shape[0]
    lane = iota((rows, LANES), 1)
    packed = jnp.zeros((rows, LANES), f32)
    for k, field in enumerate(fields):
        moved = roll(field, H * k - (LANES - H) if right else H * k)
        packed = jnp.where((lane >= H * k) & (lane < H * (k + 1)), moved, packed)
    return packed


def unpack_columns(from_left, from_right, k):
    lane = iota(from_left.shape, 1)
    left = jnp.where(lane >= LANES - H, roll(from_left, LANES - H - H * k), 0.0)
    return jnp.where(lane < H, roll(from_right, -H * k), left)


def shifted(inner, edge, dy):
    if dy == 0:
        return inner
    lane = iota(inner.shape, 1)
    outside = lane >= LANES - dy if dy > 0 else lane < -dy
    return jnp.where(outside, roll(edge, -dy), roll(inner, -dy))


N_FIELDS = 4 * F + 1
ROWS_SENT = 48
GENS_AT = 40


def columns_body(fields, send_a, send_b):
    values = [fields[k] for k in range(N_FIELDS)]
    right = pack_columns(values, True)
    left = pack_columns(values, False)
    even = (lax.axis_index("xr") & 1) == 0
    send_a[...] = jnp.where(even, right, left)
    send_b[...] = jnp.where(even, left, right)


def rows_body(fields, gens, recv_a, recv_b, send_a, send_b):
    d, c = place_of()
    even_c = (c & 1) == 0
    even_r = (d & 1) == 0
    rows = fields.shape[1]
    values = [fields[k] for k in range(N_FIELDS)]
    values.append(jnp.where(even_c, recv_b[...], recv_a[...]))
    values.append(jnp.where(even_c, recv_a[...], recv_b[...]))
    for k, field in enumerate(values):
        last, first = field[rows - H :], field[:H]
        send_a[H * k : H * (k + 1)] = jnp.where(even_r, last, first)
        send_b[H * k : H * (k + 1)] = jnp.where(even_r, first, last)
    used = H * len(values)
    send_a[used:GENS_AT] = jnp.zeros((GENS_AT - used, LANES), f32)
    send_b[used:GENS_AT] = jnp.zeros((GENS_AT - used, LANES), f32)
    down, up = gens[0:SUB], gens[SUB : 2 * SUB]
    send_a[GENS_AT:] = jnp.where(even_r, down, up)
    send_b[GENS_AT:] = jnp.where(even_r, up, down)


def tables_body(fields, tables, gens, left_mat, right_mat):
    d, c = place_of()
    rows = fields.shape[1]
    x0 = d * rows
    y0 = c * LANES
    angle = iota((2 * SUB, LANES), 0) - SUB
    y = iota((2 * SUB, LANES), 1) + y0
    for i in range(rows):
        x = jnp.full((2 * SUB, LANES), x0 + i, jnp.int32)
        lanes = pl.ds(i * LANES, LANES)
        h2 = jnp.broadcast_to(fields[2 * F, i : i + 1, :], (2 * SUB, LANES)) * angle.astype(f32)
        c2, s2 = wave(0, x, angle, y, 0.03, h2)
        tables[4, i] = c2[SUB:]
        tables[5, i] = s2[SUB:]
        right_mat[0 : 2 * SUB, lanes] = c2
        right_mat[2 * SUB : 4 * SUB, lanes] = s2
        for direction in range(2):
            c1, s1 = wave(angle * (1 - 2 * direction), x, 0, y, 0.24, h2)
            tables[2 * direction, i] = c1[SUB:]
            tables[2 * direction + 1, i] = s1[SUB:]
            for f in range(F):
                zr = fields[2 * F + 1 + 2 * f, i : i + 1, :]
                zi = fields[2 * F + 2 + 2 * f, i : i + 1, :]
                base = (direction * F + f) * 4 * SUB
                left_mat[base : base + 2 * SUB, lanes] = zr * c1 - zi * s1
                left_mat[base + 2 * SUB : base + 4 * SUB, lanes] = zr * s1 + zi * c1
    right_mat[4 * SUB :] = jnp.zeros((right_mat.shape[0] - 4 * SUB, right_mat.shape[1]), f32)
    both = lax.dot_general(
        left_mat[...], right_mat[...], (((1,), (1,)), ((), ())), precision=HIGHEST, preferred_element_type=f32
    )
    lane = iota((SUB, LANES), 1)
    for direction in range(2):
        for f in range(F):
            base = (direction * F + f) * 4 * SUB
            for half in range(2):
                p = both[base + half * SUB : base + (half + 1) * SUB]
                q = both[base + (2 + half) * SUB : base + (3 + half) * SUB]
                for part in range(2):
                    if part == 0:
                        g = p - roll(q, -2 * SUB)
                    else:
                        g = roll(p, -2 * SUB) + q
                    g = jnp.where(lane < 2 * SUB, g, 0.0)
                    g = pltpu.roll(g, 0, 1, stride=2 * SUB, stride_axis=0)
                    row = jnp.sum(g, axis=0, keepdims=True)
                    at = direction * SUB + f * 4 + part * 2 + (1 - half)
                    gens[at : at + 1] = row


def lists_body(lists, params, bits, weights, share):
    count = lists[LMAX]
    low = jnp.zeros(count.shape, jnp.int32)
    high = jnp.zeros(count.shape, jnp.int32)
    half = OFFSETS // 2
    one = jnp.ones(count.shape, jnp.int32)
    for slot in range(LMAX):
        code = lists[slot]
        live = count > slot
        is_low = code < half
        bit = lax.shift_left(one, jnp.where(is_low, code, code - half))
        low = low | jnp.where(live & is_low, bit, 0)
        high = high | jnp.where(live & (code >= half), bit, 0)
    bits[0] = low
    bits[1] = high
    spot = iota((Q, LANES), 0)
    spot = 2 * SUB * (spot // SUB) + (spot & (SUB - 1))
    values = params[...]
    placed = [
        lax.dot_general(
            values,
            (iota((Q, LANES), 1) == spot + SUB * k).astype(f32),
            (((1,), (0,)), ((), ())),
            precision=HIGHEST,
            preferred_element_type=f32,
        )
        for k in range(2)
    ]
    weights[...] = placed[0][: 2 * F] + placed[1][: 2 * F]
    share[...] = placed[0][2 * F : 2 * F + 1] + placed[1][2 * F + 1 : 2 * F + 2]


def project(left_mat, right_mat, tables, first, cs, rows, f_out):
    for i in range(rows):
        lanes = pl.ds(i * LANES, LANES)
        right_mat[0:SUB, lanes] = tables[4, i]
        right_mat[SUB : 2 * SUB, lanes] = tables[5, i]
        c1, s1 = tables[first, i], tables[first + 1, i]
        for f in range(F):
            re, im = conj_times((c1, s1), (cs[2 * f, i : i + 1, :], cs[2 * f + 1, i : i + 1, :]))
            left_mat[2 * f * SUB : (2 * f + 1) * SUB, lanes] = re
            left_mat[(2 * f + 1) * SUB : (2 * f + 2) * SUB, lanes] = im
    sums = lax.dot_general(
        left_mat[0 : 4 * SUB], right_mat[...], (((1,), (1,)), ((), ())), precision=HIGHEST, preferred_element_type=f32
    )
    lane = iota((SUB, LANES), 1)
    for f in range(F):
        gr = sums[2 * f * SUB : (2 * f + 1) * SUB]
        gi = sums[(2 * f + 1) * SUB : (2 * f + 2) * SUB]
        re = gr + roll(gi, -SUB)
        im = gi - roll(gr, -SUB)
        packed = jnp.where(lane < SUB, re, jnp.where(lane < 2 * SUB, roll(im, SUB), 0.0))
        packed = pltpu.roll(packed, 0, 1, stride=2 * SUB, stride_axis=0)
        f_out(f, jnp.sum(packed, axis=0, keepdims=True))


def carrier(f, direction, x, y, heights):
    sign = 1 - 2 * direction
    return wave(sign * (1 + 2 * f), x, f - 4, y, 0.3 + 0.2 * f, heights)


def place_ids(rows, cols, first_row, first_col, own_rows):
    d, c = place_of()
    x = d * own_rows + first_row + iota((rows, cols), 0)
    y = c * LANES + first_col + iota((rows, cols), 1)
    return x, y


def near_body(
    n_r, n_c, fields, fed, bits, share, cols_a, cols_b, rows_a, rows_b, gens, tables,
    payload, green, source, ext, near_gens, inner, edge_l, edge_r, moved, cs, left_mat, right_mat, common, halo,
):
    rows = fields.shape[1]
    d, c = place_of()
    even_c = (c & 1) == 0
    even_r = (d & 1) == 0
    below = jnp.where(even_r, rows_a[...], rows_b[...])
    above = jnp.where(even_r, rows_b[...], rows_a[...])
    near_gens[0] = above[GENS_AT:]
    near_gens[1] = below[GENS_AT:]
    edge_l[...] = jnp.zeros(edge_l.shape, f32)
    edge_r[...] = jnp.zeros(edge_r.shape, f32)
    edge_l[TOP : TOP + rows] = jnp.where(even_c, cols_b[...], cols_a[...])
    edge_r[TOP : TOP + rows] = jnp.where(even_c, cols_a[...], cols_b[...])
    at = H * N_FIELDS
    edge_l[TOP - H : TOP] = above[at : at + H]
    edge_l[TOP + rows : TOP + rows + H] = below[at : at + H]
    edge_r[TOP - H : TOP] = above[at + H : at + 2 * H]
    edge_r[TOP + rows : TOP + rows + H] = below[at + H : at + 2 * H]
    from_left, from_right = edge_l[...], edge_r[...]
    for k in range(N_FIELDS):
        inner[k] = jnp.zeros(inner.shape[1:], f32)
        inner[k, TOP : TOP + rows] = fields[k]
        inner[k, TOP - H : TOP] = above[H * k : H * (k + 1)]
        inner[k, TOP + rows : TOP + rows + H] = below[H * k : H * (k + 1)]
        side = unpack_columns(from_left, from_right, k)
        if k >= 2 * F:
            ext[2 * (k - 2 * F)] = inner[k]
            ext[2 * (k - 2 * F) + 1] = side
        if k <= 2 * F:
            middle = inner[k]
            for dy in range(-H, H + 1):
                moved[k * (2 * H + 1) + dy + H] = shifted(middle, side, dy)
    h = fields[2 * F]
    inverse = [fields[2 * F + 1 + k] for k in range(2 * F)]
    incident = [fed[k] for k in range(2 * F)]
    low, high = bits[0], bits[1]
    half = OFFSETS // 2
    near = [jnp.zeros((rows, LANES), f32) for _ in range(2 * F)]
    for code in range(OFFSETS):
        dx, dy = offset_of(code)
        window = lambda k: moved[k * (2 * H + 1) + dy + H, TOP + dx : TOP + dx + rows]
        lift = window(2 * F) - h
        squared = float(dx * dx + dy * dy) + lift * lift
        inverse_r = lax.rsqrt(squared)
        r = squared * inverse_r
        bits = low if code < half else high
        there = (bits & (1 << (code % half))) != 0
        size = jnp.where(there, GREEN * inverse_r, 0.0)
        for f in range(F):
            cos, sin = cos_sin(r * (0.25 * (1.0 + 0.25 * f)))
            g = (size * cos, size * sin)
            green[4 * code + 2 * f] = g[0]
            green[4 * code + 2 * f + 1] = g[1]
            got = times(g, (window(2 * f), window(2 * f + 1)))
            near[2 * f] += got[0]
            near[2 * f + 1] += got[1]
    x, y = place_ids(rows, LANES, 0, 0, rows)
    sources = []
    for f in range(F):
        z = (inverse[2 * f], inverse[2 * f + 1])
        s = times(z, (incident[2 * f] - near[2 * f], incident[2 * f + 1] - near[2 * f + 1]))
        sources += s
        source[2 * f] = s[0]
        source[2 * f + 1] = s[1]
        got = conj_times(carrier(f, 0, x, y, h), s)
        cs[2 * f] = got[0]
        cs[2 * f + 1] = got[1]

    def keep(f, row):
        common[2 * SUB + f : 2 * SUB + f + 1] = row

    right_mat[2 * SUB :] = jnp.zeros((right_mat.shape[0] - 2 * SUB, right_mat.shape[1]), f32)
    common[2 * SUB :] = jnp.zeros((SUB, LANES), f32)
    project(left_mat, right_mat, tables, 0, cs, rows, keep)
    common[0 : 2 * SUB] = gens[...]
    common[2 * SUB + 2 : 2 * SUB + 3] = share[...]
    tail = common[2 * SUB : 3 * SUB]
    for direction in range(2):
        part = common[direction * SUB : (direction + 1) * SUB]

        def fill(s, _, part=part, tail=tail):
            payload[s, 0:SUB] = part
            payload[s, SUB : 2 * SUB] = tail
            return 0

        if direction == 0:
            lax.fori_loop(d * n_c, n_r * n_c, fill, 0)
        else:
            lax.fori_loop(0, d * n_c, fill, 0)
    lasts = pack_columns(sources, True)
    firsts = pack_columns(sources, False)
    at = HALO_AT

    def send(dr, dc, put):
        dst = (d + dr) * n_c + c + dc
        ok = (d + dr >= 0) & (d + dr < n_r) & (c + dc >= 0) & (c + dc < n_c)

        @pl.when(ok)
        def _():
            put(dst)

    def rows_to(dr):
        for k in range(2 * F):
            s = sources[k]
            halo[H * k : H * (k + 1)] = s[rows - H :] if dr > 0 else s[:H]
        first, rest = halo[0:SUB], halo[SUB : 2 * F * H]

        def put(dst):
            payload[dst, 0:SUB] = first
            payload[dst, at : at + 2 * F * H - SUB] = rest

        return put

    def cols_to(dc):
        packed = lasts if dc > 0 else firsts
        quarter = rows // 4
        parts = [roll(packed, 4 * SUB * i)[quarter * i : quarter * (i + 1)] for i in range(4)]
        packed = parts[0] + parts[1] + parts[2] + parts[3]

        def put(dst):
            payload[dst, at : at + quarter] = packed

        return put

    def corner_to(dr, dc):
        packed = lasts if dc > 0 else firsts

        def put(dst):
            payload[dst, at : at + H] = packed[rows - H :] if dr > 0 else packed[:H]

        return put

    for dr in (-1, 1):
        send(dr, 0, rows_to(dr))
        send(0, dr, cols_to(dr))
        for dc in (-1, 1):
            send(dr, dc, corner_to(dr, dc))


def toeplitz(gens, sub, lane):
    wide = [jnp.broadcast_to(gens[k : k + 1], (SUB, LANES)) for k in range(4)]
    low = (lane & SUB) == 0

    def tile(part, by):
        inside = (lane >= by + sub) & (lane < by + sub + LANES)
        one = pltpu.roll(wide[2 * part], by % LANES, 1, stride=1, stride_axis=0)
        two = pltpu.roll(wide[2 * part + 1], by % LANES, 1, stride=1, stride_axis=0)
        return jnp.where(inside, one, two)

    out = []
    for a1 in range(Q // SUB):
        by = 2 * SUB * a1 - SUB
        out.append(jnp.where(low, tile(0, by), -tile(1, by + SUB)))
    for a1 in range(Q // SUB):
        by = 2 * SUB * a1 - SUB
        out.append(jnp.where(low, tile(1, by), tile(0, by + SUB)))
    return out


def to_columns(row, sub, lane):
    return [
        jnp.sum(jnp.where(lane == 2 * SUB * a1 + SUB * part + sub, row, 0.0), axis=1, keepdims=True)
        for part in range(2)
        for a1 in range(Q // SUB)
    ]


def to_row(columns, sub, lane):
    total = jnp.zeros((SUB, LANES), f32)
    for k, column in enumerate(columns):
        part, a1 = k // (Q // SUB), k % (Q // SUB)
        total = jnp.where(lane == 2 * SUB * a1 + SUB * part + sub, column, total)
    return jnp.broadcast_to(jnp.sum(total, axis=0, keepdims=True), (SUB, LANES))


def wide(row):
    return jnp.broadcast_to(row, (SUB, LANES))


def packed_times(wr, wi, row, low):
    turned = jnp.where(low, -roll(row, -SUB), roll(row, SUB))
    return wr * row + wi * turned


def sweep_step(maps, feeds, shares, weights, carry, spread):
    sub = iota((SUB, LANES), 0)
    lane = iota((SUB, LANES), 1)
    low = (lane & SUB) == 0
    out = []
    for f in range(F):
        amp = packed_times(weights[2 * f], weights[2 * f + 1], carry[f], low)
        columns = [jnp.sum(maps(f, k) * amp, axis=1, keepdims=True) for k in range(2 * Q // SUB)]
        out.append(shares[f] * (carry[f] + feeds[f] - spread * to_row(columns, sub, lane)))
    return out


def shares_of(row):
    lane = iota((SUB, LANES), 1)
    low = (lane & SUB) == 0
    row = wide(row)
    return jnp.where(low, row, roll(row, SUB)), jnp.where(low, roll(row, -SUB), row)


def put_amplitudes(put, weights, carry, spread):
    sub = iota((SUB, LANES), 0)
    lane = iota((SUB, LANES), 1)
    low = (lane & SUB) == 0
    for f in range(F):
        amp = spread * packed_times(weights[2 * f], weights[2 * f + 1], carry[f], low)
        for k, column in enumerate(to_columns(amp, sub, lane)):
            put(f, slice(SUB * k, SUB * (k + 1)), jnp.broadcast_to(column, (SUB, LANES)))


def laps(n, body):
    if n <= SUB:
        for j in range(n):
            body(j)
    else:
        lax.fori_loop(0, n, lambda j, _: (body(j), 0)[1], 0)


def gens_sum(recv, j, n_c, d, c, step, own):
    total = None
    for k in range(n_c):
        part = recv[j * n_c + k, 0:SUB]
        part = jnp.where((j == d + step) & (k == c), own, part)
        total = part if total is None else total + part
    return total


def store_maps(maps, j, gens):
    sub = iota((SUB, LANES), 0)
    lane = iota((SUB, LANES), 1)
    for f in range(F):
        for k, tile in enumerate(toeplitz(gens[4 * f : 4 * f + 4], sub, lane)):
            maps[j, f, SUB * k : SUB * (k + 1)] = tile


def powers(base, count):
    out = [None, base]
    for _ in range(2, count):
        out.append(times(out[-1], base))
    return out


def wave_powers(direction, x, y, heights):
    u1 = powers(wave(1 - 2 * direction, x, 0, y, 0.24, heights), Q // SUB)
    u2 = powers(wave(0, x, 1, y, 0.03, heights), SUB)
    return u1, u2


def radiated(f, splat, u1, u2, carried):
    total = None
    for a1 in range(Q // SUB):
        ar, ai = splat(f, SUB * a1), splat(f, Q + SUB * a1)
        inner = (ar, ai)
        for a2 in range(1, SUB):
            got = times((splat(f, SUB * a1 + a2), splat(f, Q + SUB * a1 + a2)), u2[a2])
            inner = (inner[0] + got[0], inner[1] + got[1])
        if a1 == 0:
            total = inner
        else:
            got = times(u1[a1], inner)
            total = (total[0] + got[0], total[1] + got[1])
    return times(carried, total)


def back_body(n_r, n_c, recv, near_gens, maps):
    d, c = place_of()
    below = near_gens[1]

    def body(j):
        store_maps(maps, j, gens_sum(recv, j + 1, n_c, d, c, 1, below))

    laps(n_r - 1, body)


def new_body(
    n_r, n_c, spread, recv, green, source, ext, fields, fed, near_gens, tables, weights,
    forward, driven, payload, maps, feeds, carries, amps, inner, moved, edge_l, edge_r, cs, left_mat, right_mat, common, halo,
):
    rows = fields.shape[1]
    d, c = place_of()
    wts = [wide(weights[k : k + 1]) for k in range(2 * F)]
    zero = jnp.zeros((SUB, LANES), f32)
    above = near_gens[0]

    def prepare(j):
        store_maps(maps, j, gens_sum(recv, j, n_c, d, c, -1, above))
        feed = recv[j * n_c, SUB : 2 * SUB]
        for k in range(1, n_c):
            feed = feed + recv[j * n_c + k, SUB : 2 * SUB]
        feeds[j] = feed

    laps(n_r - 1, prepare)
    for f in range(F):
        carries[0, f] = zero

    def lap(j, carry):
        new = sweep_step(
            lambda f, k: maps[j, f, SUB * k : SUB * (k + 1)],
            [wide(feeds[j, f : f + 1]) for f in range(F)],
            shares_of(recv[j * n_c, SUB + 2 : SUB + 3]),
            wts,
            carry,
            spread,
        )
        for f in range(F):
            carries[j + 1, f] = new[f]
        return tuple(new)

    lax.fori_loop(0, jnp.minimum(d + 1, n_r - 1), lap, (zero,) * F)
    for which in range(3):
        at = jnp.clip(d + which - 1, 0, n_r - 1)

        def put(f, at_rows, tile, which=which):
            amps[which, f, at_rows] = tile

        put_amplitudes(put, wts, [carries[at, f] for f in range(F)], spread)

    at = HALO_AT

    def got(dr, dc, start, size):
        src = jnp.clip(d + dr, 0, n_r - 1) * n_c + jnp.clip(c + dc, 0, n_c - 1)
        ok = (d + dr >= 0) & (d + dr < n_r) & (c + dc >= 0) & (c + dc < n_c)
        return jnp.where(ok, recv[src, start : start + size], 0.0)

    edge_l[...] = jnp.zeros(edge_l.shape, f32)
    edge_r[...] = jnp.zeros(edge_r.shape, f32)
    quarter = rows // 4
    for edge, dc in ((edge_l, -1), (edge_r, 1)):
        side = got(0, dc, at, quarter)
        for i in range(4):
            edge[TOP + quarter * i : TOP + quarter * (i + 1)] = roll(side, -4 * SUB * i)
        edge[TOP - H : TOP] = got(-1, dc, at, H)
        edge[TOP + rows : TOP + rows + H] = got(1, dc, at, H)
    from_left, from_right = edge_l[...], edge_r[...]
    for i, dr in enumerate((-1, 1)):
        halo[i, 0:SUB] = got(dr, 0, 0, SUB)
        halo[i, SUB : 2 * F * H] = got(dr, 0, at, 2 * F * H - SUB)
    for k in range(2 * F):
        inner[k] = jnp.zeros(inner.shape[1:], f32)
        inner[k, TOP : TOP + rows] = source[k]
        inner[k, TOP - H : TOP] = halo[0, H * k : H * (k + 1)]
        inner[k, TOP + rows : TOP + rows + H] = halo[1, H * k : H * (k + 1)]
    sides = [unpack_columns(from_left, from_right, k) for k in range(2 * F)]

    weak = {}
    tiles = (rows + 2 * SUB) // SUB
    for tile in range(tiles):
        which = 0 if tile == 0 else 2 if tile == tiles - 1 else 1
        splat = lambda f, a, which=which: amps[which, f, a : a + 1]
        rows_at = slice(SUB * tile, SUB * (tile + 1))
        for side in range(2):
            x, y = place_ids(SUB, LANES, SUB * tile - TOP, 0, rows)
            if side == 1:
                lane = iota((SUB, LANES), 1)
                y = y + jnp.where(lane < LANES // 2, LANES, -LANES)
            h = ext[side, rows_at]
            u1, u2 = wave_powers(0, x, y, h)
            for f in range(F):
                w = radiated(f, splat, u1, u2, carrier(f, 0, x, y, h))
                z = (ext[2 * (1 + 2 * f) + side, rows_at], ext[2 * (2 + 2 * f) + side, rows_at])
                lost = times(z, w)
                for part in range(2):
                    k = 2 * f + part
                    if side == 0:
                        inner[k, rows_at] = inner[k, rows_at] - lost[part]
                        weak[tile, k] = w[part]
                    else:
                        sides[k] = (sides[k] if isinstance(sides[k], list) else [sides[k]]) + [
                            sides_tile(sides[k], rows_at) - lost[part]
                        ]
    for k in range(2 * F):
        side = jnp.concatenate(sides[k][1:], axis=0)
        middle = inner[k]
        forward[k] = middle[TOP : TOP + rows]
        for dy in range(-H, H + 1):
            moved[k * (2 * H + 1) + dy + H] = shifted(middle, side, dy)
    near = [jnp.zeros((rows, LANES), f32) for _ in range(2 * F)]
    for code in range(OFFSETS):
        dx, dy = offset_of(code)
        window = lambda k: moved[k * (2 * H + 1) + dy + H, TOP + dx : TOP + dx + rows]
        for f in range(F):
            g = (green[4 * code + 2 * f], green[4 * code + 2 * f + 1])
            add = times(g, (window(2 * f), window(2 * f + 1)))
            near[2 * f] += add[0]
            near[2 * f + 1] += add[1]
    x, y = place_ids(rows, LANES, 0, 0, rows)
    h = fields[2 * F]
    for f in range(F):
        rest = []
        for part in range(2):
            k = 2 * f + part
            w = jnp.concatenate([weak[tile, k] for tile in range(1, tiles - 1)], axis=0)
            rest.append(fed[k] - near[k] - w)
        s = times((fields[2 * F + 1 + 2 * f], fields[2 * F + 2 + 2 * f]), rest)
        driven[2 * f] = s[0]
        driven[2 * f + 1] = s[1]
        add = conj_times(carrier(f, 1, x, y, h), s)
        cs[2 * f] = add[0]
        cs[2 * f + 1] = add[1]

    def keep(f, row):
        common[f : f + 1] = row

    right_mat[2 * SUB :] = jnp.zeros((right_mat.shape[0] - 2 * SUB, right_mat.shape[1]), f32)
    project(left_mat, right_mat, tables, 2, cs, rows, keep)
    pair = common[0:2]

    def fill(s, _):
        payload[s] = pair
        return 0

    lax.fori_loop(0, n_r * n_c, fill, 0)


def sides_tile(side, rows_at):
    return side[0][rows_at] if isinstance(side, list) else side[rows_at]


def last_body(n_r, n_c, spread, recv, maps, feeds, driven, fields, weights, currents, amps):
    rows = fields.shape[1]
    d, _ = place_of()
    wts = [wide(weights[k : k + 1]) for k in range(2 * F)]
    zero = jnp.zeros((SUB, LANES), f32)

    def lap(k, carry):
        j = n_r - 1 - k
        feed = feeds[j * n_c]
        for i in range(1, n_c):
            feed = feed + feeds[j * n_c + i]
        new = sweep_step(
            lambda f, k: maps[j - 1, f, SUB * k : SUB * (k + 1)],
            [wide(feed[f : f + 1]) for f in range(F)],
            shares_of(recv[j * n_c, SUB + 2 : SUB + 3]),
            wts,
            carry,
            spread,
        )
        return tuple(new)

    carry = lax.fori_loop(0, n_r - 1 - d, lap, (zero,) * F)

    def put(f, at_rows, tile):
        amps[f, at_rows] = tile

    put_amplitudes(put, wts, carry, spread)
    splat = lambda f, a: amps[f, a : a + 1]
    for tile in range(rows // SUB):
        rows_at = slice(SUB * tile, SUB * (tile + 1))
        x, y = place_ids(SUB, LANES, SUB * tile, 0, rows)
        h = fields[2 * F, rows_at]
        u1, u2 = wave_powers(1, x, y, h)
        for f in range(F):
            w = radiated(f, splat, u1, u2, carrier(f, 1, x, y, h))
            lost = times((fields[2 * F + 1 + 2 * f, rows_at], fields[2 * F + 2 + 2 * f, rows_at]), w)
            currents[2 * f, rows_at] = driven[2 * f, rows_at] - lost[0]
            currents[2 * f + 1, rows_at] = driven[2 * f + 1, rows_at] - lost[1]


def swaps(n):
    first = [(i, i ^ 1) for i in range(n) if i ^ 1 < n]
    second = [(i, i + 1) for i in range(1, n - 1, 2)] + [(i + 1, i) for i in range(1, n - 1, 2)]
    return first, second


def swap(axis, n, a, b):
    first, second = swaps(n)
    b = lax.ppermute(b, axis, second)
    return lax.ppermute(a, axis, first), b


def per_device(n_r, n_c, incident, inverse_diag, previous, heights, neighbours, counts, transmit, angle_weights):
    rows, cols = heights.shape
    patches = rows * cols
    spread = 1.0 / math.sqrt(rows * cols * n_c)
    slots = n_r * n_c
    tall = rows + 2 * SUB
    fields = jnp.concatenate([previous, heights[None], inverse_diag])
    cols_a, cols_b = call(columns_body, [(rows, LANES)] * 2, [VMEM], flops=500_000)(fields)
    cols_a, cols_b = swap("xr", n_c, cols_a, cols_b)
    tables, gens = call(
        tables_body,
        [(6, rows, SUB, LANES), (2 * SUB, LANES)],
        [VMEM],
        [pltpu.VMEM((16 * SUB, patches), f32), pltpu.VMEM((16 * SUB, patches), f32)],
    )(fields)
    rows_a, rows_b = call(rows_body, [(ROWS_SENT, LANES)] * 2, [VMEM] * 4, flops=500_000)(fields, gens, cols_a, cols_b)
    rows_a, rows_b, neighbours, counts, transmit, angle_weights = lax.optimization_barrier(
        (rows_a, rows_b, neighbours, counts, transmit, angle_weights)
    )
    rows_a, rows_b = swap("rng", n_r, rows_a, rows_b)
    lists = jnp.concatenate([neighbours, counts[None]])
    params = jnp.concatenate([angle_weights.reshape(2 * F, Q), transmit.reshape(F, Q)])
    bits, weights, share = call(
        lists_body, [jax.ShapeDtypeStruct((2, rows, LANES), jnp.int32), (2 * F, LANES), (1, LANES)], [VMEM] * 2
    )(lists, params)
    payload, green, source, ext, near_gens = call(
        functools.partial(near_body, n_r, n_c),
        [
            (slots, SLOT, LANES),
            (4 * OFFSETS, rows, LANES),
            (2 * F, rows, LANES),
            (4 * F + 2, tall, LANES),
            (2, SUB, LANES),
        ],
        [VMEM] * 10,
        [
            pltpu.VMEM((N_FIELDS, tall, LANES), f32),
            pltpu.VMEM((tall, LANES), f32),
            pltpu.VMEM((tall, LANES), f32),
            pltpu.VMEM(((2 * F + 1) * (2 * H + 1), tall, LANES), f32),
            pltpu.VMEM((2 * F, rows, LANES), f32),
            pltpu.VMEM((4 * SUB, patches), f32),
            pltpu.VMEM((16 * SUB, patches), f32),
            pltpu.VMEM((3 * SUB, LANES), f32),
            pltpu.VMEM((2 * SUB, LANES), f32),
        ],
    )(fields, incident, bits, share, cols_a, cols_b, rows_a, rows_b, gens, tables)
    recv = lax.all_to_all(payload, BOTH, 0, 0)
    forward, driven, payload = call(
        functools.partial(new_body, n_r, n_c, spread),
        [(2 * F, rows, LANES), (2 * F, rows, LANES), (slots, 2, LANES)],
        [VMEM] * 9,
        [
            pltpu.VMEM((n_r - 1, F, 2 * Q, LANES), f32),
            pltpu.VMEM((n_r - 1, SUB, LANES), f32),
            pltpu.VMEM((n_r, F, SUB, LANES), f32),
            pltpu.VMEM((3, F, 2 * Q, LANES), f32),
            pltpu.VMEM((2 * F, tall, LANES), f32),
            pltpu.VMEM((2 * F * (2 * H + 1), tall, LANES), f32),
            pltpu.VMEM((tall, LANES), f32),
            pltpu.VMEM((tall, LANES), f32),
            pltpu.VMEM((2 * F, rows, LANES), f32),
            pltpu.VMEM((4 * SUB, patches), f32),
            pltpu.VMEM((16 * SUB, patches), f32),
            pltpu.VMEM((SUB, LANES), f32),
            pltpu.VMEM((2, 2 * SUB, LANES), f32),
        ],
    )(recv, green, source, ext, fields, incident, near_gens, tables, weights)
    feeds = lax.all_to_all(payload, BOTH, 0, 0)
    (maps,) = call(functools.partial(back_body, n_r, n_c), [(n_r - 1, F, 2 * Q, LANES)], [VMEM] * 2)(recv, near_gens)
    (currents,) = call(
        functools.partial(last_body, n_r, n_c, spread),
        [(2 * F, rows, LANES)],
        [VMEM] * 6,
        [pltpu.VMEM((F, 2 * Q, LANES), f32)],
    )(recv, maps, feeds, driven, fields, weights)
    return forward, currents


def solution(mesh):
    body = functools.partial(per_device, mesh.shape["rng"], mesh.shape["xr"])
    field = P(None, "rng", "xr")
    return jax.shard_map(
        body,
        mesh=mesh,
        in_specs=(field, field, field, P("rng", "xr"), field, P("rng", "xr"), P("rng", None, None), P()),
        out_specs=(field, field),
        check_vma=False,
    )
```

time: 67.6 us -> 52.1 us (0.77)
  blocking collectives: 34.7 us -> 20.6 us
  local copies, waits for them, and re-layouts: 12.3 us -> 0.76 us
  waiting for transfers between devices: 0.05 us -> 6.27 us
  starting transfers between devices: 4.47 us -> 8.22 us
  other arithmetic: 0.15 us -> 2.47 us
  Pallas kernels: 14.1 us -> 12.7 us
    all_to_all x1 -> x0, blocking collectives: 12.4 us -> none  [per_device(): feeds = lax.all_to_all(payload, BOTH, 0, 0)]
    unnamed x30 -> x2, local copies, waits for them, and re-layouts: 10.5 us -> 0.76 us
    all_to_all x0 -> x1, waiting for transfers between devices: none -> 6.26 us  [per_device(): feeds = lax.all_to_all(payload, BOTH, 0, 0)]
    all_to_all x0 -> x1, starting transfers between devices: none -> 3.75 us  [per_device(): feeds = lax.all_to_all(payload, BOTH, 0, 0)]
    concatenate x1 -> x3, other arithmetic: 0.08 us -> 2.47 us  [the longest x1 0.96 us: per_device(): lists = jnp.concatenate([neighbours, counts[None]])]
    all_to_all x1, blocking collectives: 22.3 us -> 20.6 us  [per_device(): recv = lax.all_to_all(payload, BOTH, 0, 0)]
    pallas_call x1, Pallas kernels: 3.41 us -> 2.45 us  [per_device(): call(functools.partial(last_body, n_r, n_c, spread), [(2 * F, rows, LANES...]
    slice x1 -> x0, local copies, waits for them, and re-layouts: 0.77 us -> none  [per_device(): share = jnp.concatenate([share[0], share[1]], -1).reshape(1, 2 * Q)]
  transfers between devices with their start and end apart: 4 -> 5, of which waited for: 0 -> 1; matrix products, arithmetic and copies ran while one was open for 3% -> 3% of each run, Pallas kernels for 3% -> 6%
where the time goes in v1:
time: 52.1 us; the launch traced here: 51.7 us
  blocking collectives  20.6 us (40%)
  Pallas kernels  12.7 us (24%)
  starting transfers between devices  8.22 us (16%)
  waiting for transfers between devices  6.27 us (12%)
  other arithmetic  2.47 us (5%)
  local copies, waits for them, and re-layouts  0.76 us (1%)
  between operations  0.72 us (1%)
    all_to_all x1, blocking collectives, per_device(): recv = lax.all_to_all(payload, BOTH, 0, 0)  20.6 us
    all_to_all x1, waiting for transfers between devices, per_device(): feeds = lax.all_to_all(payload, BOTH, 0, 0)  6.26 us
    pallas_call x1, Pallas kernels, per_device(): call(functools.partial(new_body, n_r, n_c, spread), [(2 * F, rows, LANES)...  4.58 us
    all_to_all x1, starting transfers between devices, per_device(): feeds = lax.all_to_all(payload, BOTH, 0, 0)  3.75 us
    ppermute x2, starting transfers between devices, swap(): return (lax.ppermute(a, axis, first), b)  3.16 us
    pallas_call x1, Pallas kernels, per_device(): call(functools.partial(near_body, n_r, n_c), [(slots, SLOT, LANES), (4 *...  2.63 us
    pallas_call x1, Pallas kernels, per_device(): call(functools.partial(last_body, n_r, n_c, spread), [(2 * F, rows, LANES...  2.45 us
    pallas_call x1, Pallas kernels, per_device(): call(tables_body, [(6, rows, SUB, LANES), (2 * SUB, LANES)], [VMEM], [plt...  1.67 us
  transfers between devices with their start and end apart: 5, of which 1 were waited for; matrix products, arithmetic and copies ran while one was open for 3% of the time, Pallas kernels for 6%

profile of v1, /device:TPU:0, one launch (start us, length us, event | category | flops | bytes accessed | tf_op | source)
XLA Modules:
  0.0 51.7 jit_solution(16648896595490185747)
XLA Ops:
  0.6 0.8 %pad_maximum_fusion.fields = f32[9,16,128]{2,1,0:T(8,128)S(1)} fusion(f32[4,16,128]{2,1,0:T(8,128)} %param.9, f32[1,16,128]{2,1,0:T(8,128)} %bitcast.4, f32[4,16,128]{2,1,0:T(8,128)} %param.10), kind=kLoop, calls=%fused_computation.1 | loop fusion | flops 36864 | bytes 147456 | tf_op jit(solution)/shard_map/concatenate | solution.py:748
  1.4 0.1 shard_map.96
  1.5 3.1 %collective-permute-start = (f32[16,128]{1,0:T(8,128)S(1)}, f32[16,128]{1,0:T(8,128)S(1)}, u32[]{:S(2)}, u32[]{:S(2)}) collective-permute-start(f32[16,128]{1,0:T(8,128)S(1)} %get-tuple-element.26), channel_id=1, source_target_pairs={{0,1},{1,0},{2,3},{3,2},{4,5},{5,4},{6,7},{7,6},{8,9},{9,8},{10,11... | collective-permute-start | bytes 24584 | tf_op jit(solution)/shard_map/ppermute | solution.py:739
  4.6 0.6 %collective-permute-start.1 = (f32[16,128]{1,0:T(8,128)S(1)}, f32[16,128]{1,0:T(8,128)S(1)}, u32[]{:S(2)}, u32[]{:S(2)}) collective-permute-start(f32[16,128]{1,0:T(8,128)S(1)} %get-tuple-element.27), channel_id=1, source_target_pairs={{1,2},{2,1},{5,6},{6,5},{9,10},{10,9},{13,14},{14,13},{17,18},{18,... | collective-permute-start | bytes 24584 | tf_op jit(solution)/shard_map/ppermute | solution.py:738
  5.3 1.7 %shard_map.95 = (f32[6,16,8,128]{3,2,1,0:T(8,128)S(1)}, f32[16,128]{1,0:T(8,128)S(1)}) custom-call(f32[9,16,128]{2,1,0:T(8,128)S(1)} %pad_maximum_fusion.fields), custom_call_target="tpu_custom_call" | custom-call | flops 2000000 | bytes 1048576 | tf_op jit(solution)/shard_map/pallas_call | solution.py:751
  7.0 0.0 collective-permute-done.recv_a.cols_a
  7.0 0.0 collective-permute-done.1.recv_b.cols_b
  7.0 0.1 collective-permute-start.2
  7.1 0.7 %collective-permute-start.3 = (f32[48,128]{1,0:T(8,128)S(1)}, f32[48,128]{1,0:T(8,128)S(1)}, u32[]{:S(2)}, u32[]{:S(2)}) collective-permute-start(f32[48,128]{1,0:T(8,128)S(1)} %get-tuple-element.37), channel_id=1, source_target_pairs={{4,8},{12,16},{20,24},{8,4},{16,12},{24,20},{5,9},{13,17},{21,25},... | collective-permute-start | bytes 73736 | tf_op jit(solution)/shard_map/ppermute | solution.py:738
  7.8 1.0 %pad_add_fusion.lists = s32[25,16,128]{2,1,0:T(8,128)S(1)} fusion(s32[1,16,128]{2,1,0:T(8,128)} %bitcast.5, s32[24,16,128]{2,1,0:T(8,128)} %param.12), kind=kLoop, calls=%fused_computation | loop fusion | flops 51200 | bytes 409600 | tf_op jit(solution)/shard_map/concatenate | solution.py:762
  8.7 0.7 %pad_maximum_fusion.1.params = f32[6,64]{1,0:T(8,128)S(1)} fusion(f32[2,64]{1,0:T(2,128)} %bitcast.7, f32[4,64]{1,0:T(4,128)} %bitcast.6), kind=kLoop, calls=%fused_computation.2 | loop fusion | flops 384 | bytes 3072 | tf_op jit(solution)/shard_map/concatenate | solution.py:763
  9.4 0.2 shard_map.98
  9.7 0.0 collective-permute-done.2.rows_a
  9.7 0.0 collective-permute-done.3.rows_b
  9.7 0.0 copy-start
  9.7 0.8 %copy-done = f32[4,16,128]{2,1,0:T(8,128)S(1)} copy-done((f32[4,16,128]{2,1,0:T(8,128)S(1)}, f32[4,16,128]{2,1,0:T(8,128)}, u32[]{:S(2)}) %copy-start) | copy-done | bytes 32792
  10.5 2.6 %shard_map.99 = (f32[32,16,128]{2,1,0:T(8,128)S(1)}, f32[192,16,128]{2,1,0:T(8,128)S(1)}, f32[4,16,128]{2,1,0:T(8,128)S(1)}, f32[10,32,128]{2,1,0:T(8,128)S(1)}, f32[2,8,128]{2,1,0:T(8,128)S(1)}) custom-call(f32[9,16,128]{2,1,0:T(8,128)S(1)} %pad_maximum_fusion.fields, f32[4,16,128]{2,1,0:T(8,128)S(1)} %copy-done, s32[2,16,128]{2,1,0:T(8,128)S(1)} %get-tuple-element.34.bits, ...), custom_call_target="tpu_custom_call" | custom-call | flops 2000000 | bytes 1048576 | tf_op jit(solution)/shard_map/pallas_call | solution.py:767
  13.1 20.6 %all_to_all.10.recv = f32[32,16,128]{2,1,0:T(8,128)S(1)} all-to-all(f32[32,16,128]{2,1,0:T(8,128)S(1)} %get-tuple-element.39), channel_id=1, replica_groups=mesh['rng'=8,'xr'=4] {'rng','xr'}, dimensions={0} | all-to-all | bytes 524288 | tf_op jit(solution)/shard_map/all_to_all | solution.py:789
  33.7 4.6 %shard_map.100 = (f32[4,16,128]{2,1,0:T(8,128)}, f32[4,16,128]{2,1,0:T(8,128)S(1)}, f32[32,2,128]{2,1,0:T(2,128)}) custom-call(f32[32,16,128]{2,1,0:T(8,128)S(1)} %all_to_all.10.recv, f32[192,16,128]{2,1,0:T(8,128)S(1)} %get-tuple-element.40.green, f32[4,16,128]{2,1,0:T(8,128)S(1)} %get-tuple-element.41.source, f32[10,32,128]{2,1,0:T(8,128)S(1)} %get-tuple-element.42.ext, ...), custom_call_target="tpu_custom_call" | custom-call | flops 2000000 | bytes 1048576 | tf_op jit(solution)/shard_map/pallas_call | solution.py:790
  38.2 3.8 %all-to-all-start.1 = ((f32[32,2,128]{2,1,0:T(2,128)}), f32[32,2,128]{2,1,0:T(2,128)S(1)}, u32[]{:S(2)}, u32[]{:S(2)}) async-start(f32[32,2,128]{2,1,0:T(2,128)} %get-tuple-element.46), calls=%async_computation.1 | async-start | bytes 65536 | tf_op jit(solution)/shard_map/all_to_all | solution.py:810
  42.0 1.0 %shard_map.101.maps = f32[7,2,128,128]{3,2,1,0:T(8,128)S(1)} custom-call(f32[32,16,128]{2,1,0:T(8,128)S(1)} %all_to_all.10.recv, f32[2,8,128]{2,1,0:T(8,128)S(1)} %get-tuple-element.43.near_gens), custom_call_target="tpu_custom_call" | custom-call | flops 2000000 | bytes 1048576 | tf_op jit(solution)/shard_map/pallas_call | solution.py:811
  43.0 6.3 %all-to-all-done.1.feeds = f32[32,2,128]{2,1,0:T(2,128)S(1)} async-done(((f32[32,2,128]{2,1,0:T(2,128)}), f32[32,2,128]{2,1,0:T(2,128)S(1)}, u32[]{:S(2)}, u32[]{:S(2)}) %all-to-all-start.1) | async-done | bytes 32800 | tf_op jit(solution)/shard_map/all_to_all | solution.py:810
  49.3 2.5 %shard_map.102 = f32[4,16,128]{2,1,0:T(8,128)} custom-call(f32[32,16,128]{2,1,0:T(8,128)S(1)} %all_to_all.10.recv, f32[7,2,128,128]{3,2,1,0:T(8,128)S(1)} %shard_map.101.maps, f32[32,2,128]{2,1,0:T(2,128)S(1)} %all-to-all-done.1.feeds, f32[4,16,128]{2,1,0:T(8,128)S(1)} %get-tuple-element.47.driven, f32[9,16,128]{2,1,0:T(8,128)S(1)} %pad_maximum_fusion.fields, ...), custom_call_target="tpu_custom_call" | custom-call | flops 2000000 | bytes 1048576 | tf_op jit(solution)/shard_map/pallas_call | solution.py:812
  (1 shorter events, 0.0 us)
Async XLA Ops:
  1.5 5.4 %collective-permute-start = (f32[16,128]{1,0:T(8,128)S(1)}, f32[16,128]{1,0:T(8,128)S(1)}, u32[]{:S(2)}, u32[]{:S(2)}) collective-permute-start(f32[16,128]{1,0:T(8,128)S(1)} %get-tuple-element.26), channel_id=1, source_target_pairs={{0,1},{1,0},{2,3},{3,2},{4,5},{5,4},{6,7},{7,6},{8,9},{9,8},{10,11... | collective-permute-start | bytes 24584 | tf_op jit(solution)/shard_map/ppermute | solution.py:739
  4.6 2.3 %collective-permute-start.1 = (f32[16,128]{1,0:T(8,128)S(1)}, f32[16,128]{1,0:T(8,128)S(1)}, u32[]{:S(2)}, u32[]{:S(2)}) collective-permute-start(f32[16,128]{1,0:T(8,128)S(1)} %get-tuple-element.27), channel_id=1, source_target_pairs={{1,2},{2,1},{5,6},{6,5},{9,10},{10,9},{13,14},{14,13},{17,18},{18,... | collective-permute-start | bytes 24584 | tf_op jit(solution)/shard_map/ppermute | solution.py:738
  7.0 2.7 %collective-permute-start.2 = (f32[48,128]{1,0:T(8,128)S(1)}, f32[48,128]{1,0:T(8,128)S(1)}, u32[]{:S(2)}, u32[]{:S(2)}) collective-permute-start(f32[48,128]{1,0:T(8,128)S(1)} %get-tuple-element.36), channel_id=1, source_target_pairs={{0,4},{4,0},{8,12},{12,8},{16,20},{20,16},{24,28},{28,24},{1,5},{5... | collective-permute-start | bytes 73736 | tf_op jit(solution)/shard_map/ppermute | solution.py:739
  7.1 2.6 %collective-permute-start.3 = (f32[48,128]{1,0:T(8,128)S(1)}, f32[48,128]{1,0:T(8,128)S(1)}, u32[]{:S(2)}, u32[]{:S(2)}) collective-permute-start(f32[48,128]{1,0:T(8,128)S(1)} %get-tuple-element.37), channel_id=1, source_target_pairs={{4,8},{12,16},{20,24},{8,4},{16,12},{24,20},{5,9},{13,17},{21,25},... | collective-permute-start | bytes 73736 | tf_op jit(solution)/shard_map/ppermute | solution.py:738
  9.7 0.8 %copy-start = (f32[4,16,128]{2,1,0:T(8,128)S(1)}, f32[4,16,128]{2,1,0:T(8,128)}, u32[]{:S(2)}) copy-start(f32[4,16,128]{2,1,0:T(8,128)} %fed.3) | copy-start | bytes 98308
  38.2 11.1 %all-to-all-start.1 = ((f32[32,2,128]{2,1,0:T(2,128)}), f32[32,2,128]{2,1,0:T(2,128)S(1)}, u32[]{:S(2)}, u32[]{:S(2)}) async-start(f32[32,2,128]{2,1,0:T(2,128)} %get-tuple-element.46), calls=%async_computation.1 | async-start | bytes 65536 | tf_op jit(solution)/shard_map/all_to_all | solution.py:810

commit v2 on v1

--- a/solution.py
+++ b/solution.py
@@ -117,7 +117,7 @@
 GENS_AT = 40
 
 
-def columns_body(fields, send_a, send_b):
+def columns_body(fields, send_b, send_a):
     values = [fields[k] for k in range(N_FIELDS)]
     right = pack_columns(values, True)
     left = pack_columns(values, False)
@@ -126,7 +126,7 @@
     send_b[...] = jnp.where(even, left, right)
 
 
-def rows_body(fields, gens, recv_a, recv_b, send_a, send_b):
+def rows_body(fields, gens, recv_b, recv_a, send_b, send_a):
     d, c = place_of()
     even_c = (c & 1) == 0
     even_r = (d & 1) == 0
@@ -146,8 +146,10 @@
     send_b[GENS_AT:] = jnp.where(even_r, up, down)
 
 
-def tables_body(fields, tables, gens, left_mat, right_mat):
+def tables_body(n_r, fields, tables, gens, left_mat, right_mat):
     d, c = place_of()
+    turned = [d & 1, (n_r - 1 - d) & 1]
+    signs = [jnp.where(t == 1, -1.0, 1.0) for t in turned]
     rows = fields.shape[1]
     x0 = d * rows
     y0 = c * LANES
@@ -166,6 +168,7 @@
             c1, s1 = wave(angle * (1 - 2 * direction), x, 0, y, 0.24, h2)
             tables[2 * direction, i] = c1[SUB:]
             tables[2 * direction + 1, i] = s1[SUB:]
+            s1 = signs[direction] * s1
             for f in range(F):
                 zr = fields[2 * F + 1 + 2 * f, i : i + 1, :]
                 zi = fields[2 * F + 2 + 2 * f, i : i + 1, :]
@@ -184,10 +187,11 @@
                 p = both[base + half * SUB : base + (half + 1) * SUB]
                 q = both[base + (2 + half) * SUB : base + (3 + half) * SUB]
                 for part in range(2):
+                    sign = signs[direction]
                     if part == 0:
-                        g = p - roll(q, -2 * SUB)
+                        g = p - sign * roll(q, -2 * SUB)
                     else:
-                        g = roll(p, -2 * SUB) + q
+                        g = roll(p, -2 * SUB) + sign * q
                     g = jnp.where(lane < 2 * SUB, g, 0.0)
                     g = pltpu.roll(g, 0, 1, stride=2 * SUB, stride_axis=0)
                     row = jnp.sum(g, axis=0, keepdims=True)
@@ -195,7 +199,7 @@
                     gens[at : at + 1] = row
 
 
-def lists_body(lists, params, bits, weights, share):
+def lists_body(lists, bits):
     count = lists[LMAX]
     low = jnp.zeros(count.shape, jnp.int32)
     high = jnp.zeros(count.shape, jnp.int32)
@@ -210,6 +214,9 @@
         high = high | jnp.where(live & (code >= half), bit, 0)
     bits[0] = low
     bits[1] = high
+
+
+def params_body(params, weights, share, columns):
     spot = iota((Q, LANES), 0)
     spot = 2 * SUB * (spot // SUB) + (spot & (SUB - 1))
     values = params[...]
@@ -225,6 +232,9 @@
     ]
     weights[...] = placed[0][: 2 * F] + placed[1][: 2 * F]
     share[...] = placed[0][2 * F : 2 * F + 1] + placed[1][2 * F + 1 : 2 * F + 2]
+    for k in range(2 * F):
+        for a1, column in enumerate(to_columns(wide(placed[0][k : k + 1]))[::2]):
+            columns[k, SUB * a1 : SUB * (a1 + 1)] = wide(column)
 
 
 def project(left_mat, right_mat, tables, first, cs, rows, f_out):
@@ -263,44 +273,49 @@
     return x, y
 
 
-def near_body(
-    n_r, n_c, fields, fed, bits, share, cols_a, cols_b, rows_a, rows_b, gens, tables,
-    payload, green, source, ext, near_gens, inner, edge_l, edge_r, moved, cs, left_mat, right_mat, common, halo,
-):
+def halo_rows(rows_a, rows_b):
+    even = (lax.axis_index("rng") & 1) == 0
+    return jnp.where(even, rows_b[...], rows_a[...]), jnp.where(even, rows_a[...], rows_b[...])
+
+
+def with_halo(ks, fields, cols_a, cols_b, above, below, inner, edge_l, edge_r):
     rows = fields.shape[1]
-    d, c = place_of()
-    even_c = (c & 1) == 0
-    even_r = (d & 1) == 0
-    below = jnp.where(even_r, rows_a[...], rows_b[...])
-    above = jnp.where(even_r, rows_b[...], rows_a[...])
-    near_gens[0] = above[GENS_AT:]
-    near_gens[1] = below[GENS_AT:]
+    even = (lax.axis_index("xr") & 1) == 0
     edge_l[...] = jnp.zeros(edge_l.shape, f32)
     edge_r[...] = jnp.zeros(edge_r.shape, f32)
-    edge_l[TOP : TOP + rows] = jnp.where(even_c, cols_b[...], cols_a[...])
-    edge_r[TOP : TOP + rows] = jnp.where(even_c, cols_a[...], cols_b[...])
+    edge_l[TOP : TOP + rows] = jnp.where(even, cols_b[...], cols_a[...])
+    edge_r[TOP : TOP + rows] = jnp.where(even, cols_a[...], cols_b[...])
     at = H * N_FIELDS
     edge_l[TOP - H : TOP] = above[at : at + H]
     edge_l[TOP + rows : TOP + rows + H] = below[at : at + H]
     edge_r[TOP - H : TOP] = above[at + H : at + 2 * H]
     edge_r[TOP + rows : TOP + rows + H] = below[at + H : at + 2 * H]
     from_left, from_right = edge_l[...], edge_r[...]
-    for k in range(N_FIELDS):
-        inner[k] = jnp.zeros(inner.shape[1:], f32)
-        inner[k, TOP : TOP + rows] = fields[k]
-        inner[k, TOP - H : TOP] = above[H * k : H * (k + 1)]
-        inner[k, TOP + rows : TOP + rows + H] = below[H * k : H * (k + 1)]
-        side = unpack_columns(from_left, from_right, k)
-        if k >= 2 * F:
-            ext[2 * (k - 2 * F)] = inner[k]
-            ext[2 * (k - 2 * F) + 1] = side
-        if k <= 2 * F:
-            middle = inner[k]
-            for dy in range(-H, H + 1):
-                moved[k * (2 * H + 1) + dy + H] = shifted(middle, side, dy)
+    sides = []
+    for i, k in enumerate(ks):
+        inner[i] = jnp.zeros(inner.shape[1:], f32)
+        inner[i, TOP : TOP + rows] = fields[k]
+        inner[i, TOP - H : TOP] = above[H * k : H * (k + 1)]
+        inner[i, TOP + rows : TOP + rows + H] = below[H * k : H * (k + 1)]
+        sides.append(unpack_columns(from_left, from_right, k))
+    return sides
+
+
+def near_body(
+    n_r, n_c, fields, bits, share, cols_b, cols_a, rows_b, rows_a, gens, tables,
+    payload, green, source, inner, edge_l, edge_r, moved, cs, left_mat, right_mat, common, halo,
+):
+    rows = fields.shape[1]
+    d, c = place_of()
+    above, below = halo_rows(rows_a, rows_b)
+    sides = with_halo(range(2 * F + 1), fields, cols_a, cols_b, above, below, inner, edge_l, edge_r)
+    for k, side in enumerate(sides):
+        middle = inner[k]
+        for dy in range(-H, H + 1):
+            moved[k * (2 * H + 1) + dy + H] = shifted(middle, side, dy)
     h = fields[2 * F]
     inverse = [fields[2 * F + 1 + k] for k in range(2 * F)]
-    incident = [fed[k] for k in range(2 * F)]
+    incident = [fields[N_FIELDS + k] for k in range(2 * F)]
     low, high = bits[0], bits[1]
     half = OFFSETS // 2
     near = [jnp.zeros((rows, LANES), f32) for _ in range(2 * F)]
@@ -405,78 +420,140 @@
             send(dr, dc, corner_to(dr, dc))
 
 
-def toeplitz(gens, sub, lane):
-    wide = [jnp.broadcast_to(gens[k : k + 1], (SUB, LANES)) for k in range(4)]
+def toeplitz(gens, late):
+    lane = iota((SUB, LANES), 1)
     low = (lane & SUB) == 0
-
-    def tile(part, by):
-        inside = (lane >= by + sub) & (lane < by + sub + LANES)
-        one = pltpu.roll(wide[2 * part], by % LANES, 1, stride=1, stride_axis=0)
-        two = pltpu.roll(wide[2 * part + 1], by % LANES, 1, stride=1, stride_axis=0)
-        return jnp.where(inside, one, two)
-
+    slid = [slide(wide(gens[k : k + 1])) for k in range(4)]
+    re, im = slid[0:2], slid[2:4]
+    bases = [
+        [jnp.where(low, re[half], -roll(im[half], SUB)) for half in range(2)],
+        [jnp.where(low, im[half], roll(re[half], SUB)) for half in range(2)],
+    ]
     out = []
     for a1 in range(Q // SUB):
-        by = 2 * SUB * a1 - SUB
-        out.append(jnp.where(low, tile(0, by), -tile(1, by + SUB)))
-    for a1 in range(Q // SUB):
-        by = 2 * SUB * a1 - SUB
-        out.append(jnp.where(low, tile(1, by), tile(0, by + SUB)))
+        for first, second in bases:
+            tile = jnp.where(lane < LANES - 2 * SUB * a1, first, second)
+            out.append(tile if late else roll(tile, 2 * SUB * a1))
     return out
 
 
-def to_columns(row, sub, lane):
-    return [
-        jnp.sum(jnp.where(lane == 2 * SUB * a1 + SUB * part + sub, row, 0.0), axis=1, keepdims=True)
-        for part in range(2)
-        for a1 in range(Q // SUB)
-    ]
-
-
-def to_row(columns, sub, lane):
-    total = jnp.zeros((SUB, LANES), f32)
-    for k, column in enumerate(columns):
-        part, a1 = k // (Q // SUB), k % (Q // SUB)
-        total = jnp.where(lane == 2 * SUB * a1 + SUB * part + sub, column, total)
-    return jnp.broadcast_to(jnp.sum(total, axis=0, keepdims=True), (SUB, LANES))
+def slide(row):
+    return pltpu.roll(row, LANES - SUB, 1, stride=1, stride_axis=0)
+
+
+TILES = 2 * Q // SUB
+
+
+def diagonal(k):
+    return iota((SUB, LANES), 1) == SUB * k + iota((SUB, LANES), 0)
+
+
+def to_columns(row):
+    return [jnp.sum(jnp.where(diagonal(k), row, 0.0), axis=1, keepdims=True) for k in range(TILES)]
 
 
 def wide(row):
     return jnp.broadcast_to(row, (SUB, LANES))
 
 
-def packed_times(wr, wi, row, low):
+def tree_sum(parts):
+    while len(parts) > 1:
+        parts = [sum(parts[i : i + 2]) for i in range(0, len(parts), 2)]
+    return parts[0]
+
+
+def packed_times(wr, wi, row):
+    low = (iota((SUB, LANES), 1) & SUB) == 0
     turned = jnp.where(low, -roll(row, -SUB), roll(row, SUB))
     return wr * row + wi * turned
 
 
-def sweep_step(maps, feeds, shares, weights, carry, spread):
-    sub = iota((SUB, LANES), 0)
-    lane = iota((SUB, LANES), 1)
-    low = (lane & SUB) == 0
+def column_times(weights, columns, f):
+    out = []
+    for a1 in range(Q // SUB):
+        at = slice(SUB * a1, SUB * (a1 + 1))
+        out += times((weights[2 * f, at], weights[2 * f + 1, at]), (columns[2 * a1], columns[2 * a1 + 1]))
+    return out
+
+
+def shares_of(row):
+    low = (iota((SUB, LANES), 1) & SUB) == 0
+    row = wide(row)
+    return jnp.where(low, row, roll(row, SUB)), jnp.where(low, roll(row, -SUB), row)
+
+
+def row_step(maps, feeds, shares, weights, carry, spread, put, late):
     out = []
     for f in range(F):
-        amp = packed_times(weights[2 * f], weights[2 * f + 1], carry[f], low)
-        columns = [jnp.sum(maps(f, k) * amp, axis=1, keepdims=True) for k in range(2 * Q // SUB)]
-        out.append(shares[f] * (carry[f] + feeds[f] - spread * to_row(columns, sub, lane)))
+        full = feeds[f] if carry is None else carry[f] + feeds[f]
+        full = [jnp.where(diagonal(k), full, 0.0) for k in range(TILES)]
+        if carry is None:
+            put(f, [jnp.zeros((SUB, LANES), f32)] * TILES)
+        else:
+            amp = spread * packed_times(weights[2 * f], weights[2 * f + 1], carry[f])
+            put(f, to_columns(amp))
+            turns = [roll(amp, -2 * SUB * a1) if late else amp for a1 in range(Q // SUB)]
+            full = [part - tile * turns[k // 2] for k, (part, tile) in enumerate(zip(full, maps(f), strict=True))]
+        share = [jnp.sum(jnp.where(diagonal(k), shares[f], 0.0), axis=1, keepdims=True) for k in range(0, TILES, 2)]
+        out.append([share[k // 2] * jnp.sum(full[k], axis=1, keepdims=True) for k in range(TILES)])
     return out
 
 
-def shares_of(row):
-    lane = iota((SUB, LANES), 1)
-    low = (lane & SUB) == 0
-    row = wide(row)
-    return jnp.where(low, row, roll(row, SUB)), jnp.where(low, roll(row, -SUB), row)
-
-
-def put_amplitudes(put, weights, carry, spread):
-    sub = iota((SUB, LANES), 0)
-    lane = iota((SUB, LANES), 1)
-    low = (lane & SUB) == 0
+def column_step(maps, feeds, shares, columns, carry, spread, put, late):
+    out = []
     for f in range(F):
-        amp = spread * packed_times(weights[2 * f], weights[2 * f + 1], carry[f], low)
-        for k, column in enumerate(to_columns(amp, sub, lane)):
-            put(f, slice(SUB * k, SUB * (k + 1)), jnp.broadcast_to(column, (SUB, LANES)))
+        amp = [spread * part for part in column_times(columns, carry[f], f)]
+        put(f, amp)
+        tiles = maps(f)
+        pairs = [tiles[k] * amp[k] + tiles[k + 1] * amp[k + 1] for k in range(0, TILES, 2)]
+        parts = [roll(pair, 2 * SUB * a1) if late else pair for a1, pair in enumerate(pairs)]
+        kept = [jnp.where(diagonal(k), carry[f][k], 0.0) for k in range(TILES)]
+        total = wide(jnp.sum(tree_sum(kept) - tree_sum(parts), axis=0, keepdims=True))
+        out.append(shares[f] * (total + feeds[f]))
+    return out
+
+
+def sweep(n_r, maps, feeds, share, weights, columns, spread, put, late):
+    rows = [wide(weights[k : k + 1]) for k in range(2 * F)]
+
+    def pair(j, carry):
+        between = row_step(
+            lambda f: maps(j, f), feeds(j), shares_of(share(j)), rows, carry, spread, lambda f, v: put(j, f, v),
+            late,
+        )
+        return column_step(
+            lambda f: maps(j + 1, f), feeds(j + 1), shares_of(share(j + 1)), columns, between, spread,
+            lambda f, v: put(j + 1, f, v), late,
+        )
+
+    carry = None
+    pairs = (n_r - 1) // 2
+    if pairs > 0:
+        carry = pair(0, carry)
+    if n_r <= SUB:
+        for i in range(1, pairs):
+            carry = pair(2 * i, carry)
+    else:
+        carry = lax.fori_loop(1, pairs, lambda i, now: tuple(pair(2 * i, now)), tuple(carry))
+    if (n_r - 1) % 2:
+        j = n_r - 2
+        last = row_step(
+            lambda f: maps(j, f), feeds(j), shares_of(share(j)), rows, carry, spread, lambda f, v: put(j, f, v),
+            late,
+        )
+        for f in range(F):
+            put(n_r - 1, f, [spread * part for part in column_times(columns, last[f], f)])
+    elif carry is not None:
+        for f in range(F):
+            put(n_r - 1, f, to_columns(spread * packed_times(rows[2 * f], rows[2 * f + 1], carry[f])))
+
+
+def putter(amps):
+    def put(j, f, columns):
+        for k, column in enumerate(columns):
+            amps[j, f, SUB * k : SUB * (k + 1)] = jnp.broadcast_to(column, (SUB, LANES))
+
+    return put
 
 
 def laps(n, body):
@@ -496,14 +573,6 @@
     return total
 
 
-def store_maps(maps, j, gens):
-    sub = iota((SUB, LANES), 0)
-    lane = iota((SUB, LANES), 1)
-    for f in range(F):
-        for k, tile in enumerate(toeplitz(gens[4 * f : 4 * f + 4], sub, lane)):
-            maps[j, f, SUB * k : SUB * (k + 1)] = tile
-
-
 def powers(base, count):
     out = [None, base]
     for _ in range(2, count):
@@ -511,80 +580,116 @@
     return out
 
 
-def wave_powers(direction, x, y, heights):
-    u1 = powers(wave(1 - 2 * direction, x, 0, y, 0.24, heights), Q // SUB)
-    u2 = powers(wave(0, x, 1, y, 0.03, heights), SUB)
-    return u1, u2
-
-
-def radiated(f, splat, u1, u2, carried):
+MERGED = 5
+
+
+def merged(middle, side):
+    sub = iota((SUB, LANES), 0)
+    return [
+        jnp.where(sub < H, roll(side[0:SUB], H, 0), middle[0:SUB]),
+        middle[SUB : 2 * SUB],
+        middle[2 * SUB : 3 * SUB],
+        jnp.where(sub >= SUB - H, roll(side[3 * SUB :], -H, 0), middle[3 * SUB :]),
+        side[SUB : 2 * SUB] + roll(side[2 * SUB : 3 * SUB], LANES // 2),
+    ]
+
+
+def apart(tiles):
+    return [roll(tiles[0], -H, 0), tiles[4], roll(tiles[4], LANES // 2), roll(tiles[3], H, 0)]
+
+
+def merged_places(rows):
+    d, c = place_of()
+    sub = iota((SUB, LANES), 0)
+    lane = iota((SUB, LANES), 1)
+    x0 = d * rows + sub
+    y0 = c * LANES + lane
+    side = y0 + jnp.where(lane < LANES // 2, LANES, -LANES)
+    turned = (lane + LANES // 2) & (LANES - 1)
+    side_turned = c * LANES + turned + jnp.where(turned < LANES // 2, LANES, -LANES)
+    second = (lane >= LANES // 4) & (lane < 3 * LANES // 4)
+    return [
+        (jnp.where(sub < H, x0 - H, x0 - SUB), jnp.where(sub < H, side, y0)),
+        (x0, y0),
+        (x0 + SUB, y0),
+        (jnp.where(sub >= SUB - H, x0 + rows - (SUB - H), x0 + rows), jnp.where(sub >= SUB - H, side, y0)),
+        (jnp.where(second, x0 + SUB, x0), jnp.where(second, side_turned, side)),
+    ]
+
+
+def store_waves(
+    fields, cols_a, cols_b, above, below, loss, first, second, carriers, back_first, back_carriers, inner, edge_l, edge_r
+):
+    rows = fields.shape[1]
+    ks = range(2 * F, N_FIELDS)
+    sides = with_halo(ks, fields, cols_a, cols_b, above, below, inner, edge_l, edge_r)
+    tiles = [merged(inner[i], side) for i, side in enumerate(sides)]
+    for k in range(2 * F):
+        for t in range(MERGED):
+            loss[t, k] = tiles[1 + k][t]
+
+    def keep(out, t, values):
+        for k, value in enumerate(values):
+            for part in range(2):
+                out[t, k, part] = value[part]
+
+    for t, (x, y) in enumerate(merged_places(rows)):
+        h = tiles[0][t]
+        keep(first, t, powers(wave(1, x, 0, y, 0.24, h), Q // SUB)[1:])
+        keep(second, t, powers(wave(0, x, 1, y, 0.03, h), SUB)[1:])
+        keep(carriers, t, [carrier(f, 0, x, y, h) for f in range(F)])
+        if t in (1, 2):
+            keep(back_first, t - 1, powers(wave(-1, x, 0, y, 0.24, h), Q // SUB)[1:])
+            keep(back_carriers, t - 1, [carrier(f, 1, x, y, h) for f in range(F)])
+
+
+def radiated(amps, at, f, first, second, carriers, t, t_second):
+    splat = lambda a: wide(amps[at, f, a : a + 1])
     total = None
     for a1 in range(Q // SUB):
-        ar, ai = splat(f, SUB * a1), splat(f, Q + SUB * a1)
-        inner = (ar, ai)
+        base = 2 * SUB * a1
+        inner = (splat(base), splat(base + SUB))
         for a2 in range(1, SUB):
-            got = times((splat(f, SUB * a1 + a2), splat(f, Q + SUB * a1 + a2)), u2[a2])
+            u2 = (second[t_second, a2 - 1, 0], second[t_second, a2 - 1, 1])
+            got = times((splat(base + a2), splat(base + SUB + a2)), u2)
             inner = (inner[0] + got[0], inner[1] + got[1])
         if a1 == 0:
             total = inner
         else:
-            got = times(u1[a1], inner)
+            got = times((first[t, a1 - 1, 0], first[t, a1 - 1, 1]), inner)
             total = (total[0] + got[0], total[1] + got[1])
-    return times(carried, total)
-
-
-def back_body(n_r, n_c, recv, near_gens, maps):
-    d, c = place_of()
-    below = near_gens[1]
-
-    def body(j):
-        store_maps(maps, j, gens_sum(recv, j + 1, n_c, d, c, 1, below))
-
-    laps(n_r - 1, body)
+    return times((carriers[t, f, 0], carriers[t, f, 1]), total)
 
 
 def new_body(
-    n_r, n_c, spread, recv, green, source, ext, fields, fed, near_gens, tables, weights,
-    forward, driven, payload, maps, feeds, carries, amps, inner, moved, edge_l, edge_r, cs, left_mat, right_mat, common, halo,
+    n_r, n_c, spread, recv, green, source, fields, cols_b, cols_a, rows_b, rows_a, tables, weights, columns,
+    forward, driven, payload, second, back_first, back_carriers, below_gens,
+    loss, first, carriers, amps, held, inner, moved, edge_l, edge_r, cs, left_mat, right_mat, common, halo,
 ):
     rows = fields.shape[1]
     d, c = place_of()
-    wts = [wide(weights[k : k + 1]) for k in range(2 * F)]
-    zero = jnp.zeros((SUB, LANES), f32)
-    above = near_gens[0]
-
-    def prepare(j):
-        store_maps(maps, j, gens_sum(recv, j, n_c, d, c, -1, above))
+    above_rows, below_rows = halo_rows(rows_a, rows_b)
+    above = above_rows[GENS_AT:]
+    below_gens[...] = below_rows[GENS_AT:]
+    store_waves(
+        fields, cols_a, cols_b, above_rows, below_rows,
+        loss, first, second, carriers, back_first, back_carriers, held, edge_l, edge_r,
+    )
+
+    if n_r <= SUB:
+        sums = [gens_sum(recv, j, n_c, d, c, -1, above) for j in range(n_r - 1)]
+
+    def maps(j, f):
+        gens = sums[j] if n_r <= SUB else gens_sum(recv, j, n_c, d, c, -1, above)
+        return toeplitz(gens[4 * f : 4 * f + 4], False)
+
+    def feeds(j):
         feed = recv[j * n_c, SUB : 2 * SUB]
         for k in range(1, n_c):
             feed = feed + recv[j * n_c + k, SUB : 2 * SUB]
-        feeds[j] = feed
-
-    laps(n_r - 1, prepare)
-    for f in range(F):
-        carries[0, f] = zero
-
-    def lap(j, carry):
-        new = sweep_step(
-            lambda f, k: maps[j, f, SUB * k : SUB * (k + 1)],
-            [wide(feeds[j, f : f + 1]) for f in range(F)],
-            shares_of(recv[j * n_c, SUB + 2 : SUB + 3]),
-            wts,
-            carry,
-            spread,
-        )
-        for f in range(F):
-            carries[j + 1, f] = new[f]
-        return tuple(new)
-
-    lax.fori_loop(0, jnp.minimum(d + 1, n_r - 1), lap, (zero,) * F)
-    for which in range(3):
-        at = jnp.clip(d + which - 1, 0, n_r - 1)
-
-        def put(f, at_rows, tile, which=which):
-            amps[which, f, at_rows] = tile
-
-        put_amplitudes(put, wts, [carries[at, f] for f in range(F)], spread)
+        return [wide(feed[f : f + 1]) for f in range(F)]
+
+    sweep(n_r, maps, feeds, lambda j: recv[j * n_c, SUB + 2 : SUB + 3], weights, columns, spread, putter(amps), False)
 
     at = HALO_AT
 
@@ -614,34 +719,19 @@
     sides = [unpack_columns(from_left, from_right, k) for k in range(2 * F)]
 
     weak = {}
-    tiles = (rows + 2 * SUB) // SUB
-    for tile in range(tiles):
-        which = 0 if tile == 0 else 2 if tile == tiles - 1 else 1
-        splat = lambda f, a, which=which: amps[which, f, a : a + 1]
-        rows_at = slice(SUB * tile, SUB * (tile + 1))
-        for side in range(2):
-            x, y = place_ids(SUB, LANES, SUB * tile - TOP, 0, rows)
-            if side == 1:
-                lane = iota((SUB, LANES), 1)
-                y = y + jnp.where(lane < LANES // 2, LANES, -LANES)
-            h = ext[side, rows_at]
-            u1, u2 = wave_powers(0, x, y, h)
-            for f in range(F):
-                w = radiated(f, splat, u1, u2, carrier(f, 0, x, y, h))
-                z = (ext[2 * (1 + 2 * f) + side, rows_at], ext[2 * (2 + 2 * f) + side, rows_at])
-                lost = times(z, w)
-                for part in range(2):
-                    k = 2 * f + part
-                    if side == 0:
-                        inner[k, rows_at] = inner[k, rows_at] - lost[part]
-                        weak[tile, k] = w[part]
-                    else:
-                        sides[k] = (sides[k] if isinstance(sides[k], list) else [sides[k]]) + [
-                            sides_tile(sides[k], rows_at) - lost[part]
-                        ]
+    lost = {}
+    for t, step in enumerate((-1, 0, 0, 1, 0)):
+        at = jnp.clip(d + step, 0, n_r - 1)
+        for f in range(F):
+            w = radiated(amps, at, f, first, second, carriers, t, t)
+            got = times((loss[t, 2 * f], loss[t, 2 * f + 1]), w)
+            for part in range(2):
+                weak[t, 2 * f + part] = w[part]
+                lost[t, 2 * f + part] = got[part]
     for k in range(2 * F):
-        side = jnp.concatenate(sides[k][1:], axis=0)
-        middle = inner[k]
+        tiles = [lost[t, k] for t in range(MERGED)]
+        side = sides[k] - jnp.concatenate(apart(tiles), axis=0)
+        middle = inner[k] - jnp.concatenate(tiles[:4], axis=0)
         forward[k] = middle[TOP : TOP + rows]
         for dy in range(-H, H + 1):
             moved[k * (2 * H + 1) + dy + H] = shifted(middle, side, dy)
@@ -654,18 +744,17 @@
             add = times(g, (window(2 * f), window(2 * f + 1)))
             near[2 * f] += add[0]
             near[2 * f + 1] += add[1]
-    x, y = place_ids(rows, LANES, 0, 0, rows)
-    h = fields[2 * F]
     for f in range(F):
         rest = []
         for part in range(2):
             k = 2 * f + part
-            w = jnp.concatenate([weak[tile, k] for tile in range(1, tiles - 1)], axis=0)
-            rest.append(fed[k] - near[k] - w)
+            w = jnp.concatenate([weak[1, k], weak[2, k]], axis=0)
+            rest.append(fields[N_FIELDS + k] - near[k] - w)
         s = times((fields[2 * F + 1 + 2 * f], fields[2 * F + 2 + 2 * f]), rest)
         driven[2 * f] = s[0]
         driven[2 * f + 1] = s[1]
-        add = conj_times(carrier(f, 1, x, y, h), s)
+        base = [jnp.concatenate([back_carriers[t, f, part] for t in range(2)], axis=0) for part in range(2)]
+        add = conj_times(base, s)
         cs[2 * f] = add[0]
         cs[2 * f + 1] = add[1]
 
@@ -683,45 +772,34 @@
     lax.fori_loop(0, n_r * n_c, fill, 0)
 
 
-def sides_tile(side, rows_at):
-    return side[0][rows_at] if isinstance(side, list) else side[rows_at]
-
-
-def last_body(n_r, n_c, spread, recv, maps, feeds, driven, fields, weights, currents, amps):
+def last_body(
+    n_r, n_c, spread, recv, fed, new, driven, fields, weights, columns, first, second, carriers, below_gens,
+    forward, currents, amps,
+):
     rows = fields.shape[1]
-    d, _ = place_of()
-    wts = [wide(weights[k : k + 1]) for k in range(2 * F)]
-    zero = jnp.zeros((SUB, LANES), f32)
-
-    def lap(k, carry):
+    d, c = place_of()
+    forward[...] = new[...]
+    below = below_gens[...]
+
+    def feeds(k):
         j = n_r - 1 - k
-        feed = feeds[j * n_c]
+        feed = fed[j * n_c]
         for i in range(1, n_c):
-            feed = feed + feeds[j * n_c + i]
-        new = sweep_step(
-            lambda f, k: maps[j - 1, f, SUB * k : SUB * (k + 1)],
-            [wide(feed[f : f + 1]) for f in range(F)],
-            shares_of(recv[j * n_c, SUB + 2 : SUB + 3]),
-            wts,
-            carry,
-            spread,
-        )
-        return tuple(new)
-
-    carry = lax.fori_loop(0, n_r - 1 - d, lap, (zero,) * F)
-
-    def put(f, at_rows, tile):
-        amps[f, at_rows] = tile
-
-    put_amplitudes(put, wts, carry, spread)
-    splat = lambda f, a: amps[f, a : a + 1]
+            feed = feed + fed[j * n_c + i]
+        return [wide(feed[f : f + 1]) for f in range(F)]
+
+    def share(k):
+        return recv[(n_r - 1 - k) * n_c, SUB + 2 : SUB + 3]
+
+    def maps(k, f):
+        return toeplitz(gens_sum(recv, n_r - 1 - k, n_c, d, c, 1, below)[4 * f : 4 * f + 4], True)
+
+    sweep(n_r, maps, feeds, share, weights, columns, spread, putter(amps), True)
+    at = n_r - 1 - d
     for tile in range(rows // SUB):
         rows_at = slice(SUB * tile, SUB * (tile + 1))
-        x, y = place_ids(SUB, LANES, SUB * tile, 0, rows)
-        h = fields[2 * F, rows_at]
-        u1, u2 = wave_powers(1, x, y, h)
         for f in range(F):
-            w = radiated(f, splat, u1, u2, carrier(f, 1, x, y, h))
+            w = radiated(amps, at, f, first, second, carriers, tile, tile + 1)
             lost = times((fields[2 * F + 1 + 2 * f, rows_at], fields[2 * F + 2 + 2 * f, rows_at]), w)
             currents[2 * f, rows_at] = driven[2 * f, rows_at] - lost[0]
             currents[2 * f + 1, rows_at] = driven[2 * f + 1, rows_at] - lost[1]
@@ -745,39 +823,34 @@
     spread = 1.0 / math.sqrt(rows * cols * n_c)
     slots = n_r * n_c
     tall = rows + 2 * SUB
-    fields = jnp.concatenate([previous, heights[None], inverse_diag])
-    cols_a, cols_b = call(columns_body, [(rows, LANES)] * 2, [VMEM], flops=500_000)(fields)
+    fields = jnp.concatenate([previous, heights[None], inverse_diag, incident])
+    cols_b, cols_a = call(columns_body, [(rows, LANES)] * 2, [VMEM], flops=500_000)(fields)
+    cols_a, cols_b, transmit, angle_weights = lax.optimization_barrier((cols_a, cols_b, transmit, angle_weights))
     cols_a, cols_b = swap("xr", n_c, cols_a, cols_b)
     tables, gens = call(
-        tables_body,
+        functools.partial(tables_body, n_r),
         [(6, rows, SUB, LANES), (2 * SUB, LANES)],
         [VMEM],
         [pltpu.VMEM((16 * SUB, patches), f32), pltpu.VMEM((16 * SUB, patches), f32)],
     )(fields)
-    rows_a, rows_b = call(rows_body, [(ROWS_SENT, LANES)] * 2, [VMEM] * 4, flops=500_000)(fields, gens, cols_a, cols_b)
-    rows_a, rows_b, neighbours, counts, transmit, angle_weights = lax.optimization_barrier(
-        (rows_a, rows_b, neighbours, counts, transmit, angle_weights)
-    )
+    params = jnp.concatenate([angle_weights.reshape(2 * F, Q), transmit.reshape(F, Q)])
+    weights, share, columns = call(
+        params_body, [(2 * F, LANES), (1, LANES), (2 * F, Q, LANES)], [VMEM], flops=500_000
+    )(params)
+    gens, weights, share, columns = lax.optimization_barrier((gens, weights, share, columns))
+    rows_b, rows_a = call(rows_body, [(ROWS_SENT, LANES)] * 2, [VMEM] * 4, flops=500_000)(fields, gens, cols_b, cols_a)
+    rows_a, rows_b, neighbours, counts = lax.optimization_barrier((rows_a, rows_b, neighbours, counts))
     rows_a, rows_b = swap("rng", n_r, rows_a, rows_b)
     lists = jnp.concatenate([neighbours, counts[None]])
-    params = jnp.concatenate([angle_weights.reshape(2 * F, Q), transmit.reshape(F, Q)])
-    bits, weights, share = call(
-        lists_body, [jax.ShapeDtypeStruct((2, rows, LANES), jnp.int32), (2 * F, LANES), (1, LANES)], [VMEM] * 2
-    )(lists, params)
-    payload, green, source, ext, near_gens = call(
+    (bits,) = call(lists_body, [jax.ShapeDtypeStruct((2, rows, LANES), jnp.int32)], [VMEM], flops=500_000)(lists)
+    edges = [pltpu.VMEM((tall, LANES), f32)] * 2
+    payload, green, source = call(
         functools.partial(near_body, n_r, n_c),
+        [(slots, SLOT, LANES), (4 * OFFSETS, rows, LANES), (2 * F, rows, LANES)],
+        [VMEM] * 9,
         [
-            (slots, SLOT, LANES),
-            (4 * OFFSETS, rows, LANES),
-            (2 * F, rows, LANES),
-            (4 * F + 2, tall, LANES),
-            (2, SUB, LANES),
-        ],
-        [VMEM] * 10,
-        [
-            pltpu.VMEM((N_FIELDS, tall, LANES), f32),
-            pltpu.VMEM((tall, LANES), f32),
-            pltpu.VMEM((tall, LANES), f32),
+            pltpu.VMEM((2 * F + 1, tall, LANES), f32),
+            *edges,
             pltpu.VMEM(((2 * F + 1) * (2 * H + 1), tall, LANES), f32),
             pltpu.VMEM((2 * F, rows, LANES), f32),
             pltpu.VMEM((4 * SUB, patches), f32),
@@ -785,37 +858,44 @@
             pltpu.VMEM((3 * SUB, LANES), f32),
             pltpu.VMEM((2 * SUB, LANES), f32),
         ],
-    )(fields, incident, bits, share, cols_a, cols_b, rows_a, rows_b, gens, tables)
+    )(fields, bits, share, cols_b, cols_a, rows_b, rows_a, gens, tables)
     recv = lax.all_to_all(payload, BOTH, 0, 0)
-    forward, driven, payload = call(
+    tile = (2, SUB, LANES)
+    new, driven, payload, second, back_first, back_carriers, below_gens = call(
         functools.partial(new_body, n_r, n_c, spread),
-        [(2 * F, rows, LANES), (2 * F, rows, LANES), (slots, 2, LANES)],
-        [VMEM] * 9,
         [
-            pltpu.VMEM((n_r - 1, F, 2 * Q, LANES), f32),
-            pltpu.VMEM((n_r - 1, SUB, LANES), f32),
-            pltpu.VMEM((n_r, F, SUB, LANES), f32),
-            pltpu.VMEM((3, F, 2 * Q, LANES), f32),
+            (2 * F, rows, LANES),
+            (2 * F, rows, LANES),
+            (slots, 2, LANES),
+            (MERGED, SUB - 1, *tile),
+            (2, Q // SUB - 1, *tile),
+            (2, F, *tile),
+            (SUB, LANES),
+        ],
+        [VMEM] * 11,
+        [
+            pltpu.VMEM((MERGED, 2 * F, SUB, LANES), f32),
+            pltpu.VMEM((MERGED, Q // SUB - 1, *tile), f32),
+            pltpu.VMEM((MERGED, F, *tile), f32),
+            pltpu.VMEM((n_r, F, 2 * Q, LANES), f32),
+            pltpu.VMEM((2 * F + 1, tall, LANES), f32),
             pltpu.VMEM((2 * F, tall, LANES), f32),
             pltpu.VMEM((2 * F * (2 * H + 1), tall, LANES), f32),
-            pltpu.VMEM((tall, LANES), f32),
-            pltpu.VMEM((tall, LANES), f32),
+            *edges,
             pltpu.VMEM((2 * F, rows, LANES), f32),
             pltpu.VMEM((4 * SUB, patches), f32),
             pltpu.VMEM((16 * SUB, patches), f32),
             pltpu.VMEM((SUB, LANES), f32),
             pltpu.VMEM((2, 2 * SUB, LANES), f32),
         ],
-    )(recv, green, source, ext, fields, incident, near_gens, tables, weights)
-    feeds = lax.all_to_all(payload, BOTH, 0, 0)
-    (maps,) = call(functools.partial(back_body, n_r, n_c), [(n_r - 1, F, 2 * Q, LANES)], [VMEM] * 2)(recv, near_gens)
-    (currents,) = call(
+    )(recv, green, source, fields, cols_b, cols_a, rows_b, rows_a, tables, weights, columns)
+    fed = lax.all_to_all(payload, BOTH, 0, 0)
+    return call(
         functools.partial(last_body, n_r, n_c, spread),
-        [(2 * F, rows, LANES)],
-        [VMEM] * 6,
-        [pltpu.VMEM((F, 2 * Q, LANES), f32)],
-    )(recv, maps, feeds, driven, fields, weights)
-    return forward, currents
+        [(2 * F, rows, LANES), (2 * F, rows, LANES)],
+        [VMEM] * 11,
+        [pltpu.VMEM((n_r, F, 2 * Q, LANES), f32)],
+    )(recv, fed, new, driven, fields, weights, columns, back_first, second, back_carriers, below_gens)
 
 
 def solution(mesh):

time: 52.1 us -> 48.3 us (0.927)
  waiting for transfers between devices: 6.27 us -> 0.01 us
  blocking collectives: 20.6 us -> 23.9 us
  Pallas kernels: 12.7 us -> 10.7 us
  starting transfers between devices: 8.22 us -> 10.2 us
  local copies, waits for them, and re-layouts: 0.76 us -> 0 us
    all_to_all x0 -> x1, blocking collectives: none -> 9.82 us  [per_device(): fed = lax.all_to_all(payload, BOTH, 0, 0)]
    all_to_all x1, blocking collectives: 20.6 us -> 14.1 us  [per_device(): recv = lax.all_to_all(payload, BOTH, 0, 0)]
    all_to_all x1 -> x0, waiting for transfers between devices: 6.26 us -> none  [per_device(): feeds = lax.all_to_all(payload, BOTH, 0, 0)]
    ppermute x2, starting transfers between devices: 3.16 us -> 8.83 us  [swap(): return (lax.ppermute(a, axis, first), b)]
    all_to_all x1 -> x0, starting transfers between devices: 3.75 us -> none  [per_device(): feeds = lax.all_to_all(payload, BOTH, 0, 0)]
    pallas_call x1, Pallas kernels: 4.58 us -> 3.53 us  [per_device(): call(functools.partial(new_body, n_r, n_c, spread), [(2 * F, rows, LANES)...]
    pallas_call x3, Pallas kernels: 2.94 us -> 2.06 us  [the longest x1 1.69 us: per_device(): call(functools.partial(tables_body, n_r), [(6, rows, SUB, LANES), (2 * SU...]
    unnamed x2 -> x0, local copies, waits for them, and re-layouts: 0.76 us -> none
  transfers between devices with their start and end apart: 5 -> 4, of which waited for: 1 -> 0; matrix products, arithmetic and copies ran while one was open for 3% -> 3% of each run, Pallas kernels for 6% -> 4%
where the time goes in v2:
time: 48.3 us; the launch traced here: 48 us
  blocking collectives  23.9 us (49%)
  Pallas kernels  10.7 us (22%)
  starting transfers between devices  10.2 us (21%)
  other arithmetic  2.48 us (5%)
  between operations  0.72 us (1%)
    all_to_all x1, blocking collectives, per_device(): recv = lax.all_to_all(payload, BOTH, 0, 0)  14.1 us
    all_to_all x1, blocking collectives, per_device(): fed = lax.all_to_all(payload, BOTH, 0, 0)  9.82 us
    ppermute x2, starting transfers between devices, swap(): return (lax.ppermute(a, axis, first), b)  8.83 us
    pallas_call x1, Pallas kernels, per_device(): call(functools.partial(new_body, n_r, n_c, spread), [(2 * F, rows, LANES)...  3.53 us
    pallas_call x1, Pallas kernels, per_device(): call(functools.partial(near_body, n_r, n_c), [(slots, SLOT, LANES), (4 *...  2.59 us
    pallas_call x1, Pallas kernels, per_device(): call(functools.partial(last_body, n_r, n_c, spread), [(2 * F, rows, LANES...  2.42 us
    pallas_call x1, Pallas kernels, per_device(): call(functools.partial(tables_body, n_r), [(6, rows, SUB, LANES), (2 * SU...  1.69 us
    ppermute x2, starting transfers between devices, swap(): b = lax.ppermute(b, axis, second)  1.32 us
  transfers between devices with their start and end apart: 4, of which 0 were waited for; matrix products, arithmetic and copies ran while one was open for 3% of the time, Pallas kernels for 4%

profile of v2, /device:TPU:0, one launch (start us, length us, event | category | flops | bytes accessed | tf_op | source)
XLA Modules:
  0.0 48.0 jit_solution(8388229114649914905)
XLA Ops:
  0.6 0.8 %pad_maximum_fusion.fields = f32[13,16,128]{2,1,0:T(8,128)S(1)} fusion(f32[4,16,128]{2,1,0:T(8,128)} %param.8, f32[4,16,128]{2,1,0:T(8,128)} %param.9, f32[1,16,128]{2,1,0:T(8,128)} %bitcast.5, f32[4,16,128]{2,1,0:T(8,128)} %param.10), kind=kLoop, calls=%fused_computation.1 | loop fusion | flops 79872 | bytes 212992 | tf_op jit(solution)/shard_map/concatenate | solution.py:826
  1.5 0.1 shard_map.96
  1.6 0.7 %collective-permute-start = (f32[16,128]{1,0:T(8,128)S(1)}, f32[16,128]{1,0:T(8,128)S(1)}, u32[]{:S(2)}, u32[]{:S(2)}) collective-permute-start(f32[16,128]{1,0:T(8,128)S(1)} %get-tuple-element.42), channel_id=1, source_target_pairs={{1,2},{2,1},{5,6},{6,5},{9,10},{10,9},{13,14},{14,13},{17,18},{18,... | collective-permute-start | bytes 24584 | tf_op jit(solution)/shard_map/ppermute | solution.py:816
  2.2 5.9 %collective-permute-start.1 = (f32[16,128]{1,0:T(8,128)S(1)}, f32[16,128]{1,0:T(8,128)S(1)}, u32[]{:S(2)}, u32[]{:S(2)}) collective-permute-start(f32[16,128]{1,0:T(8,128)S(1)} %get-tuple-element.43), channel_id=1, source_target_pairs={{0,1},{1,0},{2,3},{3,2},{4,5},{5,4},{6,7},{7,6},{8,9},{9,8},{10,11... | collective-permute-start | bytes 24584 | tf_op jit(solution)/shard_map/ppermute | solution.py:817
  8.1 0.7 %pad_maximum_fusion.1.params = f32[6,64]{1,0:T(8,128)S(1)} fusion(f32[2,64]{1,0:T(2,128)} %bitcast.7, f32[4,64]{1,0:T(4,128)} %bitcast.6), kind=kLoop, calls=%fused_computation.2 | loop fusion | flops 384 | bytes 3072 | tf_op jit(solution)/shard_map/concatenate | solution.py:836
  8.8 0.3 shard_map.97
  9.1 1.7 %shard_map.95 = (f32[6,16,8,128]{3,2,1,0:T(8,128)S(1)}, f32[16,128]{1,0:T(8,128)S(1)}) custom-call(f32[13,16,128]{2,1,0:T(8,128)S(1)} %pad_maximum_fusion.fields), custom_call_target="tpu_custom_call" | custom-call | flops 2000000 | bytes 1048576 | tf_op jit(solution)/shard_map/pallas_call | solution.py:830
  10.8 0.0 collective-permute-done.recv_b.cols_b
  10.8 0.0 collective-permute-done.1.recv_a.cols_a
  10.9 0.7 %collective-permute-start.2 = (f32[48,128]{1,0:T(8,128)S(1)}, f32[48,128]{1,0:T(8,128)S(1)}, u32[]{:S(2)}, u32[]{:S(2)}) collective-permute-start(f32[48,128]{1,0:T(8,128)S(1)} %get-tuple-element.49), channel_id=1, source_target_pairs={{4,8},{12,16},{20,24},{8,4},{16,12},{24,20},{5,9},{13,17},{21,25},... | collective-permute-start | bytes 73736 | tf_op jit(solution)/shard_map/ppermute | solution.py:816
  11.5 2.9 %collective-permute-start.3 = (f32[48,128]{1,0:T(8,128)S(1)}, f32[48,128]{1,0:T(8,128)S(1)}, u32[]{:S(2)}, u32[]{:S(2)}) collective-permute-start(f32[48,128]{1,0:T(8,128)S(1)} %get-tuple-element.50), channel_id=1, source_target_pairs={{0,4},{4,0},{8,12},{12,8},{16,20},{20,16},{24,28},{28,24},{1,5},{5... | collective-permute-start | bytes 73736 | tf_op jit(solution)/shard_map/ppermute | solution.py:817
  14.5 1.0 %pad_add_fusion.lists = s32[25,16,128]{2,1,0:T(8,128)S(1)} fusion(s32[1,16,128]{2,1,0:T(8,128)} %bitcast.4, s32[24,16,128]{2,1,0:T(8,128)} %param.12), kind=kLoop, calls=%fused_computation | loop fusion | flops 51200 | bytes 409600 | tf_op jit(solution)/shard_map/concatenate | solution.py:844
  15.4 0.1 shard_map.99.bits
  15.5 0.0 collective-permute-done.2.rows_b
  15.5 0.0 collective-permute-done.3.rows_a
  15.5 2.6 %shard_map.100 = (f32[32,16,128]{2,1,0:T(8,128)S(1)}, f32[192,16,128]{2,1,0:T(8,128)S(1)}, f32[4,16,128]{2,1,0:T(8,128)S(1)}) custom-call(f32[13,16,128]{2,1,0:T(8,128)S(1)} %pad_maximum_fusion.fields, s32[2,16,128]{2,1,0:T(8,128)S(1)} %shard_map.99.bits, f32[1,128]{1,0:T(1,128)S(1)} %get-tuple-element.48.share, ...), custom_call_target="tpu_custom_call" | custom-call | flops 2000000 | bytes 1048576 | tf_op jit(solution)/shard_map/pallas_call | solution.py:847
  18.1 14.1 %all_to_all.10.recv = f32[32,16,128]{2,1,0:T(8,128)S(1)} all-to-all(f32[32,16,128]{2,1,0:T(8,128)S(1)} %get-tuple-element.52), channel_id=1, replica_groups=mesh['rng'=8,'xr'=4] {'rng','xr'}, dimensions={0} | all-to-all | bytes 524288 | tf_op jit(solution)/shard_map/all_to_all | solution.py:862
  32.2 3.5 %shard_map.101 = (f32[4,16,128]{2,1,0:T(8,128)S(1)}, f32[4,16,128]{2,1,0:T(8,128)S(1)}, f32[32,2,128]{2,1,0:T(2,128)S(1)}, f32[5,7,2,8,128]{4,3,2,1,0:T(8,128)S(...) custom-call(f32[32,16,128]{2,1,0:T(8,128)S(1)} %all_to_all.10.recv, ...), custom_call_target="tpu_custom_call" | custom-call | flops 2000000 | bytes 1048576 | tf_op jit(solution)/shard_map/pallas_call | solution.py:864
  35.7 9.8 %all_to_all.11.fed = f32[32,2,128]{2,1,0:T(2,128)S(1)} all-to-all(f32[32,2,128]{2,1,0:T(2,128)S(1)} %get-tuple-element.57), channel_id=1, replica_groups=mesh['rng'=8,'xr'=4] {'rng','xr'}, dimensions={0} | all-to-all | bytes 65536 | tf_op jit(solution)/shard_map/all_to_all | solution.py:892
  45.6 2.4 %shard_map.102 = (f32[4,16,128]{2,1,0:T(8,128)}, f32[4,16,128]{2,1,0:T(8,128)}) custom-call(f32[32,16,128]{2,1,0:T(8,128)S(1)} %all_to_all.10.recv, f32[32,2,128]{2,1,0:T(2,128)S(1)} %all_to_all.11.fed, f32[4,16,128]{2,1,0:T(8,128)S(1)} %get-tuple-element.58.new, f32[4,16,128]{2,1,0:T(8,128)S(1)} %get-tuple-element.59.driven, ...), custom_call_target="tpu_custom_call" | custom-call | flops 2000000 | bytes 1048576 | tf_op jit(solution)/shard_map/pallas_call | solution.py:893
  (1 shorter events, 0.0 us)
Async XLA Ops:
  1.6 9.3 %collective-permute-start = (f32[16,128]{1,0:T(8,128)S(1)}, f32[16,128]{1,0:T(8,128)S(1)}, u32[]{:S(2)}, u32[]{:S(2)}) collective-permute-start(f32[16,128]{1,0:T(8,128)S(1)} %get-tuple-element.42), channel_id=1, source_target_pairs={{1,2},{2,1},{5,6},{6,5},{9,10},{10,9},{13,14},{14,13},{17,18},{18,... | collective-permute-start | bytes 24584 | tf_op jit(solution)/shard_map/ppermute | solution.py:816
  2.2 8.6 %collective-permute-start.1 = (f32[16,128]{1,0:T(8,128)S(1)}, f32[16,128]{1,0:T(8,128)S(1)}, u32[]{:S(2)}, u32[]{:S(2)}) collective-permute-start(f32[16,128]{1,0:T(8,128)S(1)} %get-tuple-element.43), channel_id=1, source_target_pairs={{0,1},{1,0},{2,3},{3,2},{4,5},{5,4},{6,7},{7,6},{8,9},{9,8},{10,11... | collective-permute-start | bytes 24584 | tf_op jit(solution)/shard_map/ppermute | solution.py:817
  10.9 4.6 %collective-permute-start.2 = (f32[48,128]{1,0:T(8,128)S(1)}, f32[48,128]{1,0:T(8,128)S(1)}, u32[]{:S(2)}, u32[]{:S(2)}) collective-permute-start(f32[48,128]{1,0:T(8,128)S(1)} %get-tuple-element.49), channel_id=1, source_target_pairs={{4,8},{12,16},{20,24},{8,4},{16,12},{24,20},{5,9},{13,17},{21,25},... | collective-permute-start | bytes 73736 | tf_op jit(solution)/shard_map/ppermute | solution.py:816
  11.5 4.0 %collective-permute-start.3 = (f32[48,128]{1,0:T(8,128)S(1)}, f32[48,128]{1,0:T(8,128)S(1)}, u32[]{:S(2)}, u32[]{:S(2)}) collective-permute-start(f32[48,128]{1,0:T(8,128)S(1)} %get-tuple-element.50), channel_id=1, source_target_pairs={{0,4},{4,0},{8,12},{12,8},{16,20},{20,16},{24,28},{28,24},{1,5},{5... | collective-permute-start | bytes 73736 | tf_op jit(solution)/shard_map/ppermute | solution.py:817

commit v3 on v2

--- a/solution.py
+++ b/solution.py
@@ -199,7 +199,7 @@
                     gens[at : at + 1] = row
 
 
-def lists_body(lists, bits):
+def list_bits(lists):
     count = lists[LMAX]
     low = jnp.zeros(count.shape, jnp.int32)
     high = jnp.zeros(count.shape, jnp.int32)
@@ -212,8 +212,7 @@
         bit = lax.shift_left(one, jnp.where(is_low, code, code - half))
         low = low | jnp.where(live & is_low, bit, 0)
         high = high | jnp.where(live & (code >= half), bit, 0)
-    bits[0] = low
-    bits[1] = high
+    return low, high
 
 
 def params_body(params, weights, share, columns):
@@ -301,42 +300,164 @@
     return sides
 
 
+PAIRS = [(row, beyond) for row in range(H) for beyond in range(H - row)]
+SHIFTS = 2 * H + 1
+
+
+def pair_rows(top, bottom, beyond):
+    which = [pair[1 if beyond else 0] for pair in PAIRS]
+    rest = jnp.zeros((SUB - len(PAIRS), LANES), top[0].dtype)
+    parts = []
+    for edge in (top, bottom):
+        parts += [edge[i] for i in which] + [rest]
+    return jnp.concatenate(parts, axis=0)
+
+
+def row_list(array, indices):
+    return [array[i : i + 1] for i in indices]
+
+
+def put_pairs(near, spill, k):
+    rows = spill.shape[1]
+    spill[k] = jnp.zeros(spill.shape[1:], f32)
+    for edge in range(2):
+        at = SUB * edge
+        for row in range(H):
+            count = H - row
+            total = near[at : at + 1]
+            for i in range(1, count):
+                total = total + near[at + i : at + i + 1]
+            at += count
+            to = rows - 1 - row if edge else row
+            spill[k, to : to + 1] = total
+
+
+def coupling(squared, there):
+    inverse_r = lax.rsqrt(squared)
+    size = jnp.where(there, GREEN * inverse_r, 0.0)
+    off = squared * inverse_r * (1.0 / 16.0) - 0.25
+    sq = off * off
+    w = (-off * polynomial(SINE, sq), polynomial(COSINE, sq))
+    fourth = square(square(w))
+    out = []
+    for power in (fourth, times(fourth, w)):
+        out += [size * power[0], size * power[1]]
+    return out
+
+
+def square(a):
+    return a[0] * a[0] - a[1] * a[1], 2.0 * a[0] * a[1]
+
+
+def polynomial(coefficients, x):
+    total = coefficients[-1]
+    for value in coefficients[-2::-1]:
+        total = total * x + value
+    return total
+
+
+SINE = (6.283185280367426, -41.341680722295834, 81.60248507719457, -76.58139539835082, 39.76160778337109)
+COSINE = (1.0, -19.739208548909147, 64.93934662883956, -85.4535715937672, 60.144014415422156, -24.982233003994804)
+
+
+def add_near(near, g, window):
+    for f in range(F):
+        got = times((g[2 * f], g[2 * f + 1]), (window(2 * f), window(2 * f + 1)))
+        near[2 * f] = near[2 * f] + got[0]
+        near[2 * f + 1] = near[2 * f + 1] + got[1]
+
+
+def side_columns(cols_a, cols_b):
+    even = (lax.axis_index("xr") & 1) == 0
+    return jnp.where(even, cols_b[...], cols_a[...]), jnp.where(even, cols_a[...], cols_b[...])
+
+
+def store_shifted(moved, k, middle, side):
+    rows = middle.shape[0]
+    for dy in range(-H, H + 1):
+        moved[k * SHIFTS + dy + H, TOP : TOP + rows] = shifted(middle, side, dy)
+
+
+def inner_body(fields, lists, cols_b, cols_a, green, near_out, bits, moved):
+    rows = fields.shape[1]
+    low, high = list_bits(lists)
+    bits[0] = low
+    bits[1] = high
+    from_left, from_right = side_columns(cols_a, cols_b)
+    for k in range(2 * F + 1):
+        for i in range(SHIFTS):
+            moved[k * SHIFTS + i, 0:TOP] = jnp.zeros((TOP, LANES), f32)
+            moved[k * SHIFTS + i, TOP + rows :] = jnp.zeros((TOP, LANES), f32)
+        store_shifted(moved, k, fields[k], unpack_columns(from_left, from_right, k))
+    h = fields[2 * F]
+    half = OFFSETS // 2
+    row = iota((rows, LANES), 0)
+    masked = {}
+    for dx in range(-H, H + 1):
+        inside = (row + dx >= 0) & (row + dx < rows)
+        masked[dx] = (jnp.where(inside, low, 0), jnp.where(inside, high, 0))
+    near = [jnp.zeros((rows, LANES), f32) for _ in range(2 * F)]
+    for code in range(OFFSETS):
+        dx, dy = offset_of(code)
+        window = lambda k: moved[k * SHIFTS + dy + H, TOP + dx : TOP + dx + rows]
+        lift = window(2 * F) - h
+        there = (masked[dx][code // half] & (1 << (code % half))) != 0
+        g = coupling(float(dx * dx + dy * dy) + lift * lift, there)
+        for k in range(2 * F):
+            green[4 * code + k] = g[k]
+        add_near(near, g, window)
+    for k in range(2 * F):
+        near_out[k] = near[k]
+
+
 def near_body(
-    n_r, n_c, fields, bits, share, cols_b, cols_a, rows_b, rows_a, gens, tables,
-    payload, green, source, inner, edge_l, edge_r, moved, cs, left_mat, right_mat, common, halo,
+    n_r, n_c, fields, bits, inner_near, share, cols_b, cols_a, rows_b, rows_a, gens, tables,
+    payload, edge_green, source, spill, cs, left_mat, right_mat, common, halo,
 ):
     rows = fields.shape[1]
     d, c = place_of()
     above, below = halo_rows(rows_a, rows_b)
-    sides = with_halo(range(2 * F + 1), fields, cols_a, cols_b, above, below, inner, edge_l, edge_r)
-    for k, side in enumerate(sides):
-        middle = inner[k]
-        for dy in range(-H, H + 1):
-            moved[k * (2 * H + 1) + dy + H] = shifted(middle, side, dy)
+    backwards = range(H - 1, -1, -1)
+    last_rows = range(rows - 1, rows - 1 - H, -1)
+    at = H * N_FIELDS
+    from_left, from_right = (
+        pair_rows(
+            row_list(above[at + H * i : at + H * (i + 1)], backwards),
+            row_list(below[at + H * i : at + H * (i + 1)], range(H)),
+            True,
+        )
+        for i in range(2)
+    )
     h = fields[2 * F]
     inverse = [fields[2 * F + 1 + k] for k in range(2 * F)]
     incident = [fields[N_FIELDS + k] for k in range(2 * F)]
-    low, high = bits[0], bits[1]
-    half = OFFSETS // 2
-    near = [jnp.zeros((rows, LANES), f32) for _ in range(2 * F)]
-    for code in range(OFFSETS):
-        dx, dy = offset_of(code)
-        window = lambda k: moved[k * (2 * H + 1) + dy + H, TOP + dx : TOP + dx + rows]
-        lift = window(2 * F) - h
-        squared = float(dx * dx + dy * dy) + lift * lift
-        inverse_r = lax.rsqrt(squared)
-        r = squared * inverse_r
-        bits = low if code < half else high
-        there = (bits & (1 << (code % half))) != 0
-        size = jnp.where(there, GREEN * inverse_r, 0.0)
-        for f in range(F):
-            cos, sin = cos_sin(r * (0.25 * (1.0 + 0.25 * f)))
-            g = (size * cos, size * sin)
-            green[4 * code + 2 * f] = g[0]
-            green[4 * code + 2 * f + 1] = g[1]
-            got = times(g, (window(2 * f), window(2 * f + 1)))
-            near[2 * f] += got[0]
-            near[2 * f + 1] += got[1]
+    h_pairs = pair_rows(row_list(h, range(H)), row_list(h, last_rows), False)
+    flags = pair_rows(row_list(bits[0], range(H)), row_list(bits[1], last_rows), False)
+    row = iota((2 * SUB, LANES), 0)
+    lower = row >= SUB
+    nth = row & (SUB - 1)
+    reach = jnp.zeros((2 * SUB, LANES), jnp.int32)
+    for i, (inside, beyond) in enumerate(PAIRS):
+        reach = jnp.where(nth == i, inside + beyond + 1, reach)
+    first_bit = jnp.where(lower, (H + reach) * SHIFTS + H - 1 - OFFSETS // 2, (H - reach) * SHIFTS + H)
+    moved = []
+    for k in range(2 * F + 1):
+        middle = pair_rows(
+            row_list(above[H * k : H * (k + 1)], backwards), row_list(below[H * k : H * (k + 1)], range(H)), True
+        )
+        side = unpack_columns(from_left, from_right, k)
+        moved.append([shifted(middle, side, dy) for dy in range(-H, H + 1)])
+    near = [jnp.zeros((2 * SUB, LANES), f32) for _ in range(2 * F)]
+    for dy in range(-H, H + 1):
+        lift = moved[2 * F][dy + H] - h_pairs
+        there = (lax.shift_right_logical(flags, first_bit + dy) & 1) == 1
+        g = coupling((reach * reach + dy * dy).astype(f32) + lift * lift, there & (nth < len(PAIRS)))
+        for k in range(2 * F):
+            edge_green[4 * (dy + H) + k] = g[k]
+        add_near(near, g, lambda k: moved[k][dy + H])
+    for k in range(2 * F):
+        put_pairs(near[k], spill, k)
+    near = [inner_near[k] + spill[k] for k in range(2 * F)]
     x, y = place_ids(rows, LANES, 0, 0, rows)
     sources = []
     for f in range(F):
@@ -662,9 +783,9 @@
 
 
 def new_body(
-    n_r, n_c, spread, recv, green, source, fields, cols_b, cols_a, rows_b, rows_a, tables, weights, columns,
+    n_r, n_c, spread, recv, green, edge_green, source, fields, cols_b, cols_a, rows_b, rows_a, tables, weights, columns,
     forward, driven, payload, second, back_first, back_carriers, below_gens,
-    loss, first, carriers, amps, held, inner, moved, edge_l, edge_r, cs, left_mat, right_mat, common, halo,
+    loss, first, carriers, amps, held, inner, moved, edge_l, edge_r, spill, cs, left_mat, right_mat, common, halo,
 ):
     rows = fields.shape[1]
     d, c = place_of()
@@ -728,22 +849,33 @@
             for part in range(2):
                 weak[t, 2 * f + part] = w[part]
                 lost[t, 2 * f + part] = got[part]
+    beyond = []
     for k in range(2 * F):
         tiles = [lost[t, k] for t in range(MERGED)]
         side = sides[k] - jnp.concatenate(apart(tiles), axis=0)
         middle = inner[k] - jnp.concatenate(tiles[:4], axis=0)
         forward[k] = middle[TOP : TOP + rows]
-        for dy in range(-H, H + 1):
-            moved[k * (2 * H + 1) + dy + H] = shifted(middle, side, dy)
-    near = [jnp.zeros((rows, LANES), f32) for _ in range(2 * F)]
+        for i in range(SHIFTS):
+            moved[k * SHIFTS + i, 0:TOP] = jnp.zeros((TOP, LANES), f32)
+            moved[k * SHIFTS + i, TOP + rows :] = jnp.zeros((TOP, LANES), f32)
+        store_shifted(moved, k, middle[TOP : TOP + rows], side[TOP : TOP + rows])
+        above_edge = range(TOP - 1, TOP - 1 - H, -1)
+        below_edge = range(TOP + rows, TOP + rows + H)
+        pairs = [pair_rows(row_list(part, above_edge), row_list(part, below_edge), True) for part in (middle, side)]
+        beyond.append([shifted(*pairs, dy) for dy in range(-H, H + 1)])
+    near = [jnp.zeros((2 * SUB, LANES), f32) for _ in range(2 * F)]
+    for dy in range(-H, H + 1):
+        add_near(near, [edge_green[4 * (dy + H) + k] for k in range(2 * F)], lambda k: beyond[k][dy + H])
+    for k in range(2 * F):
+        put_pairs(near[k], spill, k)
+    near = [spill[k] for k in range(2 * F)]
     for code in range(OFFSETS):
         dx, dy = offset_of(code)
-        window = lambda k: moved[k * (2 * H + 1) + dy + H, TOP + dx : TOP + dx + rows]
-        for f in range(F):
-            g = (green[4 * code + 2 * f], green[4 * code + 2 * f + 1])
-            add = times(g, (window(2 * f), window(2 * f + 1)))
-            near[2 * f] += add[0]
-            near[2 * f + 1] += add[1]
+        add_near(
+            near,
+            [green[4 * code + k] for k in range(2 * F)],
+            lambda k: moved[k * SHIFTS + dy + H, TOP + dx : TOP + dx + rows],
+        )
     for f in range(F):
         rest = []
         for part in range(2):
@@ -842,23 +974,31 @@
     rows_a, rows_b, neighbours, counts = lax.optimization_barrier((rows_a, rows_b, neighbours, counts))
     rows_a, rows_b = swap("rng", n_r, rows_a, rows_b)
     lists = jnp.concatenate([neighbours, counts[None]])
-    (bits,) = call(lists_body, [jax.ShapeDtypeStruct((2, rows, LANES), jnp.int32)], [VMEM], flops=500_000)(lists)
+    green, inner_near, bits = call(
+        inner_body,
+        [
+            (4 * OFFSETS, rows, LANES),
+            (2 * F, rows, LANES),
+            jax.ShapeDtypeStruct((2, rows, LANES), jnp.int32),
+        ],
+        [VMEM] * 4,
+        [pltpu.VMEM(((2 * F + 1) * SHIFTS, tall, LANES), f32)],
+        500_000,
+    )(fields, lists, cols_b, cols_a)
     edges = [pltpu.VMEM((tall, LANES), f32)] * 2
-    payload, green, source = call(
+    payload, edge_green, source = call(
         functools.partial(near_body, n_r, n_c),
-        [(slots, SLOT, LANES), (4 * OFFSETS, rows, LANES), (2 * F, rows, LANES)],
-        [VMEM] * 9,
+        [(slots, SLOT, LANES), (4 * SHIFTS, 2 * SUB, LANES), (2 * F, rows, LANES)],
+        [VMEM] * 10,
         [
-            pltpu.VMEM((2 * F + 1, tall, LANES), f32),
-            *edges,
-            pltpu.VMEM(((2 * F + 1) * (2 * H + 1), tall, LANES), f32),
+            pltpu.VMEM((2 * F, rows, LANES), f32),
             pltpu.VMEM((2 * F, rows, LANES), f32),
             pltpu.VMEM((4 * SUB, patches), f32),
             pltpu.VMEM((16 * SUB, patches), f32),
             pltpu.VMEM((3 * SUB, LANES), f32),
             pltpu.VMEM((2 * SUB, LANES), f32),
         ],
-    )(fields, bits, share, cols_b, cols_a, rows_b, rows_a, gens, tables)
+    )(fields, bits, inner_near, share, cols_b, cols_a, rows_b, rows_a, gens, tables)
     recv = lax.all_to_all(payload, BOTH, 0, 0)
     tile = (2, SUB, LANES)
     new, driven, payload, second, back_first, back_carriers, below_gens = call(
@@ -872,7 +1012,7 @@
             (2, F, *tile),
             (SUB, LANES),
         ],
-        [VMEM] * 11,
+        [VMEM] * 12,
         [
             pltpu.VMEM((MERGED, 2 * F, SUB, LANES), f32),
             pltpu.VMEM((MERGED, Q // SUB - 1, *tile), f32),
@@ -883,12 +1023,13 @@
             pltpu.VMEM((2 * F * (2 * H + 1), tall, LANES), f32),
             *edges,
             pltpu.VMEM((2 * F, rows, LANES), f32),
+            pltpu.VMEM((2 * F, rows, LANES), f32),
             pltpu.VMEM((4 * SUB, patches), f32),
             pltpu.VMEM((16 * SUB, patches), f32),
             pltpu.VMEM((SUB, LANES), f32),
             pltpu.VMEM((2, 2 * SUB, LANES), f32),
         ],
-    )(recv, green, source, fields, cols_b, cols_a, rows_b, rows_a, tables, weights, columns)
+    )(recv, green, edge_green, source, fields, cols_b, cols_a, rows_b, rows_a, tables, weights, columns)
     fed = lax.all_to_all(payload, BOTH, 0, 0)
     return call(
         functools.partial(last_body, n_r, n_c, spread),

time: 48.3 us -> 47 us (0.973)
  blocking collectives: 23.9 us -> 22.9 us
    pallas_call x1, Pallas kernels: 2.59 us -> 1.26 us  [per_device(): call(functools.partial(near_body, n_r, n_c), [(slots, SLOT, LANES), (4 *...]
    all_to_all x1, blocking collectives: 14.1 us -> 13 us  [per_device(): recv = lax.all_to_all(payload, BOTH, 0, 0)]
    pallas_call x1, Pallas kernels: 0.09 us -> 1.13 us  [per_device(): call(inner_body, [(4 * OFFSETS, rows, LANES), (2 * F, rows, LANES), jax.S...]
  transfers between devices with their start and end apart: 4 -> 4, of which waited for: 0 -> 0; matrix products, arithmetic and copies ran while one was open for 3% -> 4% of each run, Pallas kernels for 4% -> 7%
where the time goes in v3:
time: 47 us; the launch traced here: 46.7 us
  blocking collectives  22.9 us (49%)
  Pallas kernels  10.5 us (22%)
  starting transfers between devices  10.2 us (22%)
  other arithmetic  2.48 us (5%)
  between operations  0.73 us (2%)
    all_to_all x1, blocking collectives, per_device(): recv = lax.all_to_all(payload, BOTH, 0, 0)  13 us
    all_to_all x1, blocking collectives, per_device(): fed = lax.all_to_all(payload, BOTH, 0, 0)  9.82 us
    ppermute x2, starting transfers between devices, swap(): return (lax.ppermute(a, axis, first), b)  8.83 us
    pallas_call x1, Pallas kernels, per_device(): call(functools.partial(new_body, n_r, n_c, spread), [(2 * F, rows, LANES)...  3.61 us
    pallas_call x1, Pallas kernels, per_device(): call(functools.partial(last_body, n_r, n_c, spread), [(2 * F, rows, LANES...  2.42 us
    pallas_call x1, Pallas kernels, per_device(): call(functools.partial(tables_body, n_r), [(6, rows, SUB, LANES), (2 * SU...  1.69 us
    ppermute x2, starting transfers between devices, swap(): b = lax.ppermute(b, axis, second)  1.32 us
    pallas_call x1, Pallas kernels, per_device(): call(functools.partial(near_body, n_r, n_c), [(slots, SLOT, LANES), (4 *...  1.26 us
  transfers between devices with their start and end apart: 4, of which 0 were waited for; matrix products, arithmetic and copies ran while one was open for 4% of the time, Pallas kernels for 7%

profile of v3, /device:TPU:0, one launch (start us, length us, event | category | flops | bytes accessed | tf_op | source)
XLA Modules:
  0.0 46.7 jit_solution(18331530388097011970)
XLA Ops:
  0.6 0.8 %pad_maximum_fusion.fields = f32[13,16,128]{2,1,0:T(8,128)S(1)} fusion(f32[4,16,128]{2,1,0:T(8,128)} %param.8, f32[4,16,128]{2,1,0:T(8,128)} %param.9, f32[1,16,128]{2,1,0:T(8,128)} %bitcast.5, f32[4,16,128]{2,1,0:T(8,128)} %param.10), kind=kLoop, calls=%fused_computation.1 | loop fusion | flops 79872 | bytes 212992 | tf_op jit(solution)/shard_map/concatenate | solution.py:958
  1.5 0.1 shard_map.96
  1.6 0.7 %collective-permute-start = (f32[16,128]{1,0:T(8,128)S(1)}, f32[16,128]{1,0:T(8,128)S(1)}, u32[]{:S(2)}, u32[]{:S(2)}) collective-permute-start(f32[16,128]{1,0:T(8,128)S(1)} %get-tuple-element.45), channel_id=1, source_target_pairs={{1,2},{2,1},{5,6},{6,5},{9,10},{10,9},{13,14},{14,13},{17,18},{18,... | collective-permute-start | bytes 24584 | tf_op jit(solution)/shard_map/ppermute | solution.py:948
  2.2 5.9 %collective-permute-start.1 = (f32[16,128]{1,0:T(8,128)S(1)}, f32[16,128]{1,0:T(8,128)S(1)}, u32[]{:S(2)}, u32[]{:S(2)}) collective-permute-start(f32[16,128]{1,0:T(8,128)S(1)} %get-tuple-element.46), channel_id=1, source_target_pairs={{0,1},{1,0},{2,3},{3,2},{4,5},{5,4},{6,7},{7,6},{8,9},{9,8},{10,11... | collective-permute-start | bytes 24584 | tf_op jit(solution)/shard_map/ppermute | solution.py:949
  8.1 0.7 %pad_maximum_fusion.1.params = f32[6,64]{1,0:T(8,128)S(1)} fusion(f32[2,64]{1,0:T(2,128)} %bitcast.7, f32[4,64]{1,0:T(4,128)} %bitcast.6), kind=kLoop, calls=%fused_computation.2 | loop fusion | flops 384 | bytes 3072 | tf_op jit(solution)/shard_map/concatenate | solution.py:968
  8.8 0.3 shard_map.97
  9.1 1.7 %shard_map.95 = (f32[6,16,8,128]{3,2,1,0:T(8,128)S(1)}, f32[16,128]{1,0:T(8,128)S(1)}) custom-call(f32[13,16,128]{2,1,0:T(8,128)S(1)} %pad_maximum_fusion.fields), custom_call_target="tpu_custom_call" | custom-call | flops 2000000 | bytes 1048576 | tf_op jit(solution)/shard_map/pallas_call | solution.py:962
  10.8 0.0 collective-permute-done.recv_b.cols_b
  10.8 0.0 collective-permute-done.1.recv_a.cols_a
  10.9 0.7 %collective-permute-start.2 = (f32[48,128]{1,0:T(8,128)S(1)}, f32[48,128]{1,0:T(8,128)S(1)}, u32[]{:S(2)}, u32[]{:S(2)}) collective-permute-start(f32[48,128]{1,0:T(8,128)S(1)} %get-tuple-element.54), channel_id=1, source_target_pairs={{4,8},{12,16},{20,24},{8,4},{16,12},{24,20},{5,9},{13,17},{21,25},... | collective-permute-start | bytes 73736 | tf_op jit(solution)/shard_map/ppermute | solution.py:948
  11.5 2.9 %collective-permute-start.3 = (f32[48,128]{1,0:T(8,128)S(1)}, f32[48,128]{1,0:T(8,128)S(1)}, u32[]{:S(2)}, u32[]{:S(2)}) collective-permute-start(f32[48,128]{1,0:T(8,128)S(1)} %get-tuple-element.55), channel_id=1, source_target_pairs={{0,4},{4,0},{8,12},{12,8},{16,20},{20,16},{24,28},{28,24},{1,5},{5... | collective-permute-start | bytes 73736 | tf_op jit(solution)/shard_map/ppermute | solution.py:949
  14.5 1.0 %pad_add_fusion.lists = s32[25,16,128]{2,1,0:T(8,128)S(1)} fusion(s32[1,16,128]{2,1,0:T(8,128)} %bitcast.4, s32[24,16,128]{2,1,0:T(8,128)} %param.12), kind=kLoop, calls=%fused_computation | loop fusion | flops 51200 | bytes 409600 | tf_op jit(solution)/shard_map/concatenate | solution.py:976
  15.4 1.1 %shard_map.99 = (f32[192,16,128]{2,1,0:T(8,128)S(1)}, f32[4,16,128]{2,1,0:T(8,128)S(1)}, s32[2,16,128]{2,1,0:T(8,128)S(1)}) custom-call(f32[13,16,128]{2,1,0:T(8,128)S(1)} %pad_maximum_fusion.fields, s32[25,16,128]{2,1,0:T(8,128)S(1)} %pad_add_fusion.lists, f32[16,128]{1,0:T(8,128)S(1)} %collective-permute-done.recv_b.cols_b, ...), custom_call_target="tpu_custom_call" | custom-call | flops 500000 | bytes 1048576 | tf_op jit(solution)/shard_map/pallas_call | solution.py:977
  16.6 0.0 collective-permute-done.2.rows_b
  16.6 0.0 collective-permute-done.3.rows_a
  16.6 1.3 %shard_map.100 = (f32[32,16,128]{2,1,0:T(8,128)S(1)}, f32[28,16,128]{2,1,0:T(8,128)S(1)}, f32[4,16,128]{2,1,0:T(8,128)S(1)}) custom-call(f32[13,16,128]{2,1,0:T(8,128)S(1)} %pad_maximum_fusion.fields, s32[2,16,128]{2,1,0:T(8,128)S(1)} %get-tuple-element.51.bits, f32[4,16,128]{2,1,0:T(8,128)S(1)} %get-tuple-element.52.inner_near, ...), custom_call_target="tpu_custom_call" | custom-call | flops 2000000 | bytes 1048576 | tf_op jit(solution)/shard_map/pallas_call | solution.py:989
  17.8 13.0 %all_to_all.10.recv = f32[32,16,128]{2,1,0:T(8,128)S(1)} all-to-all(f32[32,16,128]{2,1,0:T(8,128)S(1)} %get-tuple-element.57), channel_id=1, replica_groups=mesh['rng'=8,'xr'=4] {'rng','xr'}, dimensions={0} | all-to-all | bytes 524288 | tf_op jit(solution)/shard_map/all_to_all | solution.py:1002
  30.9 3.6 %shard_map.101 = (f32[4,16,128]{2,1,0:T(8,128)S(1)}, f32[4,16,128]{2,1,0:T(8,128)S(1)}, f32[32,2,128]{2,1,0:T(2,128)S(1)}, f32[5,7,2,8,128]{4,3,2,1,0:T(8,128)S(...) custom-call(f32[32,16,128]{2,1,0:T(8,128)S(1)} %all_to_all.10.recv, ...), custom_call_target="tpu_custom_call" | custom-call | flops 2000000 | bytes 1048576 | tf_op jit(solution)/shard_map/pallas_call | solution.py:1004
  34.5 9.8 %all_to_all.11.fed = f32[32,2,128]{2,1,0:T(2,128)S(1)} all-to-all(f32[32,2,128]{2,1,0:T(2,128)S(1)} %get-tuple-element.63), channel_id=1, replica_groups=mesh['rng'=8,'xr'=4] {'rng','xr'}, dimensions={0} | all-to-all | bytes 65536 | tf_op jit(solution)/shard_map/all_to_all | solution.py:1033
  44.3 2.4 %shard_map.102 = (f32[4,16,128]{2,1,0:T(8,128)}, f32[4,16,128]{2,1,0:T(8,128)}) custom-call(f32[32,16,128]{2,1,0:T(8,128)S(1)} %all_to_all.10.recv, f32[32,2,128]{2,1,0:T(2,128)S(1)} %all_to_all.11.fed, f32[4,16,128]{2,1,0:T(8,128)S(1)} %get-tuple-element.64.new, f32[4,16,128]{2,1,0:T(8,128)S(1)} %get-tuple-element.65.driven, ...), custom_call_target="tpu_custom_call" | custom-call | flops 2000000 | bytes 1048576 | tf_op jit(solution)/shard_map/pallas_call | solution.py:1034
  (1 shorter events, 0.0 us)
Async XLA Ops:
  1.6 9.3 %collective-permute-start = (f32[16,128]{1,0:T(8,128)S(1)}, f32[16,128]{1,0:T(8,128)S(1)}, u32[]{:S(2)}, u32[]{:S(2)}) collective-permute-start(f32[16,128]{1,0:T(8,128)S(1)} %get-tuple-element.45), channel_id=1, source_target_pairs={{1,2},{2,1},{5,6},{6,5},{9,10},{10,9},{13,14},{14,13},{17,18},{18,... | collective-permute-start | bytes 24584 | tf_op jit(solution)/shard_map/ppermute | solution.py:948
  2.2 8.6 %collective-permute-start.1 = (f32[16,128]{1,0:T(8,128)S(1)}, f32[16,128]{1,0:T(8,128)S(1)}, u32[]{:S(2)}, u32[]{:S(2)}) collective-permute-start(f32[16,128]{1,0:T(8,128)S(1)} %get-tuple-element.46), channel_id=1, source_target_pairs={{0,1},{1,0},{2,3},{3,2},{4,5},{5,4},{6,7},{7,6},{8,9},{9,8},{10,11... | collective-permute-start | bytes 24584 | tf_op jit(solution)/shard_map/ppermute | solution.py:949
  10.9 5.7 %collective-permute-start.2 = (f32[48,128]{1,0:T(8,128)S(1)}, f32[48,128]{1,0:T(8,128)S(1)}, u32[]{:S(2)}, u32[]{:S(2)}) collective-permute-start(f32[48,128]{1,0:T(8,128)S(1)} %get-tuple-element.54), channel_id=1, source_target_pairs={{4,8},{12,16},{20,24},{8,4},{16,12},{24,20},{5,9},{13,17},{21,25},... | collective-permute-start | bytes 73736 | tf_op jit(solution)/shard_map/ppermute | solution.py:948
  11.5 5.0 %collective-permute-start.3 = (f32[48,128]{1,0:T(8,128)S(1)}, f32[48,128]{1,0:T(8,128)S(1)}, u32[]{:S(2)}, u32[]{:S(2)}) collective-permute-start(f32[48,128]{1,0:T(8,128)S(1)} %get-tuple-element.55), channel_id=1, source_target_pairs={{0,4},{4,0},{8,12},{12,8},{16,20},{20,16},{24,28},{28,24},{1,5},{5... | collective-permute-start | bytes 73736 | tf_op jit(solution)/shard_map/ppermute | solution.py:949

commit v4 on v3

--- a/solution.py
+++ b/solution.py
@@ -215,14 +215,15 @@
     return low, high
 
 
-def params_body(params, weights, share, columns):
-    spot = iota((Q, LANES), 0)
-    spot = 2 * SUB * (spot // SUB) + (spot & (SUB - 1))
-    values = params[...]
+def params_body(fields, weights, share, columns):
+    spot = iota((LANES, LANES), 0)
+    spot = jnp.where(spot < Q, 2 * SUB * (spot // SUB) + (spot & (SUB - 1)), 2 * LANES)
+    base = N_FIELDS + 2 * F
+    values = jnp.concatenate([fields[base + i, 0:2] for i in range(F + 1)] + [fields[base + F, 2:4]], axis=0)
     placed = [
         lax.dot_general(
             values,
-            (iota((Q, LANES), 1) == spot + SUB * k).astype(f32),
+            (iota((LANES, LANES), 1) == spot + SUB * k).astype(f32),
             (((1,), (0,)), ((), ())),
             precision=HIGHEST,
             preferred_element_type=f32,
@@ -479,18 +480,13 @@
     common[0 : 2 * SUB] = gens[...]
     common[2 * SUB + 2 : 2 * SUB + 3] = share[...]
     tail = common[2 * SUB : 3 * SUB]
-    for direction in range(2):
-        part = common[direction * SUB : (direction + 1) * SUB]
-
-        def fill(s, _, part=part, tail=tail):
-            payload[s, 0:SUB] = part
-            payload[s, SUB : 2 * SUB] = tail
-            return 0
-
-        if direction == 0:
-            lax.fori_loop(d * n_c, n_r * n_c, fill, 0)
-        else:
-            lax.fori_loop(0, d * n_c, fill, 0)
+    down, up = common[0:SUB], common[SUB : 2 * SUB]
+
+    def fill(s):
+        payload[s, 0:SUB] = jnp.where(s >= d * n_c, down, up)
+        payload[s, SUB : 2 * SUB] = tail
+
+    laps(n_r * n_c, fill, 8 * SUB)
     lasts = pack_columns(sources, True)
     firsts = pack_columns(sources, False)
     at = HALO_AT
@@ -609,10 +605,10 @@
         full = feeds[f] if carry is None else carry[f] + feeds[f]
         full = [jnp.where(diagonal(k), full, 0.0) for k in range(TILES)]
         if carry is None:
-            put(f, [jnp.zeros((SUB, LANES), f32)] * TILES)
+            put(f, jnp.zeros((SUB, LANES), f32))
         else:
             amp = spread * packed_times(weights[2 * f], weights[2 * f + 1], carry[f])
-            put(f, to_columns(amp))
+            put(f, amp)
             turns = [roll(amp, -2 * SUB * a1) if late else amp for a1 in range(Q // SUB)]
             full = [part - tile * turns[k // 2] for k, (part, tile) in enumerate(zip(full, maps(f), strict=True))]
         share = [jnp.sum(jnp.where(diagonal(k), shares[f], 0.0), axis=1, keepdims=True) for k in range(0, TILES, 2)]
@@ -666,19 +662,31 @@
             put(n_r - 1, f, [spread * part for part in column_times(columns, last[f], f)])
     elif carry is not None:
         for f in range(F):
-            put(n_r - 1, f, to_columns(spread * packed_times(rows[2 * f], rows[2 * f + 1], carry[f])))
-
-
-def putter(amps):
-    def put(j, f, columns):
-        for k, column in enumerate(columns):
-            amps[j, f, SUB * k : SUB * (k + 1)] = jnp.broadcast_to(column, (SUB, LANES))
+            put(n_r - 1, f, spread * packed_times(rows[2 * f], rows[2 * f + 1], carry[f]))
+
+
+def putter(amps, held):
+    def put(j, f, value):
+        if isinstance(value, list):
+            put_columns(amps, j, f, value)
+        else:
+            held[j // 2, f] = value
 
     return put
 
 
-def laps(n, body):
-    if n <= SUB:
+def put_columns(amps, j, f, columns):
+    for k, column in enumerate(columns):
+        amps[j, f, SUB * k : SUB * (k + 1)] = jnp.broadcast_to(column, (SUB, LANES))
+
+
+def take_rows(amps, held, j):
+    for f in range(F):
+        put_columns(amps, j, f, to_columns(held[j // 2, f]))
+
+
+def laps(n, body, few):
+    if n <= few:
         for j in range(n):
             body(j)
     else:
@@ -785,7 +793,7 @@
 def new_body(
     n_r, n_c, spread, recv, green, edge_green, source, fields, cols_b, cols_a, rows_b, rows_a, tables, weights, columns,
     forward, driven, payload, second, back_first, back_carriers, below_gens,
-    loss, first, carriers, amps, held, inner, moved, edge_l, edge_r, spill, cs, left_mat, right_mat, common, halo,
+    loss, first, carriers, amps, kept, held, inner, moved, edge_l, edge_r, spill, cs, left_mat, right_mat, common, halo,
 ):
     rows = fields.shape[1]
     d, c = place_of()
@@ -810,7 +818,10 @@
             feed = feed + recv[j * n_c + k, SUB : 2 * SUB]
         return [wide(feed[f : f + 1]) for f in range(F)]
 
-    sweep(n_r, maps, feeds, lambda j: recv[j * n_c, SUB + 2 : SUB + 3], weights, columns, spread, putter(amps), False)
+    sweep(n_r, maps, feeds, lambda j: recv[j * n_c, SUB + 2 : SUB + 3], weights, columns, spread, putter(amps, kept), False)
+    even = d - (d & 1)
+    take_rows(amps, kept, even)
+    take_rows(amps, kept, jnp.minimum(even + 2 * (d & 1), n_r - 1 - ((n_r - 1) & 1)))
 
     at = HALO_AT
 
@@ -897,16 +908,15 @@
     project(left_mat, right_mat, tables, 2, cs, rows, keep)
     pair = common[0:2]
 
-    def fill(s, _):
+    def fill(s):
         payload[s] = pair
-        return 0
-
-    lax.fori_loop(0, n_r * n_c, fill, 0)
+
+    laps(n_r * n_c, fill, 8 * SUB)
 
 
 def last_body(
     n_r, n_c, spread, recv, fed, new, driven, fields, weights, columns, first, second, carriers, below_gens,
-    forward, currents, amps,
+    forward, currents, amps, kept,
 ):
     rows = fields.shape[1]
     d, c = place_of()
@@ -926,8 +936,9 @@
     def maps(k, f):
         return toeplitz(gens_sum(recv, n_r - 1 - k, n_c, d, c, 1, below)[4 * f : 4 * f + 4], True)
 
-    sweep(n_r, maps, feeds, share, weights, columns, spread, putter(amps), True)
+    sweep(n_r, maps, feeds, share, weights, columns, spread, putter(amps, kept), True)
     at = n_r - 1 - d
+    take_rows(amps, kept, at - (at & 1))
     for tile in range(rows // SUB):
         rows_at = slice(SUB * tile, SUB * (tile + 1))
         for f in range(F):
@@ -949,15 +960,28 @@
     return lax.ppermute(a, axis, first), b
 
 
+def stacked(arrays):
+    rows, cols = arrays[0].shape[1:]
+    total = sum(array.shape[0] for array in arrays)
+    out, at = None, 0
+    for array in arrays:
+        count = array.shape[0]
+        wide_array = jnp.pad(
+            array, ((at, total - at - count), (0, rows - array.shape[1]), (0, cols - array.shape[2]))
+        )
+        out = wide_array if out is None else out + wide_array
+        at += count
+    return out
+
+
 def per_device(n_r, n_c, incident, inverse_diag, previous, heights, neighbours, counts, transmit, angle_weights):
     rows, cols = heights.shape
     patches = rows * cols
     spread = 1.0 / math.sqrt(rows * cols * n_c)
     slots = n_r * n_c
     tall = rows + 2 * SUB
-    fields = jnp.concatenate([previous, heights[None], inverse_diag, incident])
+    fields = stacked([previous, heights[None], inverse_diag, incident, angle_weights, transmit])
     cols_b, cols_a = call(columns_body, [(rows, LANES)] * 2, [VMEM], flops=500_000)(fields)
-    cols_a, cols_b, transmit, angle_weights = lax.optimization_barrier((cols_a, cols_b, transmit, angle_weights))
     cols_a, cols_b = swap("xr", n_c, cols_a, cols_b)
     tables, gens = call(
         functools.partial(tables_body, n_r),
@@ -965,10 +989,9 @@
         [VMEM],
         [pltpu.VMEM((16 * SUB, patches), f32), pltpu.VMEM((16 * SUB, patches), f32)],
     )(fields)
-    params = jnp.concatenate([angle_weights.reshape(2 * F, Q), transmit.reshape(F, Q)])
     weights, share, columns = call(
         params_body, [(2 * F, LANES), (1, LANES), (2 * F, Q, LANES)], [VMEM], flops=500_000
-    )(params)
+    )(fields)
     gens, weights, share, columns = lax.optimization_barrier((gens, weights, share, columns))
     rows_b, rows_a = call(rows_body, [(ROWS_SENT, LANES)] * 2, [VMEM] * 4, flops=500_000)(fields, gens, cols_b, cols_a)
     rows_a, rows_b, neighbours, counts = lax.optimization_barrier((rows_a, rows_b, neighbours, counts))
@@ -1018,6 +1041,7 @@
             pltpu.VMEM((MERGED, Q // SUB - 1, *tile), f32),
             pltpu.VMEM((MERGED, F, *tile), f32),
             pltpu.VMEM((n_r, F, 2 * Q, LANES), f32),
+            pltpu.VMEM(((n_r + 1) // 2, F, SUB, LANES), f32),
             pltpu.VMEM((2 * F + 1, tall, LANES), f32),
             pltpu.VMEM((2 * F, tall, LANES), f32),
             pltpu.VMEM((2 * F * (2 * H + 1), tall, LANES), f32),
@@ -1035,7 +1059,7 @@
         functools.partial(last_body, n_r, n_c, spread),
         [(2 * F, rows, LANES), (2 * F, rows, LANES)],
         [VMEM] * 11,
-        [pltpu.VMEM((n_r, F, 2 * Q, LANES), f32)],
+        [pltpu.VMEM((n_r, F, 2 * Q, LANES), f32), pltpu.VMEM(((n_r + 1) // 2, F, SUB, LANES), f32)],
     )(recv, fed, new, driven, fields, weights, columns, back_first, second, back_carriers, below_gens)
 
 

time: 47 us -> 45.8 us (0.974)
  Pallas kernels: 10.5 us -> 9.65 us
  other arithmetic: 2.48 us -> 1.81 us
    concatenate x2 -> x0, other arithmetic: 1.52 us -> none  [the longest x1 0.82 us: per_device(): fields = jnp.concatenate([previous, heights[None], inverse_diag, incident])]
    add x0 -> x1, other arithmetic: none -> 0.85 us  [stacked(): out = wide_array if out is None else out + wide_array]
    pallas_call x1, Pallas kernels: 3.61 us -> 3.02 us  [per_device(): call(functools.partial(new_body, n_r, n_c, spread), [(2 * F, rows, LANES)...]
  transfers between devices with their start and end apart: 4 -> 4, of which waited for: 0 -> 0; matrix products, arithmetic and copies ran while one was open for 4% -> 2% of each run, Pallas kernels for 7% -> 7%
where the time goes in v4:
time: 45.8 us; the launch traced here: 45.5 us
  blocking collectives  23.2 us (51%)
  starting transfers between devices  10.1 us (22%)
  Pallas kernels  9.65 us (21%)
  other arithmetic  1.81 us (4%)
  between operations  0.73 us (2%)
    all_to_all x1, blocking collectives, per_device(): recv = lax.all_to_all(payload, BOTH, 0, 0)  13.3 us
    all_to_all x1, blocking collectives, per_device(): fed = lax.all_to_all(payload, BOTH, 0, 0)  9.83 us
    ppermute x2, starting transfers between devices, swap(): return (lax.ppermute(a, axis, first), b)  8.83 us
    pallas_call x1, Pallas kernels, per_device(): call(functools.partial(new_body, n_r, n_c, spread), [(2 * F, rows, LANES)...  3.02 us
    pallas_call x1, Pallas kernels, per_device(): call(functools.partial(last_body, n_r, n_c, spread), [(2 * F, rows, LANES...  2.34 us
    pallas_call x1, Pallas kernels, per_device(): call(functools.partial(tables_body, n_r), [(6, rows, SUB, LANES), (2 * SU...  1.7 us
    ppermute x2, starting transfers between devices, swap(): b = lax.ppermute(b, axis, second)  1.32 us
    pallas_call x1, Pallas kernels, per_device(): call(inner_body, [(4 * OFFSETS, rows, LANES), (2 * F, rows, LANES), jax.S...  1.13 us
  transfers between devices with their start and end apart: 4, of which 0 were waited for; matrix products, arithmetic and copies ran while one was open for 2% of the time, Pallas kernels for 7%

profile of v4, /device:TPU:0, one launch (start us, length us, event | category | flops | bytes accessed | tf_op | source)
XLA Modules:
  0.0 45.5 jit_solution(3517406262616162996)
XLA Ops:
  0.6 0.8 %pad_add_fusion.1.fields = f32[16,16,128]{2,1,0:T(8,128)S(1)} fusion(f32[1,2,64]{2,1,0:T(2,128)} %param.14, f32[2,2,64]{2,1,0:T(2,128)} %param.15, f32[4,16,128]{2,1,0:T(8,128)} %param.8, f32[4,16,128]{2,1,0:T(8,128)} %param.9, f32[1,16,128]{2,1,0:T(8,128)} %bitcast.3, f32[4,16,128]{2,1,0:T(8,128)} %param.10), kind=kLoop, calls=%fused_computation.1 | loop fusion | flops 163840 | bytes 239104 | tf_op jit(solution)/shard_map/add | solution.py:972
  1.5 0.1 shard_map.97
  1.6 0.7 %collective-permute-start = (f32[16,128]{1,0:T(8,128)S(1)}, f32[16,128]{1,0:T(8,128)S(1)}, u32[]{:S(2)}, u32[]{:S(2)}) collective-permute-start(f32[16,128]{1,0:T(8,128)S(1)} %get-tuple-element.37), channel_id=1, source_target_pairs={{1,2},{2,1},{5,6},{6,5},{9,10},{10,9},{13,14},{14,13},{17,18},{18,... | collective-permute-start | bytes 24584 | tf_op jit(solution)/shard_map/ppermute | solution.py:959
  2.3 5.9 %collective-permute-start.1 = (f32[16,128]{1,0:T(8,128)S(1)}, f32[16,128]{1,0:T(8,128)S(1)}, u32[]{:S(2)}, u32[]{:S(2)}) collective-permute-start(f32[16,128]{1,0:T(8,128)S(1)} %get-tuple-element.38), channel_id=1, source_target_pairs={{0,1},{1,0},{2,3},{3,2},{4,5},{5,4},{6,7},{7,6},{8,9},{9,8},{10,11... | collective-permute-start | bytes 24584 | tf_op jit(solution)/shard_map/ppermute | solution.py:960
  8.2 0.3 shard_map.96
  8.4 1.7 %shard_map.95 = (f32[6,16,8,128]{3,2,1,0:T(8,128)S(1)}, f32[16,128]{1,0:T(8,128)S(1)}) custom-call(f32[16,16,128]{2,1,0:T(8,128)S(1)} %pad_add_fusion.1.fields), custom_call_target="tpu_custom_call" | custom-call | flops 2000000 | bytes 1048576 | tf_op jit(solution)/shard_map/pallas_call | solution.py:986
  10.1 0.0 collective-permute-done.recv_b.cols_b
  10.2 0.0 collective-permute-done.1.recv_a.cols_a
  10.2 0.7 %collective-permute-start.2 = (f32[48,128]{1,0:T(8,128)S(1)}, f32[48,128]{1,0:T(8,128)S(1)}, u32[]{:S(2)}, u32[]{:S(2)}) collective-permute-start(f32[48,128]{1,0:T(8,128)S(1)} %get-tuple-element.46), channel_id=1, source_target_pairs={{4,8},{12,16},{20,24},{8,4},{16,12},{24,20},{5,9},{13,17},{21,25},... | collective-permute-start | bytes 73736 | tf_op jit(solution)/shard_map/ppermute | solution.py:959
  10.9 2.9 %collective-permute-start.3 = (f32[48,128]{1,0:T(8,128)S(1)}, f32[48,128]{1,0:T(8,128)S(1)}, u32[]{:S(2)}, u32[]{:S(2)}) collective-permute-start(f32[48,128]{1,0:T(8,128)S(1)} %get-tuple-element.47), channel_id=1, source_target_pairs={{0,4},{4,0},{8,12},{12,8},{16,20},{20,16},{24,28},{28,24},{1,5},{5... | collective-permute-start | bytes 73736 | tf_op jit(solution)/shard_map/ppermute | solution.py:960
  13.8 1.0 %pad_add_fusion.lists = s32[25,16,128]{2,1,0:T(8,128)S(1)} fusion(s32[1,16,128]{2,1,0:T(8,128)} %bitcast.2, s32[24,16,128]{2,1,0:T(8,128)} %param.12), kind=kLoop, calls=%fused_computation | loop fusion | flops 51200 | bytes 409600 | tf_op jit(solution)/shard_map/concatenate | solution.py:999
  14.7 1.1 %shard_map.99 = (f32[192,16,128]{2,1,0:T(8,128)S(1)}, f32[4,16,128]{2,1,0:T(8,128)S(1)}, s32[2,16,128]{2,1,0:T(8,128)S(1)}) custom-call(f32[16,16,128]{2,1,0:T(8,128)S(1)} %pad_add_fusion.1.fields, s32[25,16,128]{2,1,0:T(8,128)S(1)} %pad_add_fusion.lists, f32[16,128]{1,0:T(8,128)S(1)} %collective-permute-done.recv_b.cols_b, ...), custom_call_target="tpu_custom_call" | custom-call | flops 500000 | bytes 1048576 | tf_op jit(solution)/shard_map/pallas_call | solution.py:1000
  15.9 0.0 collective-permute-done.2.rows_b
  15.9 0.0 collective-permute-done.3.rows_a
  15.9 1.1 %shard_map.100 = (f32[32,16,128]{2,1,0:T(8,128)S(1)}, f32[28,16,128]{2,1,0:T(8,128)S(1)}, f32[4,16,128]{2,1,0:T(8,128)S(1)}) custom-call(f32[16,16,128]{2,1,0:T(8,128)S(1)} %pad_add_fusion.1.fields, s32[2,16,128]{2,1,0:T(8,128)S(1)} %get-tuple-element.43.bits, f32[4,16,128]{2,1,0:T(8,128)S(1)} %get-tuple-element.44.inner_near, ...), custom_call_target="tpu_custom_call" | custom-call | flops 2000000 | bytes 1048576 | tf_op jit(solution)/shard_map/pallas_call | solution.py:1012
  17.0 13.3 %all_to_all.10.recv = f32[32,16,128]{2,1,0:T(8,128)S(1)} all-to-all(f32[32,16,128]{2,1,0:T(8,128)S(1)} %get-tuple-element.49), channel_id=1, replica_groups=mesh['rng'=8,'xr'=4] {'rng','xr'}, dimensions={0} | all-to-all | bytes 524288 | tf_op jit(solution)/shard_map/all_to_all | solution.py:1025
  30.3 3.0 %shard_map.101 = (f32[4,16,128]{2,1,0:T(8,128)S(1)}, f32[4,16,128]{2,1,0:T(8,128)S(1)}, f32[32,2,128]{2,1,0:T(2,128)S(1)}, f32[5,7,2,8,128]{4,3,2,1,0:T(8,128)S(...) custom-call(f32[32,16,128]{2,1,0:T(8,128)S(1)} %all_to_all.10.recv, ...), custom_call_target="tpu_custom_call" | custom-call | flops 2000000 | bytes 1048576 | tf_op jit(solution)/shard_map/pallas_call | solution.py:1027
  33.3 9.8 %all_to_all.11.fed = f32[32,2,128]{2,1,0:T(2,128)S(1)} all-to-all(f32[32,2,128]{2,1,0:T(2,128)S(1)} %get-tuple-element.55), channel_id=1, replica_groups=mesh['rng'=8,'xr'=4] {'rng','xr'}, dimensions={0} | all-to-all | bytes 65536 | tf_op jit(solution)/shard_map/all_to_all | solution.py:1057
  43.2 2.3 %shard_map.102 = (f32[4,16,128]{2,1,0:T(8,128)}, f32[4,16,128]{2,1,0:T(8,128)}) custom-call(f32[32,16,128]{2,1,0:T(8,128)S(1)} %all_to_all.10.recv, f32[32,2,128]{2,1,0:T(2,128)S(1)} %all_to_all.11.fed, f32[4,16,128]{2,1,0:T(8,128)S(1)} %get-tuple-element.56.new, f32[4,16,128]{2,1,0:T(8,128)S(1)} %get-tuple-element.57.driven, ...), custom_call_target="tpu_custom_call" | custom-call | flops 2000000 | bytes 1048576 | tf_op jit(solution)/shard_map/pallas_call | solution.py:1058
  (1 shorter events, 0.0 us)
Async XLA Ops:
  1.6 8.6 %collective-permute-start = (f32[16,128]{1,0:T(8,128)S(1)}, f32[16,128]{1,0:T(8,128)S(1)}, u32[]{:S(2)}, u32[]{:S(2)}) collective-permute-start(f32[16,128]{1,0:T(8,128)S(1)} %get-tuple-element.37), channel_id=1, source_target_pairs={{1,2},{2,1},{5,6},{6,5},{9,10},{10,9},{13,14},{14,13},{17,18},{18,... | collective-permute-start | bytes 24584 | tf_op jit(solution)/shard_map/ppermute | solution.py:959
  2.3 7.9 %collective-permute-start.1 = (f32[16,128]{1,0:T(8,128)S(1)}, f32[16,128]{1,0:T(8,128)S(1)}, u32[]{:S(2)}, u32[]{:S(2)}) collective-permute-start(f32[16,128]{1,0:T(8,128)S(1)} %get-tuple-element.38), channel_id=1, source_target_pairs={{0,1},{1,0},{2,3},{3,2},{4,5},{5,4},{6,7},{7,6},{8,9},{9,8},{10,11... | collective-permute-start | bytes 24584 | tf_op jit(solution)/shard_map/ppermute | solution.py:960
  10.2 5.7 %collective-permute-start.2 = (f32[48,128]{1,0:T(8,128)S(1)}, f32[48,128]{1,0:T(8,128)S(1)}, u32[]{:S(2)}, u32[]{:S(2)}) collective-permute-start(f32[48,128]{1,0:T(8,128)S(1)} %get-tuple-element.46), channel_id=1, source_target_pairs={{4,8},{12,16},{20,24},{8,4},{16,12},{24,20},{5,9},{13,17},{21,25},... | collective-permute-start | bytes 73736 | tf_op jit(solution)/shard_map/ppermute | solution.py:959
  10.9 5.0 %collective-permute-start.3 = (f32[48,128]{1,0:T(8,128)S(1)}, f32[48,128]{1,0:T(8,128)S(1)}, u32[]{:S(2)}, u32[]{:S(2)}) collective-permute-start(f32[48,128]{1,0:T(8,128)S(1)} %get-tuple-element.47), channel_id=1, source_target_pairs={{0,4},{4,0},{8,12},{12,8},{16,20},{20,16},{24,28},{28,24},{1,5},{5... | collective-permute-start | bytes 73736 | tf_op jit(solution)/shard_map/ppermute | solution.py:960

commit v5 on v4

--- a/solution.py
+++ b/solution.py
@@ -72,7 +72,7 @@
 PLAIN = pl.BlockSpec()
 
 
-def call(body, out, ins, scratch=(), flops=2_000_000):
+def call(body, out, ins, scratch=(), flops=2_000_000_000):
     return pl.pallas_call(
         body,
         out_shape=tuple(jax.ShapeDtypeStruct(s, f32) if isinstance(s, tuple) else s for s in out),
@@ -199,14 +199,14 @@
                     gens[at : at + 1] = row
 
 
-def list_bits(lists):
-    count = lists[LMAX]
+def list_bits(neighbours, counts):
+    count = counts[...]
     low = jnp.zeros(count.shape, jnp.int32)
     high = jnp.zeros(count.shape, jnp.int32)
     half = OFFSETS // 2
     one = jnp.ones(count.shape, jnp.int32)
     for slot in range(LMAX):
-        code = lists[slot]
+        code = neighbours[slot]
         live = count > slot
         is_low = code < half
         bit = lax.shift_left(one, jnp.where(is_low, code, code - half))
@@ -379,9 +379,9 @@
         moved[k * SHIFTS + dy + H, TOP : TOP + rows] = shifted(middle, side, dy)
 
 
-def inner_body(fields, lists, cols_b, cols_a, green, near_out, bits, moved):
+def inner_body(fields, neighbours, counts, cols_b, cols_a, green, near_out, bits, moved):
     rows = fields.shape[1]
-    low, high = list_bits(lists)
+    low, high = list_bits(neighbours, counts)
     bits[0] = low
     bits[1] = high
     from_left, from_right = side_columns(cols_a, cols_b)
@@ -747,7 +747,7 @@
 
 
 def store_waves(
-    fields, cols_a, cols_b, above, below, loss, first, second, carriers, back_first, back_carriers, inner, edge_l, edge_r
+    fields, cols_a, cols_b, above, below, loss, first, second, carriers, back_first, back_carriers, back_plain, inner, edge_l, edge_r
 ):
     rows = fields.shape[1]
     ks = range(2 * F, N_FIELDS)
@@ -765,35 +765,47 @@
     for t, (x, y) in enumerate(merged_places(rows)):
         h = tiles[0][t]
         keep(first, t, powers(wave(1, x, 0, y, 0.24, h), Q // SUB)[1:])
-        keep(second, t, powers(wave(0, x, 1, y, 0.03, h), SUB)[1:])
-        keep(carriers, t, [carrier(f, 0, x, y, h) for f in range(F)])
+        odd = [cos_sin((y & (2 * PERIOD - 1)).astype(f32) * (0.5 / PERIOD) + (0.015 / TURN) * h)]
+        whole = square(odd[0])
+        for _ in range(SUB // 2 - 1):
+            odd.append(times(odd[-1], whole))
+        keep(second, t, odd)
+        keep(carriers, t, [times(carrier(f, 0, x, y, h), odd[-1]) for f in range(F)])
         if t in (1, 2):
             keep(back_first, t - 1, powers(wave(-1, x, 0, y, 0.24, h), Q // SUB)[1:])
-            keep(back_carriers, t - 1, [carrier(f, 1, x, y, h) for f in range(F)])
-
-
-def radiated(amps, at, f, first, second, carriers, t, t_second):
+            plain = [carrier(f, 1, x, y, h) for f in range(F)]
+            keep(back_plain, t - 1, plain)
+            keep(back_carriers, t - 1, [times(part, odd[-1]) for part in plain])
+
+
+def radiated(amps, at, f, first, second, carriers, tiles, shift):
     splat = lambda a: wide(amps[at, f, a : a + 1])
-    total = None
+    totals = [None] * len(tiles)
     for a1 in range(Q // SUB):
         base = 2 * SUB * a1
-        inner = (splat(base), splat(base + SUB))
-        for a2 in range(1, SUB):
-            u2 = (second[t_second, a2 - 1, 0], second[t_second, a2 - 1, 1])
-            got = times((splat(base + a2), splat(base + SUB + a2)), u2)
-            inner = (inner[0] + got[0], inner[1] + got[1])
-        if a1 == 0:
-            total = inner
-        else:
-            got = times((first[t, a1 - 1, 0], first[t, a1 - 1, 1]), inner)
-            total = (total[0] + got[0], total[1] + got[1])
-    return times((carriers[t, f, 0], carriers[t, f, 1]), total)
+        pairs = []
+        for i in range(SUB // 2):
+            up, low = SUB // 2 + i, SUB // 2 - 1 - i
+            re = splat(base + up), splat(base + low)
+            im = splat(base + SUB + up), splat(base + SUB + low)
+            pairs.append((re[0] + re[1], re[0] - re[1], im[0] + im[1], im[0] - im[1]))
+        for n, t in enumerate(tiles):
+            inner = None
+            for i, (re_sum, re_gap, im_sum, im_gap) in enumerate(pairs):
+                cos, sin = second[t + shift, i, 0], second[t + shift, i, 1]
+                got = (re_sum * cos - im_gap * sin, im_sum * cos + re_gap * sin)
+                inner = got if inner is None else (inner[0] + got[0], inner[1] + got[1])
+            if a1 > 0:
+                got = times((first[t, a1 - 1, 0], first[t, a1 - 1, 1]), inner)
+                inner = (totals[n][0] + got[0], totals[n][1] + got[1])
+            totals[n] = inner
+    return [times((carriers[t, f, 0], carriers[t, f, 1]), total) for t, total in zip(tiles, totals, strict=True)]
 
 
 def new_body(
     n_r, n_c, spread, recv, green, edge_green, source, fields, cols_b, cols_a, rows_b, rows_a, tables, weights, columns,
     forward, driven, payload, second, back_first, back_carriers, below_gens,
-    loss, first, carriers, amps, kept, held, inner, moved, edge_l, edge_r, spill, cs, left_mat, right_mat, common, halo,
+    loss, first, carriers, back_plain, amps, kept, held, inner, moved, edge_l, edge_r, spill, cs, left_mat, right_mat, common, halo,
 ):
     rows = fields.shape[1]
     d, c = place_of()
@@ -802,7 +814,7 @@
     below_gens[...] = below_rows[GENS_AT:]
     store_waves(
         fields, cols_a, cols_b, above_rows, below_rows,
-        loss, first, second, carriers, back_first, back_carriers, held, edge_l, edge_r,
+        loss, first, second, carriers, back_first, back_carriers, back_plain, held, edge_l, edge_r,
     )
 
     if n_r <= SUB:
@@ -852,14 +864,14 @@
 
     weak = {}
     lost = {}
-    for t, step in enumerate((-1, 0, 0, 1, 0)):
+    for step, group in ((-1, (0,)), (0, (1, 2, 4)), (1, (3,))):
         at = jnp.clip(d + step, 0, n_r - 1)
         for f in range(F):
-            w = radiated(amps, at, f, first, second, carriers, t, t)
-            got = times((loss[t, 2 * f], loss[t, 2 * f + 1]), w)
-            for part in range(2):
-                weak[t, 2 * f + part] = w[part]
-                lost[t, 2 * f + part] = got[part]
+            for t, w in zip(group, radiated(amps, at, f, first, second, carriers, group, 0), strict=True):
+                got = times((loss[t, 2 * f], loss[t, 2 * f + 1]), w)
+                for part in range(2):
+                    weak[t, 2 * f + part] = w[part]
+                    lost[t, 2 * f + part] = got[part]
     beyond = []
     for k in range(2 * F):
         tiles = [lost[t, k] for t in range(MERGED)]
@@ -896,7 +908,7 @@
         s = times((fields[2 * F + 1 + 2 * f], fields[2 * F + 2 + 2 * f]), rest)
         driven[2 * f] = s[0]
         driven[2 * f + 1] = s[1]
-        base = [jnp.concatenate([back_carriers[t, f, part] for t in range(2)], axis=0) for part in range(2)]
+        base = [jnp.concatenate([back_plain[t, f, part] for t in range(2)], axis=0) for part in range(2)]
         add = conj_times(base, s)
         cs[2 * f] = add[0]
         cs[2 * f + 1] = add[1]
@@ -939,10 +951,10 @@
     sweep(n_r, maps, feeds, share, weights, columns, spread, putter(amps, kept), True)
     at = n_r - 1 - d
     take_rows(amps, kept, at - (at & 1))
-    for tile in range(rows // SUB):
-        rows_at = slice(SUB * tile, SUB * (tile + 1))
-        for f in range(F):
-            w = radiated(amps, at, f, first, second, carriers, tile, tile + 1)
+    tiles = tuple(range(rows // SUB))
+    for f in range(F):
+        for tile, w in zip(tiles, radiated(amps, at, f, first, second, carriers, tiles, 1), strict=True):
+            rows_at = slice(SUB * tile, SUB * (tile + 1))
             lost = times((fields[2 * F + 1 + 2 * f, rows_at], fields[2 * F + 2 + 2 * f, rows_at]), w)
             currents[2 * f, rows_at] = driven[2 * f, rows_at] - lost[0]
             currents[2 * f + 1, rows_at] = driven[2 * f + 1, rows_at] - lost[1]
@@ -981,7 +993,7 @@
     slots = n_r * n_c
     tall = rows + 2 * SUB
     fields = stacked([previous, heights[None], inverse_diag, incident, angle_weights, transmit])
-    cols_b, cols_a = call(columns_body, [(rows, LANES)] * 2, [VMEM], flops=500_000)(fields)
+    cols_b, cols_a = call(columns_body, [(rows, LANES)] * 2, [VMEM], flops=400_000_000)(fields)
     cols_a, cols_b = swap("xr", n_c, cols_a, cols_b)
     tables, gens = call(
         functools.partial(tables_body, n_r),
@@ -990,13 +1002,11 @@
         [pltpu.VMEM((16 * SUB, patches), f32), pltpu.VMEM((16 * SUB, patches), f32)],
     )(fields)
     weights, share, columns = call(
-        params_body, [(2 * F, LANES), (1, LANES), (2 * F, Q, LANES)], [VMEM], flops=500_000
+        params_body, [(2 * F, LANES), (1, LANES), (2 * F, Q, LANES)], [VMEM], flops=400_000_000
     )(fields)
     gens, weights, share, columns = lax.optimization_barrier((gens, weights, share, columns))
-    rows_b, rows_a = call(rows_body, [(ROWS_SENT, LANES)] * 2, [VMEM] * 4, flops=500_000)(fields, gens, cols_b, cols_a)
-    rows_a, rows_b, neighbours, counts = lax.optimization_barrier((rows_a, rows_b, neighbours, counts))
+    rows_b, rows_a = call(rows_body, [(ROWS_SENT, LANES)] * 2, [VMEM] * 4, flops=400_000_000)(fields, gens, cols_b, cols_a)
     rows_a, rows_b = swap("rng", n_r, rows_a, rows_b)
-    lists = jnp.concatenate([neighbours, counts[None]])
     green, inner_near, bits = call(
         inner_body,
         [
@@ -1004,10 +1014,10 @@
             (2 * F, rows, LANES),
             jax.ShapeDtypeStruct((2, rows, LANES), jnp.int32),
         ],
-        [VMEM] * 4,
+        [VMEM] * 5,
         [pltpu.VMEM(((2 * F + 1) * SHIFTS, tall, LANES), f32)],
-        500_000,
-    )(fields, lists, cols_b, cols_a)
+        400_000_000,
+    )(fields, neighbours, counts, cols_b, cols_a)
     edges = [pltpu.VMEM((tall, LANES), f32)] * 2
     payload, edge_green, source = call(
         functools.partial(near_body, n_r, n_c),
@@ -1030,7 +1040,7 @@
             (2 * F, rows, LANES),
             (2 * F, rows, LANES),
             (slots, 2, LANES),
-            (MERGED, SUB - 1, *tile),
+            (MERGED, SUB // 2, *tile),
             (2, Q // SUB - 1, *tile),
             (2, F, *tile),
             (SUB, LANES),
@@ -1040,6 +1050,7 @@
             pltpu.VMEM((MERGED, 2 * F, SUB, LANES), f32),
             pltpu.VMEM((MERGED, Q // SUB - 1, *tile), f32),
             pltpu.VMEM((MERGED, F, *tile), f32),
+            pltpu.VMEM((2, F, *tile), f32),
             pltpu.VMEM((n_r, F, 2 * Q, LANES), f32),
             pltpu.VMEM(((n_r + 1) // 2, F, SUB, LANES), f32),
             pltpu.VMEM((2 * F + 1, tall, LANES), f32),

time: 45.8 us -> 45.6 us (level)
  other arithmetic: 1.81 us -> 0.85 us
  blocking collectives: 23.2 us -> 24.1 us
    concatenate x1 -> x0, other arithmetic: 0.96 us -> none  [per_device(): lists = jnp.concatenate([neighbours, counts[None]])]
    all_to_all x1, blocking collectives: 13.3 us -> 14.3 us  [per_device(): recv = lax.all_to_all(payload, BOTH, 0, 0)]
  transfers between devices with their start and end apart: 4 -> 4, of which waited for: 0 -> 0; matrix products, arithmetic and copies ran while one was open for 2% -> 0% of each run, Pallas kernels for 7% -> 7%
where the time goes in v5:
time: 45.6 us; the launch traced here: 45.3 us
  blocking collectives  24.1 us (53%)
  starting transfers between devices  10.2 us (22%)
  Pallas kernels  9.45 us (21%)
  other arithmetic  0.85 us (2%)
  between operations  0.74 us (2%)
    all_to_all x1, blocking collectives, per_device(): recv = lax.all_to_all(payload, BOTH, 0, 0)  14.3 us
    all_to_all x1, blocking collectives, per_device(): fed = lax.all_to_all(payload, BOTH, 0, 0)  9.82 us
    ppermute x2, starting transfers between devices, swap(): return (lax.ppermute(a, axis, first), b)  8.83 us
    pallas_call x1, Pallas kernels, per_device(): call(functools.partial(new_body, n_r, n_c, spread), [(2 * F, rows, LANES)...  2.93 us
    pallas_call x1, Pallas kernels, per_device(): call(functools.partial(last_body, n_r, n_c, spread), [(2 * F, rows, LANES...  2.24 us
    pallas_call x1, Pallas kernels, per_device(): call(functools.partial(tables_body, n_r), [(6, rows, SUB, LANES), (2 * SU...  1.69 us
    ppermute x2, starting transfers between devices, swap(): b = lax.ppermute(b, axis, second)  1.32 us
    pallas_call x1, Pallas kernels, per_device(): call(inner_body, [(4 * OFFSETS, rows, LANES), (2 * F, rows, LANES), jax.S...  1.13 us
  transfers between devices with their start and end apart: 4, of which 0 were waited for; matrix products, arithmetic and copies ran while one was open for 0% of the time, Pallas kernels for 7%

profile of v5, /device:TPU:0, one launch (start us, length us, event | category | flops | bytes accessed | tf_op | source)
XLA Modules:
  0.0 45.3 jit_solution(4278538030571564390)
XLA Ops:
  0.6 0.8 %pad_add_fusion.fields = f32[16,16,128]{2,1,0:T(8,128)S(1)} fusion(f32[1,2,64]{2,1,0:T(2,128)} %param.14, f32[2,2,64]{2,1,0:T(2,128)} %param.15, f32[4,16,128]{2,1,0:T(8,128)} %param.8, f32[4,16,128]{2,1,0:T(8,128)} %param.9, f32[1,16,128]{2,1,0:T(8,128)} %bitcast.1, f32[4,16,128]{2,1,0:T(8,128)} %param.10), kind=kLoop, calls=%fused_computation | loop fusion | flops 163840 | bytes 239104 | tf_op jit(solution)/shard_map/add | solution.py:984
  1.5 0.1 shard_map.95
  1.6 0.7 %collective-permute-start = (f32[16,128]{1,0:T(8,128)S(1)}, f32[16,128]{1,0:T(8,128)S(1)}, u32[]{:S(2)}, u32[]{:S(2)}) collective-permute-start(f32[16,128]{1,0:T(8,128)S(1)} %get-tuple-element.28), channel_id=1, source_target_pairs={{1,2},{2,1},{5,6},{6,5},{9,10},{10,9},{13,14},{14,13},{17,18},{18,... | collective-permute-start | bytes 24584 | tf_op jit(solution)/shard_map/ppermute | solution.py:971
  2.3 5.9 %collective-permute-start.1 = (f32[16,128]{1,0:T(8,128)S(1)}, f32[16,128]{1,0:T(8,128)S(1)}, u32[]{:S(2)}, u32[]{:S(2)}) collective-permute-start(f32[16,128]{1,0:T(8,128)S(1)} %get-tuple-element.29), channel_id=1, source_target_pairs={{0,1},{1,0},{2,3},{3,2},{4,5},{5,4},{6,7},{7,6},{8,9},{9,8},{10,11... | collective-permute-start | bytes 24584 | tf_op jit(solution)/shard_map/ppermute | solution.py:972
  8.2 1.7 %shard_map.97 = (f32[6,16,8,128]{3,2,1,0:T(8,128)S(1)}, f32[16,128]{1,0:T(8,128)S(1)}) custom-call(f32[16,16,128]{2,1,0:T(8,128)S(1)} %pad_add_fusion.fields), custom_call_target="tpu_custom_call" | custom-call | flops 2000000000 | bytes 1048576 | tf_op jit(solution)/shard_map/pallas_call | solution.py:998
  9.9 0.0 copy-start
  9.9 0.0 copy-start.1
  9.9 0.3 shard_map.98
  10.2 0.0 collective-permute-done.cols_b.recv_b
  10.2 0.0 collective-permute-done.1.cols_a.recv_a
  10.2 0.7 %collective-permute-start.2 = (f32[48,128]{1,0:T(8,128)S(1)}, f32[48,128]{1,0:T(8,128)S(1)}, u32[]{:S(2)}, u32[]{:S(2)}) collective-permute-start(f32[48,128]{1,0:T(8,128)S(1)} %get-tuple-element.38), channel_id=1, source_target_pairs={{4,8},{12,16},{20,24},{8,4},{16,12},{24,20},{5,9},{13,17},{21,25},... | collective-permute-start | bytes 73736 | tf_op jit(solution)/shard_map/ppermute | solution.py:971
  10.9 2.9 %collective-permute-start.3 = (f32[48,128]{1,0:T(8,128)S(1)}, f32[48,128]{1,0:T(8,128)S(1)}, u32[]{:S(2)}, u32[]{:S(2)}) collective-permute-start(f32[48,128]{1,0:T(8,128)S(1)} %get-tuple-element.39), channel_id=1, source_target_pairs={{0,4},{4,0},{8,12},{12,8},{16,20},{20,16},{24,28},{28,24},{1,5},{5... | collective-permute-start | bytes 73736 | tf_op jit(solution)/shard_map/ppermute | solution.py:972
  13.8 0.0 copy-done
  13.8 0.0 copy-done.1
  13.8 1.1 %shard_map.96 = (f32[192,16,128]{2,1,0:T(8,128)S(1)}, f32[4,16,128]{2,1,0:T(8,128)S(1)}, s32[2,16,128]{2,1,0:T(8,128)S(1)}) custom-call(f32[16,16,128]{2,1,0:T(8,128)S(1)} %pad_add_fusion.fields, s32[24,16,128]{2,1,0:T(8,128)S(1)} %copy-done, s32[16,128]{1,0:T(8,128)S(1)} %copy-done.1, f32[16,128]{1,0:T(8,128)S(1)} %collective-permute-done.cols_b.recv_b, ...), custom_call_target="tpu_custom_call" | custom-call | flops 400000000 | bytes 1048576 | tf_op jit(solution)/shard_map/pallas_call | solution.py:1010
  15.0 0.0 collective-permute-done.2.rows_b
  15.0 0.0 collective-permute-done.3.rows_a
  15.0 1.1 %shard_map.100 = (f32[32,16,128]{2,1,0:T(8,128)S(1)}, f32[28,16,128]{2,1,0:T(8,128)S(1)}, f32[4,16,128]{2,1,0:T(8,128)S(1)}) custom-call(f32[16,16,128]{2,1,0:T(8,128)S(1)} %pad_add_fusion.fields, s32[2,16,128]{2,1,0:T(8,128)S(1)} %get-tuple-element.30.bits, f32[4,16,128]{2,1,0:T(8,128)S(1)} %get-tuple-element.31.inner_near, ...), custom_call_target="tpu_custom_call" | custom-call | flops 2000000000 | bytes 1048576 | tf_op jit(solution)/shard_map/pallas_call | solution.py:1022
  16.0 14.3 %all_to_all.10.recv = f32[32,16,128]{2,1,0:T(8,128)S(1)} all-to-all(f32[32,16,128]{2,1,0:T(8,128)S(1)} %get-tuple-element.41), channel_id=1, replica_groups=mesh['rng'=8,'xr'=4] {'rng','xr'}, dimensions={0} | all-to-all | bytes 524288 | tf_op jit(solution)/shard_map/all_to_all | solution.py:1035
  30.3 2.9 %shard_map.101 = (f32[4,16,128]{2,1,0:T(8,128)S(1)}, f32[4,16,128]{2,1,0:T(8,128)S(1)}, f32[32,2,128]{2,1,0:T(2,128)S(1)}, f32[5,4,2,8,128]{4,3,2,1,0:T(8,128)S(...) custom-call(f32[32,16,128]{2,1,0:T(8,128)S(1)} %all_to_all.10.recv, ...), custom_call_target="tpu_custom_call" | custom-call | flops 2000000000 | bytes 1048576 | tf_op jit(solution)/shard_map/pallas_call | solution.py:1037
  33.3 9.8 %all_to_all.11.fed = f32[32,2,128]{2,1,0:T(2,128)S(1)} all-to-all(f32[32,2,128]{2,1,0:T(2,128)S(1)} %get-tuple-element.47), channel_id=1, replica_groups=mesh['rng'=8,'xr'=4] {'rng','xr'}, dimensions={0} | all-to-all | bytes 65536 | tf_op jit(solution)/shard_map/all_to_all | solution.py:1068
  43.1 2.2 %shard_map.102 = (f32[4,16,128]{2,1,0:T(8,128)}, f32[4,16,128]{2,1,0:T(8,128)}) custom-call(f32[32,16,128]{2,1,0:T(8,128)S(1)} %all_to_all.10.recv, f32[32,2,128]{2,1,0:T(2,128)S(1)} %all_to_all.11.fed, f32[4,16,128]{2,1,0:T(8,128)S(1)} %get-tuple-element.48.new, f32[4,16,128]{2,1,0:T(8,128)S(1)} %get-tuple-element.49.driven, ...), custom_call_target="tpu_custom_call" | custom-call | flops 2000000000 | bytes 1048576 | tf_op jit(solution)/shard_map/pallas_call | solution.py:1069
  (1 shorter events, 0.0 us)
Async XLA Ops:
  1.6 8.6 %collective-permute-start = (f32[16,128]{1,0:T(8,128)S(1)}, f32[16,128]{1,0:T(8,128)S(1)}, u32[]{:S(2)}, u32[]{:S(2)}) collective-permute-start(f32[16,128]{1,0:T(8,128)S(1)} %get-tuple-element.28), channel_id=1, source_target_pairs={{1,2},{2,1},{5,6},{6,5},{9,10},{10,9},{13,14},{14,13},{17,18},{18,... | collective-permute-start | bytes 24584 | tf_op jit(solution)/shard_map/ppermute | solution.py:971
  2.3 7.9 %collective-permute-start.1 = (f32[16,128]{1,0:T(8,128)S(1)}, f32[16,128]{1,0:T(8,128)S(1)}, u32[]{:S(2)}, u32[]{:S(2)}) collective-permute-start(f32[16,128]{1,0:T(8,128)S(1)} %get-tuple-element.29), channel_id=1, source_target_pairs={{0,1},{1,0},{2,3},{3,2},{4,5},{5,4},{6,7},{7,6},{8,9},{9,8},{10,11... | collective-permute-start | bytes 24584 | tf_op jit(solution)/shard_map/ppermute | solution.py:972
  9.9 3.9 %copy-start = (s32[24,16,128]{2,1,0:T(8,128)S(1)}, s32[24,16,128]{2,1,0:T(8,128)}, u32[]{:S(2)}) copy-start(s32[24,16,128]{2,1,0:T(8,128)} %neighbours.1) | copy-start | bytes 589828
  9.9 3.9 %copy-start.1 = (s32[16,128]{1,0:T(8,128)S(1)}, s32[16,128]{1,0:T(8,128)}, u32[]{:S(2)}) copy-start(s32[16,128]{1,0:T(8,128)} %counts.1) | copy-start | bytes 24580
  10.2 4.7 %collective-permute-start.2 = (f32[48,128]{1,0:T(8,128)S(1)}, f32[48,128]{1,0:T(8,128)S(1)}, u32[]{:S(2)}, u32[]{:S(2)}) collective-permute-start(f32[48,128]{1,0:T(8,128)S(1)} %get-tuple-element.38), channel_id=1, source_target_pairs={{4,8},{12,16},{20,24},{8,4},{16,12},{24,20},{5,9},{13,17},{21,25},... | collective-permute-start | bytes 73736 | tf_op jit(solution)/shard_map/ppermute | solution.py:971
  10.9 4.1 %collective-permute-start.3 = (f32[48,128]{1,0:T(8,128)S(1)}, f32[48,128]{1,0:T(8,128)S(1)}, u32[]{:S(2)}, u32[]{:S(2)}) collective-permute-start(f32[48,128]{1,0:T(8,128)S(1)} %get-tuple-element.39), channel_id=1, source_target_pairs={{0,4},{4,0},{8,12},{12,8},{16,20},{20,16},{24,28},{28,24},{1,5},{5... | collective-permute-start | bytes 73736 | tf_op jit(solution)/shard_map/ppermute | solution.py:972

commit v6 on v5

--- a/solution.py
+++ b/solution.py
@@ -175,10 +175,10 @@
                 base = (direction * F + f) * 4 * SUB
                 left_mat[base : base + 2 * SUB, lanes] = zr * c1 - zi * s1
                 left_mat[base + 2 * SUB : base + 4 * SUB, lanes] = zr * s1 + zi * c1
-    right_mat[4 * SUB :] = jnp.zeros((right_mat.shape[0] - 4 * SUB, right_mat.shape[1]), f32)
     both = lax.dot_general(
         left_mat[...], right_mat[...], (((1,), (1,)), ((), ())), precision=HIGHEST, preferred_element_type=f32
     )
+    both = jnp.concatenate([both, jnp.zeros((16 * SUB, LANES - 4 * SUB), f32)], axis=1)
     lane = iota((SUB, LANES), 1)
     for direction in range(2):
         for f in range(F):
@@ -250,6 +250,7 @@
     sums = lax.dot_general(
         left_mat[0 : 4 * SUB], right_mat[...], (((1,), (1,)), ((), ())), precision=HIGHEST, preferred_element_type=f32
     )
+    sums = jnp.concatenate([sums, jnp.zeros((4 * SUB, LANES - 2 * SUB), f32)], axis=1)
     lane = iota((SUB, LANES), 1)
     for f in range(F):
         gr = sums[2 * f * SUB : (2 * f + 1) * SUB]
@@ -474,7 +475,6 @@
     def keep(f, row):
         common[2 * SUB + f : 2 * SUB + f + 1] = row
 
-    right_mat[2 * SUB :] = jnp.zeros((right_mat.shape[0] - 2 * SUB, right_mat.shape[1]), f32)
     common[2 * SUB :] = jnp.zeros((SUB, LANES), f32)
     project(left_mat, right_mat, tables, 0, cs, rows, keep)
     common[0 : 2 * SUB] = gens[...]
@@ -916,7 +916,6 @@
     def keep(f, row):
         common[f : f + 1] = row
 
-    right_mat[2 * SUB :] = jnp.zeros((right_mat.shape[0] - 2 * SUB, right_mat.shape[1]), f32)
     project(left_mat, right_mat, tables, 2, cs, rows, keep)
     pair = common[0:2]
 
@@ -999,7 +998,7 @@
         functools.partial(tables_body, n_r),
         [(6, rows, SUB, LANES), (2 * SUB, LANES)],
         [VMEM],
-        [pltpu.VMEM((16 * SUB, patches), f32), pltpu.VMEM((16 * SUB, patches), f32)],
+        [pltpu.VMEM((16 * SUB, patches), f32), pltpu.VMEM((4 * SUB, patches), f32)],
     )(fields)
     weights, share, columns = call(
         params_body, [(2 * F, LANES), (1, LANES), (2 * F, Q, LANES)], [VMEM], flops=400_000_000
@@ -1027,7 +1026,7 @@
             pltpu.VMEM((2 * F, rows, LANES), f32),
             pltpu.VMEM((2 * F, rows, LANES), f32),
             pltpu.VMEM((4 * SUB, patches), f32),
-            pltpu.VMEM((16 * SUB, patches), f32),
+            pltpu.VMEM((2 * SUB, patches), f32),
             pltpu.VMEM((3 * SUB, LANES), f32),
             pltpu.VMEM((2 * SUB, LANES), f32),
         ],
@@ -1060,7 +1059,7 @@
             pltpu.VMEM((2 * F, rows, LANES), f32),
             pltpu.VMEM((2 * F, rows, LANES), f32),
             pltpu.VMEM((4 * SUB, patches), f32),
-            pltpu.VMEM((16 * SUB, patches), f32),
+            pltpu.VMEM((2 * SUB, patches), f32),
             pltpu.VMEM((SUB, LANES), f32),
             pltpu.VMEM((2, 2 * SUB, LANES), f32),
         ],

time: 45.6 us -> 45.6 us (level)
  no operation moved by 1% of the time
where the time goes in v6:
time: 45.6 us; the launch traced here: 45.3 us
  blocking collectives  24.1 us (53%)
  starting transfers between devices  10.2 us (22%)
  Pallas kernels  9.45 us (21%)
  other arithmetic  0.85 us (2%)
  between operations  0.74 us (2%)
    all_to_all x1, blocking collectives, per_device(): recv = lax.all_to_all(payload, BOTH, 0, 0)  14.3 us
    all_to_all x1, blocking collectives, per_device(): fed = lax.all_to_all(payload, BOTH, 0, 0)  9.82 us
    ppermute x2, starting transfers between devices, swap(): return (lax.ppermute(a, axis, first), b)  8.83 us
    pallas_call x1, Pallas kernels, per_device(): call(functools.partial(new_body, n_r, n_c, spread), [(2 * F, rows, LANES)...  2.93 us
    pallas_call x1, Pallas kernels, per_device(): call(functools.partial(last_body, n_r, n_c, spread), [(2 * F, rows, LANES...  2.24 us
    pallas_call x1, Pallas kernels, per_device(): call(functools.partial(tables_body, n_r), [(6, rows, SUB, LANES), (2 * SU...  1.69 us
    ppermute x2, starting transfers between devices, swap(): b = lax.ppermute(b, axis, second)  1.32 us
    pallas_call x1, Pallas kernels, per_device(): call(inner_body, [(4 * OFFSETS, rows, LANES), (2 * F, rows, LANES), jax.S...  1.13 us
  transfers between devices with their start and end apart: 4, of which 0 were waited for; matrix products, arithmetic and copies ran while one was open for 0% of the time, Pallas kernels for 7%

profile of v6, /device:TPU:0, one launch (start us, length us, event | category | flops | bytes accessed | tf_op | source)
XLA Modules:
  0.0 45.3 jit_solution(8880930205154055398)
XLA Ops:
  0.6 0.8 %pad_add_fusion.fields = f32[16,16,128]{2,1,0:T(8,128)S(1)} fusion(f32[1,2,64]{2,1,0:T(2,128)} %param.14, f32[2,2,64]{2,1,0:T(2,128)} %param.15, f32[4,16,128]{2,1,0:T(8,128)} %param.8, f32[4,16,128]{2,1,0:T(8,128)} %param.9, f32[1,16,128]{2,1,0:T(8,128)} %bitcast.1, f32[4,16,128]{2,1,0:T(8,128)} %param.10), kind=kLoop, calls=%fused_computation | loop fusion | flops 163840 | bytes 239104 | tf_op jit(solution)/shard_map/add | solution.py:983
  1.5 0.1 shard_map.95
  1.6 0.7 %collective-permute-start = (f32[16,128]{1,0:T(8,128)S(1)}, f32[16,128]{1,0:T(8,128)S(1)}, u32[]{:S(2)}, u32[]{:S(2)}) collective-permute-start(f32[16,128]{1,0:T(8,128)S(1)} %get-tuple-element.28), channel_id=1, source_target_pairs={{1,2},{2,1},{5,6},{6,5},{9,10},{10,9},{13,14},{14,13},{17,18},{18,... | collective-permute-start | bytes 24584 | tf_op jit(solution)/shard_map/ppermute | solution.py:970
  2.3 5.9 %collective-permute-start.1 = (f32[16,128]{1,0:T(8,128)S(1)}, f32[16,128]{1,0:T(8,128)S(1)}, u32[]{:S(2)}, u32[]{:S(2)}) collective-permute-start(f32[16,128]{1,0:T(8,128)S(1)} %get-tuple-element.29), channel_id=1, source_target_pairs={{0,1},{1,0},{2,3},{3,2},{4,5},{5,4},{6,7},{7,6},{8,9},{9,8},{10,11... | collective-permute-start | bytes 24584 | tf_op jit(solution)/shard_map/ppermute | solution.py:971
  8.2 1.7 %shard_map.97 = (f32[6,16,8,128]{3,2,1,0:T(8,128)S(1)}, f32[16,128]{1,0:T(8,128)S(1)}) custom-call(f32[16,16,128]{2,1,0:T(8,128)S(1)} %pad_add_fusion.fields), custom_call_target="tpu_custom_call" | custom-call | flops 2000000000 | bytes 1048576 | tf_op jit(solution)/shard_map/pallas_call | solution.py:997
  9.9 0.0 copy-start
  9.9 0.0 copy-start.1
  9.9 0.3 shard_map.98
  10.2 0.0 collective-permute-done.cols_b.recv_b
  10.2 0.0 collective-permute-done.1.cols_a.recv_a
  10.2 0.7 %collective-permute-start.2 = (f32[48,128]{1,0:T(8,128)S(1)}, f32[48,128]{1,0:T(8,128)S(1)}, u32[]{:S(2)}, u32[]{:S(2)}) collective-permute-start(f32[48,128]{1,0:T(8,128)S(1)} %get-tuple-element.38), channel_id=1, source_target_pairs={{4,8},{12,16},{20,24},{8,4},{16,12},{24,20},{5,9},{13,17},{21,25},... | collective-permute-start | bytes 73736 | tf_op jit(solution)/shard_map/ppermute | solution.py:970
  10.9 2.9 %collective-permute-start.3 = (f32[48,128]{1,0:T(8,128)S(1)}, f32[48,128]{1,0:T(8,128)S(1)}, u32[]{:S(2)}, u32[]{:S(2)}) collective-permute-start(f32[48,128]{1,0:T(8,128)S(1)} %get-tuple-element.39), channel_id=1, source_target_pairs={{0,4},{4,0},{8,12},{12,8},{16,20},{20,16},{24,28},{28,24},{1,5},{5... | collective-permute-start | bytes 73736 | tf_op jit(solution)/shard_map/ppermute | solution.py:971
  13.8 0.0 copy-done
  13.8 0.0 copy-done.1
  13.8 1.1 %shard_map.96 = (f32[192,16,128]{2,1,0:T(8,128)S(1)}, f32[4,16,128]{2,1,0:T(8,128)S(1)}, s32[2,16,128]{2,1,0:T(8,128)S(1)}) custom-call(f32[16,16,128]{2,1,0:T(8,128)S(1)} %pad_add_fusion.fields, s32[24,16,128]{2,1,0:T(8,128)S(1)} %copy-done, s32[16,128]{1,0:T(8,128)S(1)} %copy-done.1, f32[16,128]{1,0:T(8,128)S(1)} %collective-permute-done.cols_b.recv_b, ...), custom_call_target="tpu_custom_call" | custom-call | flops 400000000 | bytes 1048576 | tf_op jit(solution)/shard_map/pallas_call | solution.py:1009
  15.0 0.0 collective-permute-done.2.rows_b
  15.0 0.0 collective-permute-done.3.rows_a
  15.0 1.1 %shard_map.100 = (f32[32,16,128]{2,1,0:T(8,128)S(1)}, f32[28,16,128]{2,1,0:T(8,128)S(1)}, f32[4,16,128]{2,1,0:T(8,128)S(1)}) custom-call(f32[16,16,128]{2,1,0:T(8,128)S(1)} %pad_add_fusion.fields, s32[2,16,128]{2,1,0:T(8,128)S(1)} %get-tuple-element.30.bits, f32[4,16,128]{2,1,0:T(8,128)S(1)} %get-tuple-element.31.inner_near, ...), custom_call_target="tpu_custom_call" | custom-call | flops 2000000000 | bytes 1048576 | tf_op jit(solution)/shard_map/pallas_call | solution.py:1021
  16.0 14.3 %all_to_all.10.recv = f32[32,16,128]{2,1,0:T(8,128)S(1)} all-to-all(f32[32,16,128]{2,1,0:T(8,128)S(1)} %get-tuple-element.41), channel_id=1, replica_groups=mesh['rng'=8,'xr'=4] {'rng','xr'}, dimensions={0} | all-to-all | bytes 524288 | tf_op jit(solution)/shard_map/all_to_all | solution.py:1034
  30.3 2.9 %shard_map.101 = (f32[4,16,128]{2,1,0:T(8,128)S(1)}, f32[4,16,128]{2,1,0:T(8,128)S(1)}, f32[32,2,128]{2,1,0:T(2,128)S(1)}, f32[5,4,2,8,128]{4,3,2,1,0:T(8,128)S(...) custom-call(f32[32,16,128]{2,1,0:T(8,128)S(1)} %all_to_all.10.recv, ...), custom_call_target="tpu_custom_call" | custom-call | flops 2000000000 | bytes 1048576 | tf_op jit(solution)/shard_map/pallas_call | solution.py:1036
  33.3 9.8 %all_to_all.11.fed = f32[32,2,128]{2,1,0:T(2,128)S(1)} all-to-all(f32[32,2,128]{2,1,0:T(2,128)S(1)} %get-tuple-element.47), channel_id=1, replica_groups=mesh['rng'=8,'xr'=4] {'rng','xr'}, dimensions={0} | all-to-all | bytes 65536 | tf_op jit(solution)/shard_map/all_to_all | solution.py:1067
  43.1 2.2 %shard_map.102 = (f32[4,16,128]{2,1,0:T(8,128)}, f32[4,16,128]{2,1,0:T(8,128)}) custom-call(f32[32,16,128]{2,1,0:T(8,128)S(1)} %all_to_all.10.recv, f32[32,2,128]{2,1,0:T(2,128)S(1)} %all_to_all.11.fed, f32[4,16,128]{2,1,0:T(8,128)S(1)} %get-tuple-element.48.new, f32[4,16,128]{2,1,0:T(8,128)S(1)} %get-tuple-element.49.driven, ...), custom_call_target="tpu_custom_call" | custom-call | flops 2000000000 | bytes 1048576 | tf_op jit(solution)/shard_map/pallas_call | solution.py:1068
  (1 shorter events, 0.0 us)
Async XLA Ops:
  1.6 8.6 %collective-permute-start = (f32[16,128]{1,0:T(8,128)S(1)}, f32[16,128]{1,0:T(8,128)S(1)}, u32[]{:S(2)}, u32[]{:S(2)}) collective-permute-start(f32[16,128]{1,0:T(8,128)S(1)} %get-tuple-element.28), channel_id=1, source_target_pairs={{1,2},{2,1},{5,6},{6,5},{9,10},{10,9},{13,14},{14,13},{17,18},{18,... | collective-permute-start | bytes 24584 | tf_op jit(solution)/shard_map/ppermute | solution.py:970
  2.3 7.9 %collective-permute-start.1 = (f32[16,128]{1,0:T(8,128)S(1)}, f32[16,128]{1,0:T(8,128)S(1)}, u32[]{:S(2)}, u32[]{:S(2)}) collective-permute-start(f32[16,128]{1,0:T(8,128)S(1)} %get-tuple-element.29), channel_id=1, source_target_pairs={{0,1},{1,0},{2,3},{3,2},{4,5},{5,4},{6,7},{7,6},{8,9},{9,8},{10,11... | collective-permute-start | bytes 24584 | tf_op jit(solution)/shard_map/ppermute | solution.py:971
  9.9 3.9 %copy-start = (s32[24,16,128]{2,1,0:T(8,128)S(1)}, s32[24,16,128]{2,1,0:T(8,128)}, u32[]{:S(2)}) copy-start(s32[24,16,128]{2,1,0:T(8,128)} %neighbours.1) | copy-start | bytes 589828
  9.9 3.9 %copy-start.1 = (s32[16,128]{1,0:T(8,128)S(1)}, s32[16,128]{1,0:T(8,128)}, u32[]{:S(2)}) copy-start(s32[16,128]{1,0:T(8,128)} %counts.1) | copy-start | bytes 24580
  10.2 4.7 %collective-permute-start.2 = (f32[48,128]{1,0:T(8,128)S(1)}, f32[48,128]{1,0:T(8,128)S(1)}, u32[]{:S(2)}, u32[]{:S(2)}) collective-permute-start(f32[48,128]{1,0:T(8,128)S(1)} %get-tuple-element.38), channel_id=1, source_target_pairs={{4,8},{12,16},{20,24},{8,4},{16,12},{24,20},{5,9},{13,17},{21,25},... | collective-permute-start | bytes 73736 | tf_op jit(solution)/shard_map/ppermute | solution.py:970
  10.9 4.1 %collective-permute-start.3 = (f32[48,128]{1,0:T(8,128)S(1)}, f32[48,128]{1,0:T(8,128)S(1)}, u32[]{:S(2)}, u32[]{:S(2)}) collective-permute-start(f32[48,128]{1,0:T(8,128)S(1)} %get-tuple-element.39), channel_id=1, source_target_pairs={{0,4},{4,0},{8,12},{12,8},{16,20},{20,16},{24,28},{28,24},{1,5},{5... | collective-permute-start | bytes 73736 | tf_op jit(solution)/shard_map/ppermute | solution.py:971
